TPU v7x, 32 devices: a whole 2x2x4 slice. The times are simulated.
32 devices in a mesh: row: 8 (over y, x, core), col: 4 (over z).
Axes of the slice: x: 2, y: 2, z: 4, core: 2. Of those that a mesh axis runs over, the one named last changes fastest.
Arguments:
- queries: bfloat16 [2048, 8192], P('row', 'col'), may hold values from -96 to 96
- keys: bfloat16 [2048, 1024], P('row'), may hold values from -4.05 to 4.05
- values: bfloat16 [2048, 1024], P('row'), may hold values from -4 to 4
- grad_attn: bfloat16 [2048, 8192], P('row', 'col'), may hold values from -12 to 12
- segment_ids: int32 [2048], replicated, may hold values from 0 to 3, as said below
- q_weight: bfloat16 [8192, 8192], P('row', 'col'), may hold values from -0.0625 to 0.0625
Outputs:
- input_grad: bfloat16 [2048, 8192], P('row', 'col')
- key_grad: bfloat16 [2048, 1024], P('row')
- value_grad: bfloat16 [2048, 1024], P('row')
Inputs may be any that keep to these rules, and one draw needn't show every extreme that they name: `segment_ids`: document numbers never fall along the sequence; a document holds 1 to 1024 positions; the last document holds exactly the last 1024 positions.
All inputs are finite; a program needn't handle non-finite values.
Results may differ from a plain program's by a relative error of at most 0.015.
Values may be sent and summed in bfloat16 or wider, within the bound.
No kernel may reach another device: no remote copies, remote signals or barrier semaphores. Data moves between devices by JAX's collectives and lax.ppermute only.
A program may use at most 128 MiB of HBM per device.

v0:
```python
import math

import jax
import jax.numpy as jnp
from jax import lax
from jax.sharding import PartitionSpec as P

H = 64
KVH = 8
HD = 128


NEG_FILL = -1e30


def shortened(array):

    def short(part):
        return part.astype(jnp.bfloat16) if part.dtype == jnp.float32 else part

    return jax.tree.map(short, array)


def shifted(block, axis, distance):
    devices = range(lax.axis_size(axis))
    route = [((i - distance) % len(devices), i) for i in devices]
    return lax.ppermute(block, axis, route)


def local(queries, keys, values, grad_attn, segment_ids, q_weight):
    inv_root = 1.0 / math.sqrt(HD)
    rows_here = queries.shape[0]
    row_count = lax.axis_size("row")
    heads_here = queries.shape[1] // HD
    group_size = H // KVH
    kv_here = max(1, heads_here // group_size)
    per_kv = heads_here // kv_here
    kv_width = kv_here * HD
    half_rows = rows_here // 2
    total_rows = row_count * rows_here
    row_index = lax.axis_index("row")
    col_index = lax.axis_index("col")
    kv_first = col_index * heads_here // group_size
    key_mine = lax.dynamic_slice_in_dim(keys, kv_first * HD, kv_width, 1)
    value_mine = lax.dynamic_slice_in_dim(values, kv_first * HD, kv_width, 1)
    query_local = queries.reshape(rows_here, kv_here, per_kv, HD)
    grad_local = grad_attn.reshape(rows_here, kv_here, per_kv, HD)

    def sequence_place(array_rows):
        shard_of = array_rows // rows_here
        local_of = array_rows % rows_here
        return jnp.where(
            local_of < half_rows,
            shard_of * half_rows + local_of,
            total_rows - (shard_of + 1) * half_rows + local_of - half_rows,
        )

    query_places = sequence_place(row_index * rows_here + jnp.arange(rows_here, dtype=jnp.int32))
    query_segs = jnp.take(segment_ids, query_places)

    def block_mask(first_row, key_count):
        key_places = sequence_place(first_row + jnp.arange(key_count, dtype=jnp.int32))
        key_segs = jnp.take(segment_ids, key_places)
        return (key_places[None, :] <= query_places[:, None]) & (
            key_segs[None, :] == query_segs[:, None]
        )

    def scores_and_grads(key_blk, value_blk):
        key_count = key_blk.shape[0]
        key_split = key_blk.reshape(key_count, kv_here, HD)
        value_split = value_blk.reshape(key_count, kv_here, HD)
        scores = (
            jnp.einsum("qgph,kgh->gpqk", query_local, key_split, preferred_element_type=jnp.float32)
            * inv_root
        )
        grad_prob = jnp.einsum(
            "qgph,kgh->gpqk", grad_local, value_split, preferred_element_type=jnp.float32
        )
        return (key_split, scores, grad_prob)

    def stats_step(state_now, pieces, first_row):
        row_top, row_sum, row_dot = state_now
        key_blk, value_blk = pieces
        allowed = block_mask(first_row, key_blk.shape[0])
        key_split, scores, grad_prob = scores_and_grads(key_blk, value_blk)
        masked = jnp.where(allowed, scores, NEG_FILL)
        new_top = jnp.maximum(row_top, jnp.max(masked, axis=-1))
        expo = jnp.where(allowed, jnp.exp(masked - new_top[..., None]), 0.0)
        factor = jnp.exp(row_top - new_top)
        new_sum = row_sum * factor + jnp.sum(expo, axis=-1)
        new_dot = row_dot * factor + jnp.sum(expo * grad_prob, axis=-1)
        return (new_top, new_sum, new_dot)

    def backward_block(key_blk, value_blk, first_row, row_lse, prob_dot):
        key_count = key_blk.shape[0]
        allowed = block_mask(first_row, key_count)
        key_split, scores, grad_prob = scores_and_grads(key_blk, value_blk)
        softmax_w = jnp.exp(jnp.where(allowed, scores - row_lse[..., None], NEG_FILL))
        softmax_w = jnp.where(allowed, softmax_w, 0.0)
        dscore = (softmax_w * (grad_prob - prob_dot[..., None])).astype(jnp.bfloat16)
        soft_low = softmax_w.astype(jnp.bfloat16)
        query_part = jnp.einsum(
            "gpqk,kgh->qgph", dscore, key_split, preferred_element_type=jnp.float32
        )
        key_part = jnp.einsum(
            "gpqk,qgph->kgh", dscore, query_local, preferred_element_type=jnp.float32
        )
        value_part = jnp.einsum(
            "gpqk,qgph->kgh", soft_low, grad_local, preferred_element_type=jnp.float32
        )
        return (
            query_part,
            key_part.reshape(key_count, kv_width),
            value_part.reshape(key_count, kv_width),
        )

    stat_shape = (kv_here, per_kv, rows_here)
    stat_init = (
        jnp.full(stat_shape, NEG_FILL, jnp.float32),
        jnp.zeros(stat_shape, jnp.float32),
        jnp.zeros(stat_shape, jnp.float32),
    )
    query_zero = jnp.zeros((rows_here, kv_here, per_kv, HD), jnp.float32)

    def pass_keys(pair):
        return jax.tree.map(
            lambda part, own: part.astype(own.dtype), shifted(shortened(pair), "row", 1), pair
        )

    def stats_turn(cycle_step, state_now):
        key_blk, value_blk, stats_now = state_now
        owner_row = (row_index - cycle_step) % row_count
        stats_now = stats_step(stats_now, (key_blk, value_blk), owner_row * rows_here)
        key_blk, value_blk = pass_keys((key_blk, value_blk))
        return (key_blk, value_blk, stats_now)

    stats_loop = lax.fori_loop(0, row_count, stats_turn, (key_mine, value_mine, stat_init))
    row_top, row_sum, row_dot = stats_loop[2]
    row_lse = row_top + jnp.log(row_sum)
    prob_dot = row_dot / row_sum

    def grad_turn(cycle_step, state_now):
        key_blk, value_blk, key_acc, value_acc, query_acc = state_now
        owner_row = (row_index - cycle_step) % row_count
        query_part, key_part, value_part = backward_block(
            key_blk, value_blk, owner_row * rows_here, row_lse, prob_dot
        )
        key_blk, value_blk = pass_keys((key_blk, value_blk))
        key_acc, value_acc = shifted((key_acc + key_part, value_acc + value_part), "row", 1)
        return (key_blk, value_blk, key_acc, value_acc, query_acc + query_part)

    zero_grad = jnp.zeros((rows_here, kv_width), jnp.float32)
    grad_loop = lax.fori_loop(
        0, row_count, grad_turn, (key_mine, value_mine, zero_grad, zero_grad, query_zero)
    )
    key_mine_grad = grad_loop[2]
    value_mine_grad = grad_loop[3]
    query_acc = grad_loop[4]
    wide_zero = jnp.zeros((rows_here, KVH * HD), jnp.float32)
    key_wide = lax.dynamic_update_slice_in_dim(wide_zero, key_mine_grad, kv_first * HD, 1)
    value_wide = lax.dynamic_update_slice_in_dim(wide_zero, value_mine_grad, kv_first * HD, 1)
    key_sum, value_sum = (
        lax.psum(key_wide.astype(jnp.bfloat16), "col").astype(jnp.float32),
        lax.psum(value_wide.astype(jnp.bfloat16), "col").astype(jnp.float32),
    )
    key_grad = (key_sum * inv_root).astype(jnp.bfloat16)
    value_grad = value_sum.astype(jnp.bfloat16)
    query_grad = (query_acc * inv_root).reshape(rows_here, heads_here * HD).astype(jnp.bfloat16)
    query_wide = lax.all_gather(query_grad, "col", axis=1, tiled=True)
    input_sum = jnp.dot(
        query_wide,
        lax.all_gather(q_weight, "row", axis=0, tiled=True),
        preferred_element_type=jnp.float32,
    )
    return (input_sum.astype(jnp.bfloat16), key_grad, value_grad)


def solution(mesh):
    placed = (
        P("row", "col"),
        P("row", None),
        P("row", None),
        P("row", "col"),
        P(),
        P("row", "col"),
    )
    return jax.shard_map(
        local,
        mesh=mesh,
        in_specs=placed,
        out_specs=(P("row", "col"), P("row", None), P("row", None)),
        check_vma=False,
    )
```

profile of v0, /device:TPU:0, one launch (start us, length us, event | category | flops | bytes accessed | tf_op | source)
XLA Modules:
  0.0 564.8 jit_solution(17724108534155562820)
XLA Ops:
  7.3 1.9 gather_fusion.2
  10.8 1.7 constant_dynamic-slice_fusion
  17.8 57.9 %while.50 = (s32[]{:T(128)}, bf16[256,256]{1,0:T(8,128)(2,1)S(1)}, bf16[256,256]{1,0:T(8,128)(2,1)S(1)}, f32[2,8,256]{2,1,0:T(8,128)S(1)}, f32[2,8,256]{2,1,0:T(...) while((s32[]{:T(128)}, bf16[256,256]{1,0:T(8,128)(2,1)S(1)}, ...), condition=%wide.region_4.6_spmd.clone, body=%wide.region_0.5_spmd.clone.sunk | while | flops 551802112 | bytes 21808548 | solution.py:137
  18.3 2.7 collective-permute-start.1
  21.1 1.7 gather_fusion
  26.6 1.6 collective-permute-start.1
  28.4 1.7 gather_fusion
  33.8 1.6 collective-permute-start.1
  35.6 1.7 gather_fusion
  42.4 1.7 gather_fusion
  49.1 1.7 gather_fusion
  56.3 1.7 gather_fusion
  61.8 1.6 collective-permute-start.1
  63.5 1.7 gather_fusion
  70.3 1.7 gather_fusion
  77.7 162.5 %while.51 = (s32[]{:T(128)}, bf16[256,256]{1,0:T(8,128)(2,1)}, bf16[256,256]{1,0:T(8,128)(2,1)}, f32[256,256]{0,1:T(8,128)}, f32[256,256]{0,1:T(8,128)}, /*index...) while((s32[]{:T(128)}, bf16[256,256]{1,0:T(8,128)(2,1)}, ...), condition=%wide.region_6.8_spmd.clone, body=%wide.region_5.7_spmd.clone.sunk | while | flops 1356162304 | bytes 39061076 | solution.py:153
  81.4 1.7 gather_fusion.1
  86.7 1.7 bitcast_add_fusion.6
  89.6 1.7 bitcast_add_fusion.7
  92.8 2.3 bitcast_add_fusion.8
  95.4 2.9 collective-permute-done.5
  101.5 1.7 gather_fusion.1
  106.8 1.7 bitcast_add_fusion.6
  109.6 1.7 bitcast_add_fusion.7
  111.3 2.5 collective-permute-start.5
  113.8 3.9 bitcast_add_fusion.8
  120.1 1.6 collective-permute-start.3
  122.5 1.7 gather_fusion.1
  127.8 1.7 bitcast_add_fusion.6
  130.6 1.7 bitcast_add_fusion.7
  133.4 3.9 bitcast_add_fusion.8
  137.4 2.0 collective-permute-done.5
  142.2 1.7 gather_fusion.1
  147.5 1.7 bitcast_add_fusion.6
  150.3 1.7 bitcast_add_fusion.7
  152.0 2.0 collective-permute-start.5
  154.0 3.9 bitcast_add_fusion.8
  162.7 1.7 gather_fusion.1
  168.0 1.7 bitcast_add_fusion.6
  170.8 1.7 bitcast_add_fusion.7
  174.0 3.9 bitcast_add_fusion.8
  182.8 1.7 gather_fusion.1
  188.0 1.7 bitcast_add_fusion.6
  190.9 1.7 bitcast_add_fusion.7
  192.5 2.5 collective-permute-start.5
  195.1 3.9 bitcast_add_fusion.8
  201.4 1.6 collective-permute-start.3
  203.8 1.7 gather_fusion.1
  209.1 1.7 bitcast_add_fusion.6
  211.9 1.7 bitcast_add_fusion.7
  214.7 3.9 bitcast_add_fusion.8
  218.6 2.0 collective-permute-done.5
  223.4 1.7 gather_fusion.1
  228.7 1.7 bitcast_add_fusion.6
  231.5 1.7 bitcast_add_fusion.7
  233.2 2.0 collective-permute-start.5
  235.2 3.9 bitcast_add_fusion.8
  243.8 1.8 copy.39
  245.6 2.8 multiply_convert_fusion
  249.2 47.4 %all-reduce.3.cloned.1.call-done = (bf16[256,1024]{1,0:T(8,128)(2,1)}, bf16[256,1024]{1,0:T(8,128)(2,1)}) async-done(((bf16[256,1024]{1,0:T(8,128)(2,1)}, bf16[256,1024]{1,0:T(8,128)(2,1)}), (bf16[256,1024]{1,0:T(8,128)(2,1)}, bf16[256,1024]{1,0:T(8,128)(2,1)})) %all-reduce.3.cloned.1.call-update) | async-done | bytes 1048592 | tf_op jit(solution)/shard_map/psum | solution.py:163
  296.7 1.9 multiply_convert_fusion.1
  298.6 80.5 %all-gather.3.cloned.1.call-done = bf16[256,8192]{0,1:T(8,128)(2,1)} async-done(((bf16[256,2048]{0,1:T(8,128)(2,1)}), bf16[256,8192]{0,1:T(8,128)(2,1)}) %all-gather.3.cloned.1.call-update) | async-done | bytes 4194320 | tf_op jit(solution)/shard_map/all_gather | solution.py:169
  379.1 161.4 %all-gather.5.cloned.1.call-done = bf16[8192,2048]{1,0:T(8,128)(2,1)} async-done(((bf16[1024,2048]{1,0:T(8,128)(2,1)}), bf16[8192,2048]{1,0:T(8,128)(2,1)}) %all-gather.5.cloned.1.call-update) | async-done | bytes 33554448 | tf_op jit(solution)/shard_map/all_gather | solution.py:172
  540.5 17.0 %convolution_convert_fusion = bf16[256,2048]{1,0:T(8,128)(2,1)} fusion(bf16[256,8192]{0,1:T(8,128)(2,1)} %all-gather.3.cloned.1.call-done, bf16[8192,2048]{1,0:T(8,128)(2,1)} %all-gather.5.cloned.1.call-done), kind=kOutput, calls=%fused_computation.72 | convolution fusion | flops 8590458880 | bytes 38797312 | tf_op jit(solution)/shard_map/dot_general | solution.py:170
  (428 shorter events, 121.5 us)
Async XLA Ops:
  7.2 289.5 %all-reduce.3.cloned.1.call-start = ((), (), s32[]{:S(2)}) async-start(), calls=%async_computation.2 | async-start | bytes 2097152 | tf_op jit(solution)/shard_map/psum | solution.py:163
  10.8 7.0 %copy-start = (s32[2048]{0:T(1024)S(1)}, s32[2048]{0:T(1024)}, u32[]{:S(2)}) copy-start(s32[2048]{0:T(1024)} %param.16) | copy-start | bytes 24580
  16.4 1.3 copy-start.2
  17.8 8.6 %collective-permute-start = (bf16[256,256]{1,0:T(8,128)(2,1)S(1)}, bf16[256,256]{1,0:T(8,128)(2,1)S(1)}, u32[]{:S(2)}, u32[]{:S(2)}) collective-permute-start(bf16[256,256]{1,0:T(8,128)(2,1)S(1)} %copy.93), channel_id=1, source_target_pairs={{28,0},{0,4},{4,8},{8,12},{12,16},{16,20},{20,24},{24,28},{29,1},{... | collective-permute-start | bytes 393224 | tf_op jit(solution)/shard_map/while/body/eval_jaxpr/ppermute | solution.py:27
  18.3 8.1 %collective-permute-start.1 = (bf16[256,256]{1,0:T(8,128)(2,1)S(1)}, bf16[256,256]{1,0:T(8,128)(2,1)S(1)}, u32[]{:S(2)}, u32[]{:S(2)}) collective-permute-start(bf16[256,256]{1,0:T(8,128)(2,1)S(1)} %copy.94), channel_id=1, source_target_pairs={{28,0},{0,4},{4,8},{8,12},{12,16},{16,20},{20,24},{24,28},{29,1},{... | collective-permute-start | bytes 393224 | tf_op jit(solution)/shard_map/while/body/eval_jaxpr/ppermute | solution.py:27
  23.0 1.9 copy-start.7
  26.5 7.2 %collective-permute-start = (bf16[256,256]{1,0:T(8,128)(2,1)S(1)}, bf16[256,256]{1,0:T(8,128)(2,1)S(1)}, u32[]{:S(2)}, u32[]{:S(2)}) collective-permute-start(bf16[256,256]{1,0:T(8,128)(2,1)S(1)} %copy.93), channel_id=1, source_target_pairs={{28,0},{0,4},{4,8},{8,12},{12,16},{16,20},{20,24},{24,28},{29,1},{... | collective-permute-start | bytes 393224 | tf_op jit(solution)/shard_map/while/body/eval_jaxpr/ppermute | solution.py:27
  26.6 7.1 %collective-permute-start.1 = (bf16[256,256]{1,0:T(8,128)(2,1)S(1)}, bf16[256,256]{1,0:T(8,128)(2,1)S(1)}, u32[]{:S(2)}, u32[]{:S(2)}) collective-permute-start(bf16[256,256]{1,0:T(8,128)(2,1)S(1)} %copy.94), channel_id=1, source_target_pairs={{28,0},{0,4},{4,8},{8,12},{12,16},{16,20},{20,24},{24,28},{29,1},{... | collective-permute-start | bytes 393224 | tf_op jit(solution)/shard_map/while/body/eval_jaxpr/ppermute | solution.py:27
  30.3 1.9 copy-start.7
  33.7 7.2 %collective-permute-start = (bf16[256,256]{1,0:T(8,128)(2,1)S(1)}, bf16[256,256]{1,0:T(8,128)(2,1)S(1)}, u32[]{:S(2)}, u32[]{:S(2)}) collective-permute-start(bf16[256,256]{1,0:T(8,128)(2,1)S(1)} %copy.93), channel_id=1, source_target_pairs={{28,0},{0,4},{4,8},{8,12},{12,16},{16,20},{20,24},{24,28},{29,1},{... | collective-permute-start | bytes 393224 | tf_op jit(solution)/shard_map/while/body/eval_jaxpr/ppermute | solution.py:27
  33.8 7.1 %collective-permute-start.1 = (bf16[256,256]{1,0:T(8,128)(2,1)S(1)}, bf16[256,256]{1,0:T(8,128)(2,1)S(1)}, u32[]{:S(2)}, u32[]{:S(2)}) collective-permute-start(bf16[256,256]{1,0:T(8,128)(2,1)S(1)} %copy.94), channel_id=1, source_target_pairs={{28,0},{0,4},{4,8},{8,12},{12,16},{16,20},{20,24},{24,28},{29,1},{... | collective-permute-start | bytes 393224 | tf_op jit(solution)/shard_map/while/body/eval_jaxpr/ppermute | solution.py:27
  37.5 1.9 copy-start.7
  40.9 6.7 %collective-permute-start = (bf16[256,256]{1,0:T(8,128)(2,1)S(1)}, bf16[256,256]{1,0:T(8,128)(2,1)S(1)}, u32[]{:S(2)}, u32[]{:S(2)}) collective-permute-start(bf16[256,256]{1,0:T(8,128)(2,1)S(1)} %copy.93), channel_id=1, source_target_pairs={{28,0},{0,4},{4,8},{8,12},{12,16},{16,20},{20,24},{24,28},{29,1},{... | collective-permute-start | bytes 393224 | tf_op jit(solution)/shard_map/while/body/eval_jaxpr/ppermute | solution.py:27
  41.1 6.6 %collective-permute-start.1 = (bf16[256,256]{1,0:T(8,128)(2,1)S(1)}, bf16[256,256]{1,0:T(8,128)(2,1)S(1)}, u32[]{:S(2)}, u32[]{:S(2)}) collective-permute-start(bf16[256,256]{1,0:T(8,128)(2,1)S(1)} %copy.94), channel_id=1, source_target_pairs={{28,0},{0,4},{4,8},{8,12},{12,16},{16,20},{20,24},{24,28},{29,1},{... | collective-permute-start | bytes 393224 | tf_op jit(solution)/shard_map/while/body/eval_jaxpr/ppermute | solution.py:27
  44.3 1.9 copy-start.7
  47.7 6.7 %collective-permute-start = (bf16[256,256]{1,0:T(8,128)(2,1)S(1)}, bf16[256,256]{1,0:T(8,128)(2,1)S(1)}, u32[]{:S(2)}, u32[]{:S(2)}) collective-permute-start(bf16[256,256]{1,0:T(8,128)(2,1)S(1)} %copy.93), channel_id=1, source_target_pairs={{28,0},{0,4},{4,8},{8,12},{12,16},{16,20},{20,24},{24,28},{29,1},{... | collective-permute-start | bytes 393224 | tf_op jit(solution)/shard_map/while/body/eval_jaxpr/ppermute | solution.py:27
  47.8 6.6 %collective-permute-start.1 = (bf16[256,256]{1,0:T(8,128)(2,1)S(1)}, bf16[256,256]{1,0:T(8,128)(2,1)S(1)}, u32[]{:S(2)}, u32[]{:S(2)}) collective-permute-start(bf16[256,256]{1,0:T(8,128)(2,1)S(1)} %copy.94), channel_id=1, source_target_pairs={{28,0},{0,4},{4,8},{8,12},{12,16},{16,20},{20,24},{24,28},{29,1},{... | collective-permute-start | bytes 393224 | tf_op jit(solution)/shard_map/while/body/eval_jaxpr/ppermute | solution.py:27
  51.0 1.9 copy-start.7
  54.5 7.1 %collective-permute-start = (bf16[256,256]{1,0:T(8,128)(2,1)S(1)}, bf16[256,256]{1,0:T(8,128)(2,1)S(1)}, u32[]{:S(2)}, u32[]{:S(2)}) collective-permute-start(bf16[256,256]{1,0:T(8,128)(2,1)S(1)} %copy.93), channel_id=1, source_target_pairs={{28,0},{0,4},{4,8},{8,12},{12,16},{16,20},{20,24},{24,28},{29,1},{... | collective-permute-start | bytes 393224 | tf_op jit(solution)/shard_map/while/body/eval_jaxpr/ppermute | solution.py:27
  54.6 7.1 %collective-permute-start.1 = (bf16[256,256]{1,0:T(8,128)(2,1)S(1)}, bf16[256,256]{1,0:T(8,128)(2,1)S(1)}, u32[]{:S(2)}, u32[]{:S(2)}) collective-permute-start(bf16[256,256]{1,0:T(8,128)(2,1)S(1)} %copy.94), channel_id=1, source_target_pairs={{28,0},{0,4},{4,8},{8,12},{12,16},{16,20},{20,24},{24,28},{29,1},{... | collective-permute-start | bytes 393224 | tf_op jit(solution)/shard_map/while/body/eval_jaxpr/ppermute | solution.py:27
  58.2 1.9 copy-start.7
  61.7 7.2 %collective-permute-start = (bf16[256,256]{1,0:T(8,128)(2,1)S(1)}, bf16[256,256]{1,0:T(8,128)(2,1)S(1)}, u32[]{:S(2)}, u32[]{:S(2)}) collective-permute-start(bf16[256,256]{1,0:T(8,128)(2,1)S(1)} %copy.93), channel_id=1, source_target_pairs={{28,0},{0,4},{4,8},{8,12},{12,16},{16,20},{20,24},{24,28},{29,1},{... | collective-permute-start | bytes 393224 | tf_op jit(solution)/shard_map/while/body/eval_jaxpr/ppermute | solution.py:27
  61.8 7.1 %collective-permute-start.1 = (bf16[256,256]{1,0:T(8,128)(2,1)S(1)}, bf16[256,256]{1,0:T(8,128)(2,1)S(1)}, u32[]{:S(2)}, u32[]{:S(2)}) collective-permute-start(bf16[256,256]{1,0:T(8,128)(2,1)S(1)} %copy.94), channel_id=1, source_target_pairs={{28,0},{0,4},{4,8},{8,12},{12,16},{16,20},{20,24},{24,28},{29,1},{... | collective-permute-start | bytes 393224 | tf_op jit(solution)/shard_map/while/body/eval_jaxpr/ppermute | solution.py:27
  65.4 1.9 copy-start.7
  68.9 6.7 %collective-permute-start = (bf16[256,256]{1,0:T(8,128)(2,1)S(1)}, bf16[256,256]{1,0:T(8,128)(2,1)S(1)}, u32[]{:S(2)}, u32[]{:S(2)}) collective-permute-start(bf16[256,256]{1,0:T(8,128)(2,1)S(1)} %copy.93), channel_id=1, source_target_pairs={{28,0},{0,4},{4,8},{8,12},{12,16},{16,20},{20,24},{24,28},{29,1},{... | collective-permute-start | bytes 393224 | tf_op jit(solution)/shard_map/while/body/eval_jaxpr/ppermute | solution.py:27
  69.0 6.7 %collective-permute-start.1 = (bf16[256,256]{1,0:T(8,128)(2,1)S(1)}, bf16[256,256]{1,0:T(8,128)(2,1)S(1)}, u32[]{:S(2)}, u32[]{:S(2)}) collective-permute-start(bf16[256,256]{1,0:T(8,128)(2,1)S(1)} %copy.94), channel_id=1, source_target_pairs={{28,0},{0,4},{4,8},{8,12},{12,16},{16,20},{20,24},{24,28},{29,1},{... | collective-permute-start | bytes 393224 | tf_op jit(solution)/shard_map/while/body/eval_jaxpr/ppermute | solution.py:27
  72.2 1.9 copy-start.7
  78.6 16.5 %collective-permute-start.2 = (bf16[256,256]{1,0:T(8,128)(2,1)S(1)}, bf16[256,256]{1,0:T(8,128)(2,1)}, u32[]{:S(2)}, u32[]{:S(2)}) collective-permute-start(bf16[256,256]{1,0:T(8,128)(2,1)S(1)} %copy.111), channel_id=1, source_target_pairs={{28,0},{0,4},{4,8},{8,12},{12,16},{16,20},{20,24},{24,28},{29,1},{... | collective-permute-start | bytes 393224 | tf_op jit(solution)/shard_map/while/body/eval_jaxpr/ppermute | solution.py:27
  79.5 15.6 %collective-permute-start.3 = (bf16[256,256]{1,0:T(8,128)(2,1)S(1)}, bf16[256,256]{1,0:T(8,128)(2,1)}, u32[]{:S(2)}, u32[]{:S(2)}) collective-permute-start(bf16[256,256]{1,0:T(8,128)(2,1)S(1)} %copy.112), channel_id=1, source_target_pairs={{28,0},{0,4},{4,8},{8,12},{12,16},{16,20},{20,24},{24,28},{29,1},{... | collective-permute-start | bytes 393224 | tf_op jit(solution)/shard_map/while/body/eval_jaxpr/ppermute | solution.py:27
  83.2 1.2 copy-start.3
  88.4 7.0 %collective-permute-start.4 = (f32[256,256]{0,1:T(8,128)}, f32[256,256]{0,1:T(8,128)}, u32[]{:S(2)}, u32[]{:S(2)}) collective-permute-start(f32[256,256]{0,1:T(8,128)} %bitcast_add_fusion.6), channel_id=1, source_target_pairs={{28,0},{0,4},{4,8},{8,12},{12,16},{16,20},{20,24},{24,28},{29,1},{... | collective-permute-start | bytes 786440 | tf_op jit(solution)/shard_map/while/body/eval_jaxpr/ppermute | solution.py:27
  91.2 7.0 %collective-permute-start.5 = (f32[256,256]{0,1:T(8,128)}, f32[256,256]{0,1:T(8,128)}, u32[]{:S(2)}, u32[]{:S(2)}) collective-permute-start(f32[256,256]{0,1:T(8,128)} %bitcast_add_fusion.7), channel_id=1, source_target_pairs={{28,0},{0,4},{4,8},{8,12},{12,16},{16,20},{20,24},{24,28},{29,1},{... | collective-permute-start | bytes 786440 | tf_op jit(solution)/shard_map/while/body/eval_jaxpr/ppermute | solution.py:27
  99.2 18.6 %collective-permute-start.2 = (bf16[256,256]{1,0:T(8,128)(2,1)S(1)}, bf16[256,256]{1,0:T(8,128)(2,1)}, u32[]{:S(2)}, u32[]{:S(2)}) collective-permute-start(bf16[256,256]{1,0:T(8,128)(2,1)S(1)} %copy.111), channel_id=1, source_target_pairs={{28,0},{0,4},{4,8},{8,12},{12,16},{16,20},{20,24},{24,28},{29,1},{... | collective-permute-start | bytes 393224 | tf_op jit(solution)/shard_map/while/body/eval_jaxpr/ppermute | solution.py:27
  100.1 17.7 %collective-permute-start.3 = (bf16[256,256]{1,0:T(8,128)(2,1)S(1)}, bf16[256,256]{1,0:T(8,128)(2,1)}, u32[]{:S(2)}, u32[]{:S(2)}) collective-permute-start(bf16[256,256]{1,0:T(8,128)(2,1)S(1)} %copy.112), channel_id=1, source_target_pairs={{28,0},{0,4},{4,8},{8,12},{12,16},{16,20},{20,24},{24,28},{29,1},{... | collective-permute-start | bytes 393224 | tf_op jit(solution)/shard_map/while/body/eval_jaxpr/ppermute | solution.py:27
  108.5 9.3 %collective-permute-start.4 = (f32[256,256]{0,1:T(8,128)}, f32[256,256]{0,1:T(8,128)}, u32[]{:S(2)}, u32[]{:S(2)}) collective-permute-start(f32[256,256]{0,1:T(8,128)} %bitcast_add_fusion.6), channel_id=1, source_target_pairs={{28,0},{0,4},{4,8},{8,12},{12,16},{16,20},{20,24},{24,28},{29,1},{... | collective-permute-start | bytes 786440 | tf_op jit(solution)/shard_map/while/body/eval_jaxpr/ppermute | solution.py:27
  111.3 7.0 %collective-permute-start.5 = (f32[256,256]{0,1:T(8,128)}, f32[256,256]{0,1:T(8,128)}, u32[]{:S(2)}, u32[]{:S(2)}) collective-permute-start(f32[256,256]{0,1:T(8,128)} %bitcast_add_fusion.7), channel_id=1, source_target_pairs={{28,0},{0,4},{4,8},{8,12},{12,16},{16,20},{20,24},{24,28},{29,1},{... | collective-permute-start | bytes 786440 | tf_op jit(solution)/shard_map/while/body/eval_jaxpr/ppermute | solution.py:27
  119.2 18.1 %collective-permute-start.2 = (bf16[256,256]{1,0:T(8,128)(2,1)S(1)}, bf16[256,256]{1,0:T(8,128)(2,1)}, u32[]{:S(2)}, u32[]{:S(2)}) collective-permute-start(bf16[256,256]{1,0:T(8,128)(2,1)S(1)} %copy.111), channel_id=1, source_target_pairs={{28,0},{0,4},{4,8},{8,12},{12,16},{16,20},{20,24},{24,28},{29,1},{... | collective-permute-start | bytes 393224 | tf_op jit(solution)/shard_map/while/body/eval_jaxpr/ppermute | solution.py:27
  120.1 17.2 %collective-permute-start.3 = (bf16[256,256]{1,0:T(8,128)(2,1)S(1)}, bf16[256,256]{1,0:T(8,128)(2,1)}, u32[]{:S(2)}, u32[]{:S(2)}) collective-permute-start(bf16[256,256]{1,0:T(8,128)(2,1)S(1)} %copy.112), channel_id=1, source_target_pairs={{28,0},{0,4},{4,8},{8,12},{12,16},{16,20},{20,24},{24,28},{29,1},{... | collective-permute-start | bytes 393224 | tf_op jit(solution)/shard_map/while/body/eval_jaxpr/ppermute | solution.py:27
  129.5 7.9 %collective-permute-start.4 = (f32[256,256]{0,1:T(8,128)}, f32[256,256]{0,1:T(8,128)}, u32[]{:S(2)}, u32[]{:S(2)}) collective-permute-start(f32[256,256]{0,1:T(8,128)} %bitcast_add_fusion.6), channel_id=1, source_target_pairs={{28,0},{0,4},{4,8},{8,12},{12,16},{16,20},{20,24},{24,28},{29,1},{... | collective-permute-start | bytes 786440 | tf_op jit(solution)/shard_map/while/body/eval_jaxpr/ppermute | solution.py:27
  132.3 7.0 %collective-permute-start.5 = (f32[256,256]{0,1:T(8,128)}, f32[256,256]{0,1:T(8,128)}, u32[]{:S(2)}, u32[]{:S(2)}) collective-permute-start(f32[256,256]{0,1:T(8,128)} %bitcast_add_fusion.7), channel_id=1, source_target_pairs={{28,0},{0,4},{4,8},{8,12},{12,16},{16,20},{20,24},{24,28},{29,1},{... | collective-permute-start | bytes 786440 | tf_op jit(solution)/shard_map/while/body/eval_jaxpr/ppermute | solution.py:27
  140.2 17.7 %collective-permute-start.2 = (bf16[256,256]{1,0:T(8,128)(2,1)S(1)}, bf16[256,256]{1,0:T(8,128)(2,1)}, u32[]{:S(2)}, u32[]{:S(2)}) collective-permute-start(bf16[256,256]{1,0:T(8,128)(2,1)S(1)} %copy.111), channel_id=1, source_target_pairs={{28,0},{0,4},{4,8},{8,12},{12,16},{16,20},{20,24},{24,28},{29,1},{... | collective-permute-start | bytes 393224 | tf_op jit(solution)/shard_map/while/body/eval_jaxpr/ppermute | solution.py:27
  141.1 16.7 %collective-permute-start.3 = (bf16[256,256]{1,0:T(8,128)(2,1)S(1)}, bf16[256,256]{1,0:T(8,128)(2,1)}, u32[]{:S(2)}, u32[]{:S(2)}) collective-permute-start(bf16[256,256]{1,0:T(8,128)(2,1)S(1)} %copy.112), channel_id=1, source_target_pairs={{28,0},{0,4},{4,8},{8,12},{12,16},{16,20},{20,24},{24,28},{29,1},{... | collective-permute-start | bytes 393224 | tf_op jit(solution)/shard_map/while/body/eval_jaxpr/ppermute | solution.py:27
  149.1 8.8 %collective-permute-start.4 = (f32[256,256]{0,1:T(8,128)}, f32[256,256]{0,1:T(8,128)}, u32[]{:S(2)}, u32[]{:S(2)}) collective-permute-start(f32[256,256]{0,1:T(8,128)} %bitcast_add_fusion.6), channel_id=1, source_target_pairs={{28,0},{0,4},{4,8},{8,12},{12,16},{16,20},{20,24},{24,28},{29,1},{... | collective-permute-start | bytes 786440 | tf_op jit(solution)/shard_map/while/body/eval_jaxpr/ppermute | solution.py:27
  152.0 7.0 %collective-permute-start.5 = (f32[256,256]{0,1:T(8,128)}, f32[256,256]{0,1:T(8,128)}, u32[]{:S(2)}, u32[]{:S(2)}) collective-permute-start(f32[256,256]{0,1:T(8,128)} %bitcast_add_fusion.7), channel_id=1, source_target_pairs={{28,0},{0,4},{4,8},{8,12},{12,16},{16,20},{20,24},{24,28},{29,1},{... | collective-permute-start | bytes 786440 | tf_op jit(solution)/shard_map/while/body/eval_jaxpr/ppermute | solution.py:27
  159.9 18.1 %collective-permute-start.2 = (bf16[256,256]{1,0:T(8,128)(2,1)S(1)}, bf16[256,256]{1,0:T(8,128)(2,1)}, u32[]{:S(2)}, u32[]{:S(2)}) collective-permute-start(bf16[256,256]{1,0:T(8,128)(2,1)S(1)} %copy.111), channel_id=1, source_target_pairs={{28,0},{0,4},{4,8},{8,12},{12,16},{16,20},{20,24},{24,28},{29,1},{... | collective-permute-start | bytes 393224 | tf_op jit(solution)/shard_map/while/body/eval_jaxpr/ppermute | solution.py:27
  160.8 17.2 %collective-permute-start.3 = (bf16[256,256]{1,0:T(8,128)(2,1)S(1)}, bf16[256,256]{1,0:T(8,128)(2,1)}, u32[]{:S(2)}, u32[]{:S(2)}) collective-permute-start(bf16[256,256]{1,0:T(8,128)(2,1)S(1)} %copy.112), channel_id=1, source_target_pairs={{28,0},{0,4},{4,8},{8,12},{12,16},{16,20},{20,24},{24,28},{29,1},{... | collective-permute-start | bytes 393224 | tf_op jit(solution)/shard_map/while/body/eval_jaxpr/ppermute | solution.py:27
  169.7 8.3 %collective-permute-start.4 = (f32[256,256]{0,1:T(8,128)}, f32[256,256]{0,1:T(8,128)}, u32[]{:S(2)}, u32[]{:S(2)}) collective-permute-start(f32[256,256]{0,1:T(8,128)} %bitcast_add_fusion.6), channel_id=1, source_target_pairs={{28,0},{0,4},{4,8},{8,12},{12,16},{16,20},{20,24},{24,28},{29,1},{... | collective-permute-start | bytes 786440 | tf_op jit(solution)/shard_map/while/body/eval_jaxpr/ppermute | solution.py:27
  172.5 7.0 %collective-permute-start.5 = (f32[256,256]{0,1:T(8,128)}, f32[256,256]{0,1:T(8,128)}, u32[]{:S(2)}, u32[]{:S(2)}) collective-permute-start(f32[256,256]{0,1:T(8,128)} %bitcast_add_fusion.7), channel_id=1, source_target_pairs={{28,0},{0,4},{4,8},{8,12},{12,16},{16,20},{20,24},{24,28},{29,1},{... | collective-permute-start | bytes 786440 | tf_op jit(solution)/shard_map/while/body/eval_jaxpr/ppermute | solution.py:27
  180.4 18.6 %collective-permute-start.2 = (bf16[256,256]{1,0:T(8,128)(2,1)S(1)}, bf16[256,256]{1,0:T(8,128)(2,1)}, u32[]{:S(2)}, u32[]{:S(2)}) collective-permute-start(bf16[256,256]{1,0:T(8,128)(2,1)S(1)} %copy.111), channel_id=1, source_target_pairs={{28,0},{0,4},{4,8},{8,12},{12,16},{16,20},{20,24},{24,28},{29,1},{... | collective-permute-start | bytes 393224 | tf_op jit(solution)/shard_map/while/body/eval_jaxpr/ppermute | solution.py:27
  181.3 17.7 %collective-permute-start.3 = (bf16[256,256]{1,0:T(8,128)(2,1)S(1)}, bf16[256,256]{1,0:T(8,128)(2,1)}, u32[]{:S(2)}, u32[]{:S(2)}) collective-permute-start(bf16[256,256]{1,0:T(8,128)(2,1)S(1)} %copy.112), channel_id=1, source_target_pairs={{28,0},{0,4},{4,8},{8,12},{12,16},{16,20},{20,24},{24,28},{29,1},{... | collective-permute-start | bytes 393224 | tf_op jit(solution)/shard_map/while/body/eval_jaxpr/ppermute | solution.py:27
  189.7 9.3 %collective-permute-start.4 = (f32[256,256]{0,1:T(8,128)}, f32[256,256]{0,1:T(8,128)}, u32[]{:S(2)}, u32[]{:S(2)}) collective-permute-start(f32[256,256]{0,1:T(8,128)} %bitcast_add_fusion.6), channel_id=1, source_target_pairs={{28,0},{0,4},{4,8},{8,12},{12,16},{16,20},{20,24},{24,28},{29,1},{... | collective-permute-start | bytes 786440 | tf_op jit(solution)/shard_map/while/body/eval_jaxpr/ppermute | solution.py:27
  192.5 7.0 %collective-permute-start.5 = (f32[256,256]{0,1:T(8,128)}, f32[256,256]{0,1:T(8,128)}, u32[]{:S(2)}, u32[]{:S(2)}) collective-permute-start(f32[256,256]{0,1:T(8,128)} %bitcast_add_fusion.7), channel_id=1, source_target_pairs={{28,0},{0,4},{4,8},{8,12},{12,16},{16,20},{20,24},{24,28},{29,1},{... | collective-permute-start | bytes 786440 | tf_op jit(solution)/shard_map/while/body/eval_jaxpr/ppermute | solution.py:27
  200.5 18.2 %collective-permute-start.2 = (bf16[256,256]{1,0:T(8,128)(2,1)S(1)}, bf16[256,256]{1,0:T(8,128)(2,1)}, u32[]{:S(2)}, u32[]{:S(2)}) collective-permute-start(bf16[256,256]{1,0:T(8,128)(2,1)S(1)} %copy.111), channel_id=1, source_target_pairs={{28,0},{0,4},{4,8},{8,12},{12,16},{16,20},{20,24},{24,28},{29,1},{... | collective-permute-start | bytes 393224 | tf_op jit(solution)/shard_map/while/body/eval_jaxpr/ppermute | solution.py:27
  201.4 17.3 %collective-permute-start.3 = (bf16[256,256]{1,0:T(8,128)(2,1)S(1)}, bf16[256,256]{1,0:T(8,128)(2,1)}, u32[]{:S(2)}, u32[]{:S(2)}) collective-permute-start(bf16[256,256]{1,0:T(8,128)(2,1)S(1)} %copy.112), channel_id=1, source_target_pairs={{28,0},{0,4},{4,8},{8,12},{12,16},{16,20},{20,24},{24,28},{29,1},{... | collective-permute-start | bytes 393224 | tf_op jit(solution)/shard_map/while/body/eval_jaxpr/ppermute | solution.py:27
  210.8 7.9 %collective-permute-start.4 = (f32[256,256]{0,1:T(8,128)}, f32[256,256]{0,1:T(8,128)}, u32[]{:S(2)}, u32[]{:S(2)}) collective-permute-start(f32[256,256]{0,1:T(8,128)} %bitcast_add_fusion.6), channel_id=1, source_target_pairs={{28,0},{0,4},{4,8},{8,12},{12,16},{16,20},{20,24},{24,28},{29,1},{... | collective-permute-start | bytes 786440 | tf_op jit(solution)/shard_map/while/body/eval_jaxpr/ppermute | solution.py:27
  213.6 7.0 %collective-permute-start.5 = (f32[256,256]{0,1:T(8,128)}, f32[256,256]{0,1:T(8,128)}, u32[]{:S(2)}, u32[]{:S(2)}) collective-permute-start(f32[256,256]{0,1:T(8,128)} %bitcast_add_fusion.7), channel_id=1, source_target_pairs={{28,0},{0,4},{4,8},{8,12},{12,16},{16,20},{20,24},{24,28},{29,1},{... | collective-permute-start | bytes 786440 | tf_op jit(solution)/shard_map/while/body/eval_jaxpr/ppermute | solution.py:27
  221.5 17.7 %collective-permute-start.2 = (bf16[256,256]{1,0:T(8,128)(2,1)S(1)}, bf16[256,256]{1,0:T(8,128)(2,1)}, u32[]{:S(2)}, u32[]{:S(2)}) collective-permute-start(bf16[256,256]{1,0:T(8,128)(2,1)S(1)} %copy.111), channel_id=1, source_target_pairs={{28,0},{0,4},{4,8},{8,12},{12,16},{16,20},{20,24},{24,28},{29,1},{... | collective-permute-start | bytes 393224 | tf_op jit(solution)/shard_map/while/body/eval_jaxpr/ppermute | solution.py:27
  222.4 16.7 %collective-permute-start.3 = (bf16[256,256]{1,0:T(8,128)(2,1)S(1)}, bf16[256,256]{1,0:T(8,128)(2,1)}, u32[]{:S(2)}, u32[]{:S(2)}) collective-permute-start(bf16[256,256]{1,0:T(8,128)(2,1)S(1)} %copy.112), channel_id=1, source_target_pairs={{28,0},{0,4},{4,8},{8,12},{12,16},{16,20},{20,24},{24,28},{29,1},{... | collective-permute-start | bytes 393224 | tf_op jit(solution)/shard_map/while/body/eval_jaxpr/ppermute | solution.py:27
  230.4 8.8 %collective-permute-start.4 = (f32[256,256]{0,1:T(8,128)}, f32[256,256]{0,1:T(8,128)}, u32[]{:S(2)}, u32[]{:S(2)}) collective-permute-start(f32[256,256]{0,1:T(8,128)} %bitcast_add_fusion.6), channel_id=1, source_target_pairs={{28,0},{0,4},{4,8},{8,12},{12,16},{16,20},{20,24},{24,28},{29,1},{... | collective-permute-start | bytes 786440 | tf_op jit(solution)/shard_map/while/body/eval_jaxpr/ppermute | solution.py:27
  233.2 7.0 %collective-permute-start.5 = (f32[256,256]{0,1:T(8,128)}, f32[256,256]{0,1:T(8,128)}, u32[]{:S(2)}, u32[]{:S(2)}) collective-permute-start(f32[256,256]{0,1:T(8,128)} %bitcast_add_fusion.7), channel_id=1, source_target_pairs={{28,0},{0,4},{4,8},{8,12},{12,16},{16,20},{20,24},{24,28},{29,1},{... | collective-permute-start | bytes 786440 | tf_op jit(solution)/shard_map/while/body/eval_jaxpr/ppermute | solution.py:27
  240.2 3.6 copy-start.1
  243.6 135.5 %all-gather.3.cloned.1.call-start = ((), (), s32[]{:S(2)}) async-start(), calls=%async_computation | async-start | bytes 5242880 | tf_op jit(solution)/shard_map/all_gather | solution.py:169
  248.5 292.0 %all-gather.5.cloned.1.call-start = ((), (), s32[]{:S(2)}) async-start(), calls=%async_computation.1 | async-start | bytes 37748736 | tf_op jit(solution)/shard_map/all_gather | solution.py:172
  298.6 258.9 %copy-start.8 = (bf16[256,1024]{1,0:T(8,128)(2,1)S(1)}, bf16[256,1024]{1,0:T(8,128)(2,1)}, u32[]{:S(2)}) copy-start(bf16[256,1024]{1,0:T(8,128)(2,1)} %get-tuple-element.1188) | copy-start | bytes 1572868
  (33 other events, 39.3 us)
Sparse Core Ops, SparseCore 0:
  243.7 52.9 all-reduce.2
  298.9 80.1 all-gather.2
  381.1 159.3 all-gather.4
where the time goes:
time: 566 us; the launch traced here: 565 us
  waiting for transfers between devices  302 us (53%)
  matrix products  98.2 us (17%)
  local copies, waits for them, and re-layouts  69 us (12%)
  other arithmetic  43.8 us (8%)
  starting transfers between devices  35.6 us (6%)
  between operations  13.9 us (2%)
    all_gather x1, waiting for transfers between devices, local(): lax.all_gather(q_weight, 'row', axis=0, tiled=True)  161 us
    all_gather x1, waiting for transfers between devices, local(): query_wide = lax.all_gather(query_grad, 'col', axis=1, tiled=True)  80.5 us
    psum x1, waiting for transfers between devices, local(): lax.psum(key_wide.astype(jnp.bfloat16), 'col').astype(jnp.float32)  47.4 us
    ppermute x48, starting transfers between devices, shifted(): return lax.ppermute(block, axis, route)  35.3 us
    dot_general x8, matrix products, backward_block(): jnp.einsum('gpqk,kgh->qgph', dscore, key_split, preferred_element_type=jn...  29.7 us
    gather x16, local copies, waits for them, and re-layouts, block_mask(): key_segs = jnp.take(segment_ids, key_places)  27.6 us
    dot_general x16, matrix products, scores_and_grads(): jnp.einsum('qgph,kgh->gpqk', grad_local, value_split, preferred_element_t...  23.9 us
    while x120, local copies, waits for them, and re-layouts  17.3 us
  transfers between devices with their start and end apart: 51, of which 12 were waited for; matrix products, arithmetic and copies ran while one was open for 30% of the time, Pallas kernels for 0%

commit v1 on v0

v1 whole, which is shorter than its diff:
```python
import functools
import math

import jax
import jax.numpy as jnp
from jax import lax
from jax.experimental import pallas as pl
from jax.experimental.pallas import tpu as pltpu
from jax.sharding import PartitionSpec as P

H = 64
KVH = 8
HD = 128
CHUNKS = 4

NEG = -1e30


def attention_kernel(
    kv_here, per_kv, rows, ranks, relative, me_ref, seg_query, seg_key, q_ref, g_ref, kv_ref,
    dq_ref, dkv_ref, q_rows, g_rows, q_cols, g_cols, s_all, d_all, p_low, d_low, top, total, dots,
):
    half = rows // 2
    width = kv_here * HD
    inv_root = 1.0 / math.sqrt(HD)
    scale = inv_root * math.log2(math.e)
    me = me_ref[0]
    contract_last = (((1,), (1,)), ((), ()))
    dkv_ref[...] = jnp.zeros_like(dkv_ref)
    for g in range(kv_here):
        for side in range(2):
            here = slice(side * half, (side + 1) * half)
            blocks = me + 1 if side == 0 else ranks - me
            steps = (blocks + 1) // 2
            for p in range(per_kv):
                head = slice((g * per_kv + p) * HD, (g * per_kv + p + 1) * HD)
                q_rows[p * half:(p + 1) * half, :] = q_ref[here, head]
                g_rows[p * half:(p + 1) * half, :] = g_ref[here, head]
            q_cols[...] = q_rows[...].T
            g_cols[...] = g_rows[...].T

            def piece(block):
                owner = block if side == 0 else ranks - 1 - block
                return owner ^ me

            def pair(j, first):
                one = kv_ref[piece(2 * j), here, first:first + HD]
                two = kv_ref[piece(2 * j + 1), here, first:first + HD]
                return jnp.concatenate([one, two], axis=0)

            top[...] = jnp.full_like(top, NEG)
            total[...] = jnp.zeros_like(total)
            dots[...] = jnp.zeros_like(dots)

            def scores(j, carry):
                keys = pair(j, g * HD)
                vals = pair(j, width + g * HD)
                query_at = (blocks - 1) * half + lax.broadcasted_iota(jnp.int32, (half, 2 * half), 0)
                key_at = j * 2 * half + lax.broadcasted_iota(jnp.int32, (half, 2 * half), 1)
                segs = seg_key[side * (ranks // 2) + j]
                allowed = (key_at <= query_at) & (segs == seg_query[side])
                bias = jnp.where(allowed, 0.0, NEG)
                for p in range(per_kv):
                    at = slice(p * half, (p + 1) * half)
                    s = lax.dot_general(
                        q_rows[at, :], keys, contract_last, preferred_element_type=jnp.float32
                    )
                    s = s * scale + bias
                    s_all[j, at, :] = s
                    top[at, :] = jnp.maximum(top[at, :], jnp.maximum(s[:, :half], s[:, half:]))
                    d_all[j, at, :] = lax.dot_general(
                        g_rows[at, :], vals, contract_last, preferred_element_type=jnp.float32
                    )
                return carry

            lax.fori_loop(0, steps, scores, 0)
            top[...] = jnp.broadcast_to(jnp.max(top[...], axis=1, keepdims=True), top.shape)

            def sums(j, carry):
                for p in range(per_kv):
                    at = slice(p * half, (p + 1) * half)
                    high = top[at, :]
                    s = s_all[j, at, :]
                    e = jnp.exp2(s - jnp.concatenate([high, high], axis=1))
                    s_all[j, at, :] = e
                    total[at, :] += e[:, :half] + e[:, half:]
                    ed = e * d_all[j, at, :]
                    dots[at, :] += ed[:, :half] + ed[:, half:]
                return carry

            lax.fori_loop(0, steps, sums, 0)
            inverse = 1.0 / jnp.sum(total[...], axis=1, keepdims=True)
            delta = jnp.sum(dots[...], axis=1, keepdims=True) * inverse
            total[...] = jnp.broadcast_to(inverse, total.shape)
            dots[...] = jnp.broadcast_to(delta, dots.shape)
            top[...] = jnp.zeros_like(top)

            def grads(j, carry):
                keys = pair(j, g * HD)
                for p in range(per_kv):
                    at = slice(p * half, (p + 1) * half)
                    inv = total[at, :]
                    dot = dots[at, :]
                    prob = s_all[j, at, :] * jnp.concatenate([inv, inv], axis=1)
                    p_low[at, :] = prob.astype(jnp.bfloat16)
                    shifted = d_all[j, at, :] - jnp.concatenate([dot, dot], axis=1)
                    d_low[at, :] = (prob * shifted).astype(jnp.bfloat16)
                top[...] += jnp.dot(d_low[...], keys, preferred_element_type=jnp.float32)
                key_part = jnp.dot(q_cols[...], d_low[...], preferred_element_type=jnp.float32)
                val_part = jnp.dot(g_cols[...], p_low[...], preferred_element_type=jnp.float32)
                key_part = (key_part * inv_root).T.astype(jnp.bfloat16)
                val_part = val_part.T.astype(jnp.bfloat16)
                for i in range(2):
                    out = piece(2 * j + i)
                    rows_i = slice(i * half, (i + 1) * half)
                    dkv_ref[out, here, g * HD:(g + 1) * HD] = key_part[rows_i, :]
                    dkv_ref[out, here, width + g * HD:width + (g + 1) * HD] = val_part[rows_i, :]
                return carry

            lax.fori_loop(0, steps, grads, 0)
            for p in range(per_kv):
                at = slice(p * half, (p + 1) * half)
                slot = p ^ me if relative else p
                dq_ref[slot, g, here, :] = (top[at, :] * inv_root).astype(jnp.bfloat16)


def attention(me, seg_query, seg_key, queries, grad_attn, kv, kv_here, per_kv, relative):
    ranks, rows = kv.shape[:2]
    half = rows // 2
    stack = per_kv * half
    pairs = ranks // 2
    vmem = pl.BlockSpec(memory_space=pltpu.VMEM)
    return pl.pallas_call(
        functools.partial(attention_kernel, kv_here, per_kv, rows, ranks, relative),
        out_shape=(
            jax.ShapeDtypeStruct((per_kv, kv_here, rows, HD), jnp.bfloat16),
            jax.ShapeDtypeStruct(kv.shape, jnp.bfloat16),
        ),
        in_specs=[pl.BlockSpec(memory_space=pltpu.SMEM)] + [vmem] * 5,
        out_specs=(vmem, vmem),
        scratch_shapes=[
            pltpu.VMEM((stack, HD), jnp.bfloat16),
            pltpu.VMEM((stack, HD), jnp.bfloat16),
            pltpu.VMEM((HD, stack), jnp.bfloat16),
            pltpu.VMEM((HD, stack), jnp.bfloat16),
            pltpu.VMEM((pairs, stack, 2 * half), jnp.float32),
            pltpu.VMEM((pairs, stack, 2 * half), jnp.float32),
            pltpu.VMEM((stack, 2 * half), jnp.bfloat16),
            pltpu.VMEM((stack, 2 * half), jnp.bfloat16),
            pltpu.VMEM((stack, HD), jnp.float32),
            pltpu.VMEM((stack, HD), jnp.float32),
            pltpu.VMEM((stack, HD), jnp.float32),
        ],
        compiler_params=pltpu.CompilerParams(vmem_limit_bytes=40 << 20),
        cost_estimate=pl.CostEstimate(
            flops=20_000_000_000, bytes_accessed=8_000_000, transcendentals=3_000_000
        ),
        name="attention",
    )(me, seg_query, seg_key, queries, grad_attn, kv)


def project_kernel(ranks, order_ref, w_ref, *refs):
    parts, out_ref = refs[:-1], refs[-1]
    lhs = jnp.concatenate([part[...] for part in parts], axis=1)
    rhs = jnp.concatenate([w_ref[order_ref[i]] for i in range(len(parts))], axis=0)
    out = jnp.dot(lhs, rhs, preferred_element_type=jnp.float32)
    out_ref[...] = out.astype(jnp.bfloat16)


def project(order, weights, parts):
    ranks, depth, features = weights.shape
    rows = parts[0].shape[0]
    tile = min(256, features)
    return pl.pallas_call(
        functools.partial(project_kernel, ranks),
        out_shape=jax.ShapeDtypeStruct((rows, features), jnp.bfloat16),
        grid=(features // tile,),
        in_specs=[
            pl.BlockSpec(memory_space=pltpu.SMEM),
            pl.BlockSpec((ranks, depth, tile), lambda n: (0, 0, n)),
        ] + [pl.BlockSpec((rows, depth), lambda n: (0, 0))] * len(parts),
        out_specs=pl.BlockSpec((rows, tile), lambda n: (0, n)),
        compiler_params=pltpu.CompilerParams(vmem_limit_bytes=32 << 20),
        cost_estimate=pl.CostEstimate(
            flops=2 * rows * depth * len(parts) * features,
            bytes_accessed=2 * (rows * (depth * len(parts) + features) + ranks * depth * features),
            transcendentals=0,
        ),
        name="project",
    )(order, weights, *parts)


def across(block, mask):
    ranks = lax.axis_size("row")
    return lax.ppermute(block, "row", [(i, i ^ mask) for i in range(ranks)])


def turned(block, distance):
    count = lax.axis_size("col")
    return lax.ppermute(block, "col", [((i + distance) % count, i) for i in range(count)])


def gather_col(block):
    count = lax.axis_size("col")
    found = {0: block}
    ahead = behind = block
    for k in range(1, (count - 1) // 2 + 1):
        ahead = turned(ahead, 1)
        behind = turned(behind, -1)
        found[k], found[count - k] = ahead, behind
    if count % 2 == 0:
        cut = block.shape[0] // 2
        found[count // 2] = jnp.concatenate(
            [turned(ahead[:cut], 1), turned(behind[cut:], -1)], axis=0
        )
    return [found[k] for k in range(count)]


def added(one, two):
    return (one.astype(jnp.float32) + two.astype(jnp.float32)).astype(jnp.bfloat16)


def scatter_sum(blocks, bits):
    ranks = blocks.shape[0]
    shape = blocks.shape[1:]
    now = blocks.reshape((2,) * bits + shape)
    left = list(range(bits))
    for b in [0]:
        axis = left[::-1].index(b)
        keep = lax.index_in_dim(now, 0, axis, keepdims=False)
        send = lax.index_in_dim(now, 1, axis, keepdims=False)
        now = added(keep, across(send, 1 << b))
        left.remove(b)
    cut = shape[-1] // 2
    done = []
    for part, order in ((now[..., :cut], left), (now[..., cut:], left[::-1])):
        rest = list(left)
        for b in order:
            axis = rest[::-1].index(b)
            keep = lax.index_in_dim(part, 0, axis, keepdims=False)
            send = lax.index_in_dim(part, 1, axis, keepdims=False)
            part = added(keep, across(send, 1 << b))
            rest.remove(b)
        done.append(part)
    return jnp.concatenate(done, axis=-1)


def local(queries, keys, values, grad_attn, segment_ids, q_weight):
    rows = queries.shape[0]
    half = rows // 2
    ranks = lax.axis_size("row")
    count = lax.axis_size("col")
    bits = ranks.bit_length() - 1
    heads_here = queries.shape[1] // HD
    group = H // KVH
    kv_here = max(1, heads_here // group)
    per_kv = heads_here // kv_here
    width = kv_here * HD
    total_rows = ranks * rows
    me = lax.axis_index("row")
    col = lax.axis_index("col")
    kv_first = col * heads_here // group

    mine = jnp.concatenate(
        [
            lax.dynamic_slice_in_dim(keys, kv_first * HD, width, 1),
            lax.dynamic_slice_in_dim(values, kv_first * HD, width, 1),
        ],
        axis=1,
    )
    even = jnp.stack([mine] + [across(mine, d) for d in range(2, ranks, 2)])
    odd = across(even, 1)
    kv = jnp.stack([even, odd], axis=1).reshape(ranks, rows, 2 * width)

    rows_w = q_weight.shape[0]
    depth = rows_w // ranks
    w_cut = q_weight.reshape(ranks, depth, q_weight.shape[1])
    w_blocks = [lax.dynamic_index_in_dim(w_cut, me, 0, keepdims=False)]
    for d in range(1, ranks):
        w_blocks.append(across(lax.dynamic_index_in_dim(w_cut, me ^ d, 0, keepdims=False), d))
    weights = jnp.stack(w_blocks)

    key_segs = segment_ids.reshape(ranks, 1, 2 * half)
    own = segment_ids.reshape(2 * ranks, half)
    query_segs = jnp.stack(
        [
            lax.dynamic_index_in_dim(own, me, 0, keepdims=False),
            lax.dynamic_index_in_dim(own, 2 * ranks - 1 - me, 0, keepdims=False),
        ]
    )[:, :, None]
    direct = per_kv == ranks and depth == HD
    dq, dkv = attention(
        me.reshape(1), query_segs, key_segs, queries, grad_attn, kv, kv_here, per_kv, direct
    )
    per_col = heads_here * HD // rows_w
    if not direct:
        dq = dq.transpose(2, 1, 0, 3).reshape(rows, per_col, ranks, depth)
        dq = dq.transpose(2, 1, 0, 3)[me ^ jnp.arange(ranks)]

    spread = [dq[0]] + [across(dq[d], d) for d in range(1, ranks)]
    tokens = jnp.stack(spread)
    order = jnp.concatenate(
        [me ^ (((col + k) % count) * per_col + jnp.arange(per_col)) for k in range(count)]
    ).astype(jnp.int32)
    step = rows // CHUNKS
    outs = []
    for c in range(CHUNKS):
        chunk = tokens[:, :, c * step:(c + 1) * step, :].transpose(1, 0, 2, 3)
        parts = []
        for found in gather_col(chunk.reshape(per_col, ranks * step, depth).transpose(1, 0, 2).reshape(ranks * step, per_col * depth)):
            parts += [found[:, i * depth:(i + 1) * depth] for i in range(per_col)]
        partial = project(order, weights, parts)
        outs.append(scatter_sum(partial.reshape(ranks, step, -1), bits))
    input_grad = jnp.concatenate(outs, axis=0)

    dkv_mine = scatter_sum(dkv, bits)
    found = gather_col(dkv_mine)
    share = max(1, group // heads_here)
    whole = jnp.stack(found)
    whole = jnp.roll(whole, col, axis=0) if count > 1 else whole
    if share > 1:
        whole = whole.reshape(count // share, share, rows, 2 * width).astype(jnp.float32)
        whole = whole.sum(axis=1).astype(jnp.bfloat16)
    key_grad = whole[..., :width].transpose(1, 0, 2).reshape(rows, KVH * HD)
    value_grad = whole[..., width:].transpose(1, 0, 2).reshape(rows, KVH * HD)
    return (input_grad, key_grad, value_grad)


def solution(mesh):
    placed = (
        P("row", "col"),
        P("row", None),
        P("row", None),
        P("row", "col"),
        P(),
        P("row", "col"),
    )
    return jax.shard_map(
        local,
        mesh=mesh,
        in_specs=placed,
        out_specs=(P("row", "col"), P("row", None), P("row", None)),
        check_vma=False,
    )
```

time: 566 us -> 257 us (0.45)
  waiting for transfers between devices: 302 us -> 108 us
  matrix products: 98.2 us -> 0 us
  local copies, waits for them, and re-layouts: 69 us -> 15.9 us
  starting transfers between devices: 35.6 us -> 88.1 us
  other arithmetic: 43.8 us -> 7.7 us
  Pallas kernels: 0 us -> 34.9 us
  between operations: 13.9 us -> 1.68 us
    all_gather x2 -> x0, waiting for transfers between devices: 242 us -> none  [the longest x1 161 us: local(): lax.all_gather(q_weight, 'row', axis=0, tiled=True)]
    dot_general x57 -> x0, matrix products: 98.2 us -> none  [the longest x8 29.7 us: backward_block(): jnp.einsum('gpqk,kgh->qgph', dscore, key_split, preferred_element_type=jn...]
    ppermute x48 -> x63, waiting for transfers between devices: 12.1 us -> 108 us  [the longest x43 79.5 us: across(): return lax.ppermute(block, 'row', [(i, i ^ mask) for i in range(ranks)])]
    ppermute x48 -> x63, starting transfers between devices: 35.3 us -> 88.1 us  [the longest x20 47.4 us: turned(): lax.ppermute(block, 'col', [((i + distance) % count, i) for i in range(co...]
    psum x1 -> x0, waiting for transfers between devices: 47.4 us -> none  [local(): lax.psum(key_wide.astype(jnp.bfloat16), 'col').astype(jnp.float32)]
    pallas_call x0 -> x5, Pallas kernels: none -> 34.9 us  [the longest x4 19.6 us: project(): pl.pallas_call(functools.partial(project_kernel, ranks), out_shape=jax.Sh...]
    gather x17 -> x0, local copies, waits for them, and re-layouts: 29.5 us -> none  [the longest x16 27.6 us: block_mask(): key_segs = jnp.take(segment_ids, key_places)]
    add x24 -> x0, other arithmetic: 26.9 us -> none  [the longest x8 13.4 us: grad_turn(): key_acc + key_part]
  transfers between devices with their start and end apart: 51 -> 63, of which waited for: 12 -> 31; matrix products, arithmetic and copies ran while one was open for 30% -> 7% of each run, Pallas kernels for 0% -> 8%
where the time goes in v1:
time: 257 us
  waiting for transfers between devices  108 us (42%)
  starting transfers between devices  88.1 us (34%)
  Pallas kernels  34.9 us (14%)
  local copies, waits for them, and re-layouts  15.9 us (6%)
  other arithmetic  7.7 us (3%)
    ppermute x43, waiting for transfers between devices, across(): return lax.ppermute(block, 'row', [(i, i ^ mask) for i in range(ranks)])  79.5 us
    ppermute x20, starting transfers between devices, turned(): lax.ppermute(block, 'col', [((i + distance) % count, i) for i in range(co...  47.4 us
    ppermute x43, starting transfers between devices, across(): return lax.ppermute(block, 'row', [(i, i ^ mask) for i in range(ranks)])  40.7 us
    ppermute x20, waiting for transfers between devices, turned(): lax.ppermute(block, 'col', [((i + distance) % count, i) for i in range(co...  28.9 us
    pallas_call x4, Pallas kernels, project(): pl.pallas_call(functools.partial(project_kernel, ranks), out_shape=jax.Sh...  19.6 us
    pallas_call x1, Pallas kernels, attention(): pl.pallas_call(functools.partial(attention_kernel, kv_here, per_kv, rows,...  15.4 us
    unnamed x28, local copies, waits for them, and re-layouts  6.69 us
  transfers between devices with their start and end apart: 63, of which 31 were waited for; matrix products, arithmetic and copies ran while one was open for 7% of the time, Pallas kernels for 8%

profile of v1, /device:TPU:0, one launch (start us, length us, event | category | flops | bytes accessed | tf_op | source)
XLA Modules:
  0.0 256.6 jit_solution(12208387002967913905)
XLA Ops:
  2.4 3.9 %collective-permute-start.9 = (bf16[256,512]{1,0:T(8,128)(2,1)}, bf16[256,512]{1,0:T(8,128)(2,1)}, u32[]{:S(2)}, u32[]{:S(2)}) collective-permute-start(bf16[256,512]{1,0:T(8,128)(2,1)} %get-tuple-element.74), channel_id=1, source_target_pairs={{0,24},{4,28},{8,16},{12,20},{16,8},{20,12},{24,0},{28,4},{1,25},{... | collective-permute-start | bytes 786440 | tf_op jit(solution)/shard_map/ppermute | solution.py:195
  6.9 3.7 %dynamic-slice_bitcast_fusion.2 = (bf16[128,2048]{1,0:T(8,128)(2,1)S(1)}, bf16[128,2048]{1,0:T(8,128)(2,1)S(1)}, bf16[128,2048]{1,0:T(8,128)(2,1)S(1)}, bf16[128...) fusion(bf16[8,128,2048]{2,1,0:T(8,128)(2,1)} %bitcast.353, ...), kind=kLoop, calls=%fused_computation.52 | loop fusion | bytes 8388640 | tf_op jit(solution)/shard_map/jit(dynamic_index_in_dim)/squeeze | solution.py:280
  10.6 2.0 collective-permute-start.1
  14.0 4.5 %collective-permute-done.8 = bf16[256,512]{1,0:T(8,128)(2,1)} collective-permute-done((bf16[256,512]{1,0:T(8,128)(2,1)}, bf16[256,512]{1,0:T(8,128)(2,1)}, u32[]{:S(2)}, u32[]{:S(2)}) %collective-permute-start.8) | collective-permute-done | bytes 262176 | tf_op jit(solution)/shard_map/ppermute | solution.py:195
  18.5 1.7 collective-permute-start.3
  20.2 1.3 fusion.28
  21.5 1.5 collective-permute-start.5
  23.9 7.2 %collective-permute-done.1 = bf16[128,2048]{1,0:T(8,128)(2,1)S(1)} collective-permute-done((bf16[128,2048]{1,0:T(8,128)(2,1)}, bf16[128,2048]{1,0:T(8,128)(2,1)S(1)}, u32[]{:S(2)}, u32[]{:S(2)}) %collective-permute-start.1) | collective-permute-done | bytes 524320 | tf_op jit(solution)/shard_map/ppermute | solution.py:195
  31.9 9.5 %collective-permute-done.2 = bf16[128,2048]{1,0:T(8,128)(2,1)S(1)} collective-permute-done((bf16[128,2048]{1,0:T(8,128)(2,1)}, bf16[128,2048]{1,0:T(8,128)(2,1)S(1)}, u32[]{:S(2)}, u32[]{:S(2)}) %collective-permute-start.2) | collective-permute-done | bytes 524320 | tf_op jit(solution)/shard_map/ppermute | solution.py:195
  44.1 21.2 %collective-permute-done.4 = bf16[128,2048]{1,0:T(8,128)(2,1)S(1)} collective-permute-done((bf16[128,2048]{1,0:T(8,128)(2,1)S(1)}, bf16[128,2048]{1,0:T(8,128)(2,1)S(1)}, u32[]{:S(2)}, u32[]{:S(2)}) %collective-permute-start.4) | collective-permute-done | bytes 524320 | tf_op jit(solution)/shard_map/ppermute | solution.py:195
  69.6 15.4 %attention.1 = (bf16[8,2,256,128]{3,2,1,0:T(8,128)(2,1)S(1)}, bf16[8,256,512]{2,1,0:T(8,128)(2,1)S(1)}) custom-call(s32[1]{0:T(128)} %bitcast.15.me_ref, s32[2,128,1]{2,1,0:T(8,128)S(1)} %copy.28.seg_query, s32[8,1,256]{2,1,0:T(1,128)S(1)} %bitcast.352, bf16[256,2048]{1,0:T(8,128)(2,1)S(1)} %copy-done.2, bf16[256,2048]{1,0:T(8,128)(2,1)S(1)} %copy-done.3, ...), custom_call_target="tpu_custom_call" | custom-call | flops 20000000000 | bytes 8000000 | tf_op jit(solution)/shard_map/attention/pallas_call | solution.py:133
  85.7 1.7 collective-permute-start.12
  87.4 1.5 collective-permute-start.14
  89.3 1.5 collective-permute-start.16
  90.8 1.2 collective-permute-done.12
  92.1 2.0 collective-permute-done.13
  95.0 6.3 %collective-permute-done.15 = bf16[2,256,128]{2,1,0:T(8,128)(2,1)S(1)} collective-permute-done((bf16[2,256,128]{2,1,0:T(8,128)(2,1)S(1)}, bf16[2,256,128]{2,1,0:T(8,128)(2,1)S(1)}, u32[]{:S(2)}, u32[]{:S(2)}) %collective-permute-start.15) | collective-permute-done | bytes 131104 | tf_op jit(solution)/shard_map/ppermute | solution.py:195
  101.6 4.0 %collective-permute-start.45 = (bf16[512,256]{1,0:T(8,128)(2,1)S(1)}, bf16[512,256]{1,0:T(8,128)(2,1)S(1)}, u32[]{:S(2)}, u32[]{:S(2)}) collective-permute-start(bf16[512,256]{1,0:T(8,128)(2,1)S(1)} %bitcast.364), channel_id=1, source_target_pairs={{1,0},{2,1},{3,2},{0,3},{5,4},{6,5},{7,6},{4,7},{9,8},{10,9},{11,1... | collective-permute-start | bytes 786440 | tf_op jit(solution)/shard_map/ppermute | solution.py:200
  105.6 3.9 %collective-permute-start.36 = (bf16[512,256]{1,0:T(8,128)(2,1)S(1)}, bf16[512,256]{1,0:T(8,128)(2,1)S(1)}, u32[]{:S(2)}, u32[]{:S(2)}) collective-permute-start(bf16[512,256]{1,0:T(8,128)(2,1)S(1)} %bitcast.361), channel_id=1, source_target_pairs={{1,0},{2,1},{3,2},{0,3},{5,4},{6,5},{7,6},{4,7},{9,8},{10,9},{11,1... | collective-permute-start | bytes 786440 | tf_op jit(solution)/shard_map/ppermute | solution.py:200
  109.7 2.5 collective-permute-done.45
  112.3 4.3 %collective-permute-start.27 = (bf16[512,256]{1,0:T(8,128)(2,1)S(1)}, bf16[512,256]{1,0:T(8,128)(2,1)S(1)}, u32[]{:S(2)}, u32[]{:S(2)}) collective-permute-start(bf16[512,256]{1,0:T(8,128)(2,1)S(1)} %bitcast.358), channel_id=1, source_target_pairs={{1,0},{2,1},{3,2},{0,3},{5,4},{6,5},{7,6},{4,7},{9,8},{10,9},{11,1... | collective-permute-start | bytes 786440 | tf_op jit(solution)/shard_map/ppermute | solution.py:200
  116.6 2.2 collective-permute-done.47
  118.8 1.6 collective-permute-start.29
  120.4 3.2 %collective-permute-done.36 = bf16[512,256]{1,0:T(8,128)(2,1)S(1)} collective-permute-done((bf16[512,256]{1,0:T(8,128)(2,1)S(1)}, bf16[512,256]{1,0:T(8,128)(2,1)S(1)}, u32[]{:S(2)}, u32[]{:S(2)}) %collective-permute-start.36) | collective-permute-done | bytes 262176 | tf_op jit(solution)/shard_map/ppermute | solution.py:200
  123.5 4.3 %collective-permute-start.18 = (bf16[512,256]{1,0:T(8,128)(2,1)S(1)}, bf16[512,256]{1,0:T(8,128)(2,1)S(1)}, u32[]{:S(2)}, u32[]{:S(2)}) collective-permute-start(bf16[512,256]{1,0:T(8,128)(2,1)S(1)} %bitcast.355), channel_id=1, source_target_pairs={{1,0},{2,1},{3,2},{0,3},{5,4},{6,5},{7,6},{4,7},{9,8},{10,9},{11,1... | collective-permute-start | bytes 786440 | tf_op jit(solution)/shard_map/ppermute | solution.py:200
  127.8 2.2 collective-permute-done.38
  130.0 1.6 collective-permute-start.20
  131.7 3.1 %collective-permute-done.27 = bf16[512,256]{1,0:T(8,128)(2,1)S(1)} collective-permute-done((bf16[512,256]{1,0:T(8,128)(2,1)S(1)}, bf16[512,256]{1,0:T(8,128)(2,1)S(1)}, u32[]{:S(2)}, u32[]{:S(2)}) %collective-permute-start.27) | collective-permute-done | bytes 262176 | tf_op jit(solution)/shard_map/ppermute | solution.py:200
  134.8 4.3 %collective-permute-start.46 = (bf16[256,256]{1,0:T(8,128)(2,1)S(1)}, bf16[256,256]{1,0:T(8,128)(2,1)S(1)}, u32[]{:S(2)}, u32[]{:S(2)}) collective-permute-start(bf16[256,256]{1,0:T(8,128)(2,1)S(1)} %slice.522), channel_id=1, source_target_pairs={{1,0},{2,1},{3,2},{0,3},{5,4},{6,5},{7,6},{4,7},{9,8},{10,9},{11,1... | collective-permute-start | bytes 393224 | tf_op jit(solution)/shard_map/ppermute | solution.py:200
  139.1 2.2 collective-permute-done.29
  141.3 1.6 collective-permute-start.48
  143.0 3.1 %collective-permute-done.18 = bf16[512,256]{1,0:T(8,128)(2,1)S(1)} collective-permute-done((bf16[512,256]{1,0:T(8,128)(2,1)S(1)}, bf16[512,256]{1,0:T(8,128)(2,1)S(1)}, u32[]{:S(2)}, u32[]{:S(2)}) %collective-permute-start.18) | collective-permute-done | bytes 262176 | tf_op jit(solution)/shard_map/ppermute | solution.py:200
  146.1 4.3 %collective-permute-start.37 = (bf16[256,256]{1,0:T(8,128)(2,1)S(1)}, bf16[256,256]{1,0:T(8,128)(2,1)S(1)}, u32[]{:S(2)}, u32[]{:S(2)}) collective-permute-start(bf16[256,256]{1,0:T(8,128)(2,1)S(1)} %slice.501), channel_id=1, source_target_pairs={{1,0},{2,1},{3,2},{0,3},{5,4},{6,5},{7,6},{4,7},{9,8},{10,9},{11,1... | collective-permute-start | bytes 393224 | tf_op jit(solution)/shard_map/ppermute | solution.py:200
  150.4 2.2 collective-permute-done.20
  152.6 1.6 collective-permute-start.39
  154.6 4.3 %collective-permute-start.28 = (bf16[256,256]{1,0:T(8,128)(2,1)S(1)}, bf16[256,256]{1,0:T(8,128)(2,1)S(1)}, u32[]{:S(2)}, u32[]{:S(2)}) collective-permute-start(bf16[256,256]{1,0:T(8,128)(2,1)S(1)} %slice.480), channel_id=1, source_target_pairs={{1,0},{2,1},{3,2},{0,3},{5,4},{6,5},{7,6},{4,7},{9,8},{10,9},{11,1... | collective-permute-start | bytes 393224 | tf_op jit(solution)/shard_map/ppermute | solution.py:200
  159.9 4.9 %project.7 = bf16[512,2048]{1,0:T(8,128)(2,1)S(1)} custom-call(s32[8]{0:T(128)S(1)} %pad_add_fusion.order_ref, bf16[8,128,2048]{2,1,0:T(8,128)(2,1)S(1)} %copy-done, bf16[512,128]{1,0:T(8,128)(2,1)S(1)} %get-tuple-element.72.refs_0_, bf16[512,128]{1,0:T(8,128)(2,1)S(1)} %get-tuple-element.71.refs_1_, bf16[512,128]{1,0:T(8,128)(2,1)S(1)} %get-tuple-element.70.refs_2_, ...), custom_call_target="tpu_custom_call" | custom-call | flops 2147483648 | bytes 7340032 | tf_op jit(solution)/shard_map/project/pallas_call | solution.py:174
  164.9 2.9 %collective-permute-start.19 = (bf16[256,256]{1,0:T(8,128)(2,1)S(1)}, bf16[256,256]{1,0:T(8,128)(2,1)S(1)}, u32[]{:S(2)}, u32[]{:S(2)}) collective-permute-start(bf16[256,256]{1,0:T(8,128)(2,1)S(1)} %slice.459), channel_id=1, source_target_pairs={{1,0},{2,1},{3,2},{0,3},{5,4},{6,5},{7,6},{4,7},{9,8},{10,9},{11,1... | collective-permute-start | bytes 393224 | tf_op jit(solution)/shard_map/ppermute | solution.py:200
  168.0 4.9 %project.6 = bf16[512,2048]{1,0:T(8,128)(2,1)S(1)} custom-call(s32[8]{0:T(128)S(1)} %pad_add_fusion.order_ref, bf16[8,128,2048]{2,1,0:T(8,128)(2,1)S(1)} %copy-done, bf16[512,128]{1,0:T(8,128)(2,1)S(1)} %get-tuple-element.64.refs_0_, bf16[512,128]{1,0:T(8,128)(2,1)S(1)} %get-tuple-element.63.refs_1_, bf16[512,128]{1,0:T(8,128)(2,1)S(1)} %get-tuple-element.62.refs_2_, ...), custom_call_target="tpu_custom_call" | custom-call | flops 2147483648 | bytes 7340032 | tf_op jit(solution)/shard_map/project/pallas_call | solution.py:174
  173.8 4.9 %project.5 = bf16[512,2048]{1,0:T(8,128)(2,1)S(1)} custom-call(s32[8]{0:T(128)S(1)} %pad_add_fusion.order_ref, bf16[8,128,2048]{2,1,0:T(8,128)(2,1)S(1)} %copy-done, bf16[512,128]{1,0:T(8,128)(2,1)S(1)} %get-tuple-element.56.refs_0_, bf16[512,128]{1,0:T(8,128)(2,1)S(1)} %get-tuple-element.55.refs_1_, bf16[512,128]{1,0:T(8,128)(2,1)S(1)} %get-tuple-element.54.refs_2_, ...), custom_call_target="tpu_custom_call" | custom-call | flops 2147483648 | bytes 7340032 | tf_op jit(solution)/shard_map/project/pallas_call | solution.py:174
  178.9 4.9 %project.4 = bf16[512,2048]{1,0:T(8,128)(2,1)S(1)} custom-call(s32[8]{0:T(128)S(1)} %pad_add_fusion.order_ref, bf16[8,128,2048]{2,1,0:T(8,128)(2,1)S(1)} %copy-done, bf16[512,128]{1,0:T(8,128)(2,1)S(1)} %get-tuple-element.48.refs_0_, bf16[512,128]{1,0:T(8,128)(2,1)S(1)} %get-tuple-element.47.refs_1_, bf16[512,128]{1,0:T(8,128)(2,1)S(1)} %get-tuple-element.46.refs_2_, ...), custom_call_target="tpu_custom_call" | custom-call | flops 2147483648 | bytes 7340032 | tf_op jit(solution)/shard_map/project/pallas_call | solution.py:174
  184.2 1.6 collective-permute-start.55
  186.0 7.0 %collective-permute-done.55 = bf16[2,256,256]{2,1,0:T(8,128)(2,1)S(1)} collective-permute-done((bf16[2,256,256]{2,1,0:T(8,128)(2,1)S(1)}, bf16[2,256,256]{2,1,0:T(8,128)(2,1)S(1)}, u32[]{:S(2)}, u32[]{:S(2)}) %collective-permute-start.55) | collective-permute-done | bytes 262176 | tf_op jit(solution)/shard_map/ppermute | solution.py:195
  192.9 1.3 collective-permute-done.57
  194.9 4.5 %collective-permute-done.58 = bf16[256,256]{1,0:T(8,128)(2,1)S(1)} collective-permute-done((bf16[256,256]{1,0:T(8,128)(2,1)S(1)}, bf16[256,256]{1,0:T(8,128)(2,1)S(1)}, u32[]{:S(2)}, u32[]{:S(2)}) %collective-permute-start.58) | collective-permute-done | bytes 131104 | tf_op jit(solution)/shard_map/ppermute | solution.py:195
  199.4 1.2 collective-permute-start.56
  200.7 3.7 %collective-permute-done.56 = bf16[256,256]{1,0:T(8,128)(2,1)S(1)} collective-permute-done((bf16[256,256]{1,0:T(8,128)(2,1)S(1)}, bf16[256,256]{1,0:T(8,128)(2,1)S(1)}, u32[]{:S(2)}, u32[]{:S(2)}) %collective-permute-start.56) | collective-permute-done | bytes 131104 | tf_op jit(solution)/shard_map/ppermute | solution.py:195
  204.5 3.9 %collective-permute-start.59 = (bf16[256,512]{1,0:T(8,128)(2,1)S(1)}, bf16[256,512]{1,0:T(8,128)(2,1)S(1)}, u32[]{:S(2)}, u32[]{:S(2)}) collective-permute-start(bf16[256,512]{1,0:T(8,128)(2,1)S(1)} %pad_maximum_fusion.3), channel_id=1, source_target_pairs={{1,0},{2,1},{3,2},{0,3},{5,4},{6,5},{7,6},{4,7},{9,8},{10,9},{11,1... | collective-permute-start | bytes 786440 | tf_op jit(solution)/shard_map/ppermute | solution.py:200
  209.2 1.3 collective-permute-start.50
  211.8 1.4 collective-permute-start.41
  213.6 4.8 %collective-permute-done.61 = bf16[256,512]{1,0:T(8,128)(2,1)S(1)} collective-permute-done((bf16[256,512]{1,0:T(8,128)(2,1)S(1)}, bf16[256,512]{1,0:T(8,128)(2,1)S(1)}, u32[]{:S(2)}, u32[]{:S(2)}) %collective-permute-start.61) | collective-permute-done | bytes 262176 | tf_op jit(solution)/shard_map/ppermute | solution.py:200
  218.4 2.0 collective-permute-start.62
  220.4 1.9 collective-permute-start.60
  222.4 3.1 %collective-permute-done.62 = bf16[128,512]{1,0:T(8,128)(2,1)S(1)} collective-permute-done((bf16[128,512]{1,0:T(8,128)(2,1)S(1)}, bf16[128,512]{1,0:T(8,128)(2,1)S(1)}, u32[]{:S(2)}, u32[]{:S(2)}) %collective-permute-start.62) | collective-permute-done | bytes 131104 | tf_op jit(solution)/shard_map/ppermute | solution.py:200
  225.4 2.1 collective-permute-start.43
  231.0 1.7 collective-permute-start.23
  234.6 1.6 collective-permute-start.53
  237.6 2.6 collective-permute-done.34
  240.2 1.6 collective-permute-start.44
  242.7 3.1 %collective-permute-done.25 = bf16[2,64,1024]{2,1,0:T(8,128)(2,1)S(1)} collective-permute-done((bf16[2,64,1024]{2,1,0:T(8,128)(2,1)S(1)}, bf16[2,64,1024]{2,1,0:T(8,128)(2,1)S(1)}, u32[]{:S(2)}, u32[]{:S(2)}) %collective-permute-start.25) | collective-permute-done | bytes 262176 | tf_op jit(solution)/shard_map/ppermute | solution.py:195
  245.8 1.6 collective-permute-start.35
  248.6 1.8 collective-permute-start.26
  251.3 1.5 collective-permute-done.33
  253.6 1.9 collective-permute-done.24
  (203 shorter events, 33.1 us)
Async XLA Ops:
  2.4 11.5 %collective-permute-start.9 = (bf16[256,512]{1,0:T(8,128)(2,1)}, bf16[256,512]{1,0:T(8,128)(2,1)}, u32[]{:S(2)}, u32[]{:S(2)}) collective-permute-start(bf16[256,512]{1,0:T(8,128)(2,1)} %get-tuple-element.74), channel_id=1, source_target_pairs={{0,24},{4,28},{8,16},{12,20},{16,8},{20,12},{24,0},{28,4},{1,25},{... | collective-permute-start | bytes 786440 | tf_op jit(solution)/shard_map/ppermute | solution.py:195
  6.3 12.2 %collective-permute-start.8 = (bf16[256,512]{1,0:T(8,128)(2,1)}, bf16[256,512]{1,0:T(8,128)(2,1)}, u32[]{:S(2)}, u32[]{:S(2)}) collective-permute-start(bf16[256,512]{1,0:T(8,128)(2,1)} %get-tuple-element.74), channel_id=1, source_target_pairs={{0,16},{4,20},{8,24},{12,28},{16,0},{20,4},{24,8},{28,12},{1,17},{... | collective-permute-start | bytes 786440 | tf_op jit(solution)/shard_map/ppermute | solution.py:195
  6.8 13.4 %collective-permute-start.7 = (bf16[256,512]{1,0:T(8,128)(2,1)}, bf16[256,512]{1,0:T(8,128)(2,1)}, u32[]{:S(2)}, u32[]{:S(2)}) collective-permute-start(bf16[256,512]{1,0:T(8,128)(2,1)} %get-tuple-element.74), channel_id=1, source_target_pairs={{0,8},{4,12},{8,0},{12,4},{16,24},{20,28},{24,16},{28,20},{1,9},{5... | collective-permute-start | bytes 786440 | tf_op jit(solution)/shard_map/ppermute | solution.py:195
  10.6 11.0 %collective-permute-start = (bf16[128,2048]{1,0:T(8,128)(2,1)}, bf16[128,2048]{1,0:T(8,128)(2,1)S(1)}, u32[]{:S(2)}, u32[]{:S(2)}) collective-permute-start(bf16[128,2048]{1,0:T(8,128)(2,1)} %get-tuple-element.13), channel_id=1, source_target_pairs={{0,4},{4,0},{8,12},{12,8},{16,20},{20,16},{24,28},{28,24},{1,5},{5... | collective-permute-start | bytes 1572872 | tf_op jit(solution)/shard_map/ppermute | solution.py:195
  10.6 20.5 %collective-permute-start.1 = (bf16[128,2048]{1,0:T(8,128)(2,1)}, bf16[128,2048]{1,0:T(8,128)(2,1)S(1)}, u32[]{:S(2)}, u32[]{:S(2)}) collective-permute-start(bf16[128,2048]{1,0:T(8,128)(2,1)} %get-tuple-element.12), channel_id=1, source_target_pairs={{0,8},{4,12},{8,0},{12,4},{16,24},{20,28},{24,16},{28,20},{1,9},{5... | collective-permute-start | bytes 1572872 | tf_op jit(solution)/shard_map/ppermute | solution.py:195
  13.9 27.5 %collective-permute-start.2 = (bf16[128,2048]{1,0:T(8,128)(2,1)}, bf16[128,2048]{1,0:T(8,128)(2,1)S(1)}, u32[]{:S(2)}, u32[]{:S(2)}) collective-permute-start(bf16[128,2048]{1,0:T(8,128)(2,1)} %get-tuple-element.11), channel_id=1, source_target_pairs={{0,12},{4,8},{8,4},{12,0},{16,28},{20,24},{24,20},{28,16},{1,13},{... | collective-permute-start | bytes 1572872 | tf_op jit(solution)/shard_map/ppermute | solution.py:195
  18.5 24.8 %collective-permute-start.3 = (bf16[128,2048]{1,0:T(8,128)(2,1)S(1)}, bf16[128,2048]{1,0:T(8,128)(2,1)S(1)}, u32[]{:S(2)}, u32[]{:S(2)}) collective-permute-start(bf16[128,2048]{1,0:T(8,128)(2,1)S(1)} %get-tuple-element.10), channel_id=1, source_target_pairs={{0,16},{4,20},{8,24},{12,28},{16,0},{20,4},{24,8},{28,12},{1,17},{... | collective-permute-start | bytes 1572872 | tf_op jit(solution)/shard_map/ppermute | solution.py:195
  20.2 45.1 %collective-permute-start.4 = (bf16[128,2048]{1,0:T(8,128)(2,1)S(1)}, bf16[128,2048]{1,0:T(8,128)(2,1)S(1)}, u32[]{:S(2)}, u32[]{:S(2)}) collective-permute-start(bf16[128,2048]{1,0:T(8,128)(2,1)S(1)} %get-tuple-element.9), channel_id=1, source_target_pairs={{0,20},{4,16},{8,28},{12,24},{16,4},{20,0},{24,12},{28,8},{1,21},{... | collective-permute-start | bytes 1572872 | tf_op jit(solution)/shard_map/ppermute | solution.py:195
  21.5 44.6 %collective-permute-start.5 = (bf16[128,2048]{1,0:T(8,128)(2,1)S(1)}, bf16[128,2048]{1,0:T(8,128)(2,1)S(1)}, u32[]{:S(2)}, u32[]{:S(2)}) collective-permute-start(bf16[128,2048]{1,0:T(8,128)(2,1)S(1)} %get-tuple-element.8), channel_id=1, source_target_pairs={{0,24},{4,28},{8,16},{12,20},{16,8},{20,12},{24,0},{28,4},{1,25},{... | collective-permute-start | bytes 1572872 | tf_op jit(solution)/shard_map/ppermute | solution.py:195
  31.1 35.9 %collective-permute-start.6 = (bf16[128,2048]{1,0:T(8,128)(2,1)S(1)}, bf16[128,2048]{1,0:T(8,128)(2,1)S(1)}, u32[]{:S(2)}, u32[]{:S(2)}) collective-permute-start(bf16[128,2048]{1,0:T(8,128)(2,1)S(1)} %get-tuple-element.7), channel_id=1, source_target_pairs={{0,28},{4,24},{8,20},{12,16},{16,12},{20,8},{24,4},{28,0},{1,29},{... | collective-permute-start | bytes 1572872 | tf_op jit(solution)/shard_map/ppermute | solution.py:195
  41.4 26.5 %collective-permute-start.10 = (bf16[4,256,512]{2,1,0:T(8,128)(2,1)S(1)}, bf16[4,256,512]{2,1,0:T(8,128)(2,1)S(1)}, u32[]{:S(2)}, u32[]{:S(2)}) collective-permute-start(bf16[4,256,512]{2,1,0:T(8,128)(2,1)S(1)} %get-tuple-element.40), channel_id=1, source_target_pairs={{0,4},{4,0},{8,12},{12,8},{16,20},{20,16},{24,28},{28,24},{1,5},{5... | collective-permute-start | bytes 3145736 | tf_op jit(solution)/shard_map/ppermute | solution.py:195
  85.1 4.2 %collective-permute-start.11 = (bf16[2,256,128]{2,1,0:T(8,128)(2,1)S(1)}, bf16[2,256,128]{2,1,0:T(8,128)(2,1)S(1)}, u32[]{:S(2)}, u32[]{:S(2)}) collective-permute-start(bf16[2,256,128]{2,1,0:T(8,128)(2,1)S(1)} %get-tuple-element.37), channel_id=1, source_target_pairs={{0,4},{4,0},{8,12},{12,8},{16,20},{20,16},{24,28},{28,24},{1,5},{5... | collective-permute-start | bytes 393224 | tf_op jit(solution)/shard_map/ppermute | solution.py:195
  85.7 6.3 %collective-permute-start.12 = (bf16[2,256,128]{2,1,0:T(8,128)(2,1)S(1)}, bf16[2,256,128]{2,1,0:T(8,128)(2,1)S(1)}, u32[]{:S(2)}, u32[]{:S(2)}) collective-permute-start(bf16[2,256,128]{2,1,0:T(8,128)(2,1)S(1)} %get-tuple-element.36), channel_id=1, source_target_pairs={{0,8},{4,12},{8,0},{12,4},{16,24},{20,28},{24,16},{28,20},{1,9},{5... | collective-permute-start | bytes 393224 | tf_op jit(solution)/shard_map/ppermute | solution.py:195
  87.4 6.7 %collective-permute-start.13 = (bf16[2,256,128]{2,1,0:T(8,128)(2,1)S(1)}, bf16[2,256,128]{2,1,0:T(8,128)(2,1)S(1)}, u32[]{:S(2)}, u32[]{:S(2)}) collective-permute-start(bf16[2,256,128]{2,1,0:T(8,128)(2,1)S(1)} %get-tuple-element.35), channel_id=1, source_target_pairs={{0,12},{4,8},{8,4},{12,0},{16,28},{20,24},{24,20},{28,16},{1,13},{... | collective-permute-start | bytes 393224 | tf_op jit(solution)/shard_map/ppermute | solution.py:195
  87.4 7.5 %collective-permute-start.14 = (bf16[2,256,128]{2,1,0:T(8,128)(2,1)S(1)}, bf16[2,256,128]{2,1,0:T(8,128)(2,1)S(1)}, u32[]{:S(2)}, u32[]{:S(2)}) collective-permute-start(bf16[2,256,128]{2,1,0:T(8,128)(2,1)S(1)} %get-tuple-element.34), channel_id=1, source_target_pairs={{0,16},{4,20},{8,24},{12,28},{16,0},{20,4},{24,8},{28,12},{1,17},{... | collective-permute-start | bytes 393224 | tf_op jit(solution)/shard_map/ppermute | solution.py:195
  88.9 12.4 %collective-permute-start.15 = (bf16[2,256,128]{2,1,0:T(8,128)(2,1)S(1)}, bf16[2,256,128]{2,1,0:T(8,128)(2,1)S(1)}, u32[]{:S(2)}, u32[]{:S(2)}) collective-permute-start(bf16[2,256,128]{2,1,0:T(8,128)(2,1)S(1)} %get-tuple-element.33), channel_id=1, source_target_pairs={{0,20},{4,16},{8,28},{12,24},{16,4},{20,0},{24,12},{28,8},{1,21},{... | collective-permute-start | bytes 393224 | tf_op jit(solution)/shard_map/ppermute | solution.py:195
  89.3 12.0 %collective-permute-start.16 = (bf16[2,256,128]{2,1,0:T(8,128)(2,1)S(1)}, bf16[2,256,128]{2,1,0:T(8,128)(2,1)S(1)}, u32[]{:S(2)}, u32[]{:S(2)}) collective-permute-start(bf16[2,256,128]{2,1,0:T(8,128)(2,1)S(1)} %get-tuple-element.32), channel_id=1, source_target_pairs={{0,24},{4,28},{8,16},{12,20},{16,8},{20,12},{24,0},{28,4},{1,25},{... | collective-permute-start | bytes 393224 | tf_op jit(solution)/shard_map/ppermute | solution.py:195
  92.0 9.3 %collective-permute-start.17 = (bf16[2,256,128]{2,1,0:T(8,128)(2,1)S(1)}, bf16[2,256,128]{2,1,0:T(8,128)(2,1)S(1)}, u32[]{:S(2)}, u32[]{:S(2)}) collective-permute-start(bf16[2,256,128]{2,1,0:T(8,128)(2,1)S(1)} %get-tuple-element.31), channel_id=1, source_target_pairs={{0,28},{4,24},{8,20},{12,16},{16,12},{20,8},{24,4},{28,0},{1,29},{... | collective-permute-start | bytes 393224 | tf_op jit(solution)/shard_map/ppermute | solution.py:195
  94.1 89.7 %collective-permute-start.54 = (bf16[2,2,256,512]{3,2,1,0:T(8,128)(2,1)S(1)}, bf16[2,2,256,512]{3,2,1,0:T(8,128)(2,1)S(1)}, u32[]{:S(2)}, u32[]{:S(2)}) collective-permute-start(bf16[2,2,256,512]{3,2,1,0:T(8,128)(2,1)S(1)} %slice_bitcast_fusion), channel_id=1, source_target_pairs={{0,4},{4,0},{8,12},{12,8},{16,20},{20,16},{24,28},{28,24},{1,5},{5... | collective-permute-start | bytes 3145736 | tf_op jit(solution)/shard_map/ppermute | solution.py:195
  101.6 10.7 %collective-permute-start.45 = (bf16[512,256]{1,0:T(8,128)(2,1)S(1)}, bf16[512,256]{1,0:T(8,128)(2,1)S(1)}, u32[]{:S(2)}, u32[]{:S(2)}) collective-permute-start(bf16[512,256]{1,0:T(8,128)(2,1)S(1)} %bitcast.364), channel_id=1, source_target_pairs={{1,0},{2,1},{3,2},{0,3},{5,4},{6,5},{7,6},{4,7},{9,8},{10,9},{11,1... | collective-permute-start | bytes 786440 | tf_op jit(solution)/shard_map/ppermute | solution.py:200
  105.5 13.2 %collective-permute-start.47 = (bf16[512,256]{1,0:T(8,128)(2,1)S(1)}, bf16[512,256]{1,0:T(8,128)(2,1)S(1)}, u32[]{:S(2)}, u32[]{:S(2)}) collective-permute-start(bf16[512,256]{1,0:T(8,128)(2,1)S(1)} %bitcast.365), channel_id=1, source_target_pairs={{3,0},{0,1},{1,2},{2,3},{7,4},{4,5},{5,6},{6,7},{11,8},{8,9},{9,10... | collective-permute-start | bytes 786440 | tf_op jit(solution)/shard_map/ppermute | solution.py:200
  105.6 17.9 %collective-permute-start.36 = (bf16[512,256]{1,0:T(8,128)(2,1)S(1)}, bf16[512,256]{1,0:T(8,128)(2,1)S(1)}, u32[]{:S(2)}, u32[]{:S(2)}) collective-permute-start(bf16[512,256]{1,0:T(8,128)(2,1)S(1)} %bitcast.361), channel_id=1, source_target_pairs={{1,0},{2,1},{3,2},{0,3},{5,4},{6,5},{7,6},{4,7},{9,8},{10,9},{11,1... | collective-permute-start | bytes 786440 | tf_op jit(solution)/shard_map/ppermute | solution.py:200
  109.5 20.5 %collective-permute-start.38 = (bf16[512,256]{1,0:T(8,128)(2,1)S(1)}, bf16[512,256]{1,0:T(8,128)(2,1)S(1)}, u32[]{:S(2)}, u32[]{:S(2)}) collective-permute-start(bf16[512,256]{1,0:T(8,128)(2,1)S(1)} %bitcast.362), channel_id=1, source_target_pairs={{3,0},{0,1},{1,2},{2,3},{7,4},{4,5},{5,6},{6,7},{11,8},{8,9},{9,10... | collective-permute-start | bytes 786440 | tf_op jit(solution)/shard_map/ppermute | solution.py:200
  112.3 22.6 %collective-permute-start.27 = (bf16[512,256]{1,0:T(8,128)(2,1)S(1)}, bf16[512,256]{1,0:T(8,128)(2,1)S(1)}, u32[]{:S(2)}, u32[]{:S(2)}) collective-permute-start(bf16[512,256]{1,0:T(8,128)(2,1)S(1)} %bitcast.358), channel_id=1, source_target_pairs={{1,0},{2,1},{3,2},{0,3},{5,4},{6,5},{7,6},{4,7},{9,8},{10,9},{11,1... | collective-permute-start | bytes 786440 | tf_op jit(solution)/shard_map/ppermute | solution.py:200
  118.8 22.6 %collective-permute-start.29 = (bf16[512,256]{1,0:T(8,128)(2,1)S(1)}, bf16[512,256]{1,0:T(8,128)(2,1)S(1)}, u32[]{:S(2)}, u32[]{:S(2)}) collective-permute-start(bf16[512,256]{1,0:T(8,128)(2,1)S(1)} %bitcast.359), channel_id=1, source_target_pairs={{3,0},{0,1},{1,2},{2,3},{7,4},{4,5},{5,6},{6,7},{11,8},{8,9},{9,10... | collective-permute-start | bytes 786440 | tf_op jit(solution)/shard_map/ppermute | solution.py:200
  123.5 22.6 %collective-permute-start.18 = (bf16[512,256]{1,0:T(8,128)(2,1)S(1)}, bf16[512,256]{1,0:T(8,128)(2,1)S(1)}, u32[]{:S(2)}, u32[]{:S(2)}) collective-permute-start(bf16[512,256]{1,0:T(8,128)(2,1)S(1)} %bitcast.355), channel_id=1, source_target_pairs={{1,0},{2,1},{3,2},{0,3},{5,4},{6,5},{7,6},{4,7},{9,8},{10,9},{11,1... | collective-permute-start | bytes 786440 | tf_op jit(solution)/shard_map/ppermute | solution.py:200
  130.0 22.6 %collective-permute-start.20 = (bf16[512,256]{1,0:T(8,128)(2,1)S(1)}, bf16[512,256]{1,0:T(8,128)(2,1)S(1)}, u32[]{:S(2)}, u32[]{:S(2)}) collective-permute-start(bf16[512,256]{1,0:T(8,128)(2,1)S(1)} %bitcast.356), channel_id=1, source_target_pairs={{3,0},{0,1},{1,2},{2,3},{7,4},{4,5},{5,6},{6,7},{11,8},{8,9},{9,10... | collective-permute-start | bytes 786440 | tf_op jit(solution)/shard_map/ppermute | solution.py:200
  134.8 19.7 %collective-permute-start.46 = (bf16[256,256]{1,0:T(8,128)(2,1)S(1)}, bf16[256,256]{1,0:T(8,128)(2,1)S(1)}, u32[]{:S(2)}, u32[]{:S(2)}) collective-permute-start(bf16[256,256]{1,0:T(8,128)(2,1)S(1)} %slice.522), channel_id=1, source_target_pairs={{1,0},{2,1},{3,2},{0,3},{5,4},{6,5},{7,6},{4,7},{9,8},{10,9},{11,1... | collective-permute-start | bytes 393224 | tf_op jit(solution)/shard_map/ppermute | solution.py:200
  139.1 20.8 %copy-start = (bf16[8,128,2048]{2,1,0:T(8,128)(2,1)S(1)}, bf16[8,128,2048]{2,1,0:T(8,128)(2,1)}, u32[]{:S(2)}) copy-start(bf16[8,128,2048]{2,1,0:T(8,128)(2,1)} %bitcast_dynamic-update-slice_fusion.w_ref) | copy-start | bytes 12582916
  141.3 17.5 %collective-permute-start.48 = (bf16[256,256]{1,0:T(8,128)(2,1)S(1)}, bf16[256,256]{1,0:T(8,128)(2,1)S(1)}, u32[]{:S(2)}, u32[]{:S(2)}) collective-permute-start(bf16[256,256]{1,0:T(8,128)(2,1)S(1)} %slice.523), channel_id=1, source_target_pairs={{3,0},{0,1},{1,2},{2,3},{7,4},{4,5},{5,6},{6,7},{11,8},{8,9},{9,10... | collective-permute-start | bytes 393224 | tf_op jit(solution)/shard_map/ppermute | solution.py:200
  146.1 18.8 %collective-permute-start.37 = (bf16[256,256]{1,0:T(8,128)(2,1)S(1)}, bf16[256,256]{1,0:T(8,128)(2,1)S(1)}, u32[]{:S(2)}, u32[]{:S(2)}) collective-permute-start(bf16[256,256]{1,0:T(8,128)(2,1)S(1)} %slice.501), channel_id=1, source_target_pairs={{1,0},{2,1},{3,2},{0,3},{5,4},{6,5},{7,6},{4,7},{9,8},{10,9},{11,1... | collective-permute-start | bytes 393224 | tf_op jit(solution)/shard_map/ppermute | solution.py:200
  152.6 15.3 %collective-permute-start.39 = (bf16[256,256]{1,0:T(8,128)(2,1)S(1)}, bf16[256,256]{1,0:T(8,128)(2,1)S(1)}, u32[]{:S(2)}, u32[]{:S(2)}) collective-permute-start(bf16[256,256]{1,0:T(8,128)(2,1)S(1)} %slice.502), channel_id=1, source_target_pairs={{3,0},{0,1},{1,2},{2,3},{7,4},{4,5},{5,6},{6,7},{11,8},{8,9},{9,10... | collective-permute-start | bytes 393224 | tf_op jit(solution)/shard_map/ppermute | solution.py:200
  154.6 18.5 %collective-permute-start.28 = (bf16[256,256]{1,0:T(8,128)(2,1)S(1)}, bf16[256,256]{1,0:T(8,128)(2,1)S(1)}, u32[]{:S(2)}, u32[]{:S(2)}) collective-permute-start(bf16[256,256]{1,0:T(8,128)(2,1)S(1)} %slice.480), channel_id=1, source_target_pairs={{1,0},{2,1},{3,2},{0,3},{5,4},{6,5},{7,6},{4,7},{9,8},{10,9},{11,1... | collective-permute-start | bytes 393224 | tf_op jit(solution)/shard_map/ppermute | solution.py:200
  158.9 14.3 %collective-permute-start.30 = (bf16[256,256]{1,0:T(8,128)(2,1)S(1)}, bf16[256,256]{1,0:T(8,128)(2,1)S(1)}, u32[]{:S(2)}, u32[]{:S(2)}) collective-permute-start(bf16[256,256]{1,0:T(8,128)(2,1)S(1)} %slice.481), channel_id=1, source_target_pairs={{3,0},{0,1},{1,2},{2,3},{7,4},{4,5},{5,6},{6,7},{11,8},{8,9},{9,10... | collective-permute-start | bytes 393224 | tf_op jit(solution)/shard_map/ppermute | solution.py:200
  164.9 13.8 %collective-permute-start.19 = (bf16[256,256]{1,0:T(8,128)(2,1)S(1)}, bf16[256,256]{1,0:T(8,128)(2,1)S(1)}, u32[]{:S(2)}, u32[]{:S(2)}) collective-permute-start(bf16[256,256]{1,0:T(8,128)(2,1)S(1)} %slice.459), channel_id=1, source_target_pairs={{1,0},{2,1},{3,2},{0,3},{5,4},{6,5},{7,6},{4,7},{9,8},{10,9},{11,1... | collective-permute-start | bytes 393224 | tf_op jit(solution)/shard_map/ppermute | solution.py:200
  167.9 11.0 %collective-permute-start.21 = (bf16[256,256]{1,0:T(8,128)(2,1)S(1)}, bf16[256,256]{1,0:T(8,128)(2,1)S(1)}, u32[]{:S(2)}, u32[]{:S(2)}) collective-permute-start(bf16[256,256]{1,0:T(8,128)(2,1)S(1)} %slice.460), channel_id=1, source_target_pairs={{3,0},{0,1},{1,2},{2,3},{7,4},{4,5},{5,6},{6,7},{11,8},{8,9},{9,10... | collective-permute-start | bytes 393224 | tf_op jit(solution)/shard_map/ppermute | solution.py:200
  173.1 35.3 %collective-permute-start.49 = (bf16[2,2,64,2048]{3,2,1,0:T(8,128)(2,1)S(1)}, bf16[2,2,64,2048]{3,2,1,0:T(8,128)(2,1)S(1)}, u32[]{:S(2)}, u32[]{:S(2)}) collective-permute-start(bf16[2,2,64,2048]{3,2,1,0:T(8,128)(2,1)S(1)} %slice_bitcast_fusion.2), channel_id=1, source_target_pairs={{0,4},{4,0},{8,12},{12,8},{16,20},{20,16},{24,28},{28,24},{1,5},{5... | collective-permute-start | bytes 3145736 | tf_op jit(solution)/shard_map/ppermute | solution.py:195
  173.2 35.6 %collective-permute-start.40 = (bf16[2,2,64,2048]{3,2,1,0:T(8,128)(2,1)S(1)}, bf16[2,2,64,2048]{3,2,1,0:T(8,128)(2,1)S(1)}, u32[]{:S(2)}, u32[]{:S(2)}) collective-permute-start(bf16[2,2,64,2048]{3,2,1,0:T(8,128)(2,1)S(1)} %slice_bitcast_fusion.4), channel_id=1, source_target_pairs={{0,4},{4,0},{8,12},{12,8},{16,20},{20,16},{24,28},{28,24},{1,5},{5... | collective-permute-start | bytes 3145736 | tf_op jit(solution)/shard_map/ppermute | solution.py:195
  178.8 31.8 %collective-permute-start.31 = (bf16[2,2,64,2048]{3,2,1,0:T(8,128)(2,1)S(1)}, bf16[2,2,64,2048]{3,2,1,0:T(8,128)(2,1)S(1)}, u32[]{:S(2)}, u32[]{:S(2)}) collective-permute-start(bf16[2,2,64,2048]{3,2,1,0:T(8,128)(2,1)S(1)} %slice_bitcast_fusion.6), channel_id=1, source_target_pairs={{0,4},{4,0},{8,12},{12,8},{16,20},{20,16},{24,28},{28,24},{1,5},{5... | collective-permute-start | bytes 3145736 | tf_op jit(solution)/shard_map/ppermute | solution.py:195
  184.2 8.8 %collective-permute-start.55 = (bf16[2,256,256]{2,1,0:T(8,128)(2,1)S(1)}, bf16[2,256,256]{2,1,0:T(8,128)(2,1)S(1)}, u32[]{:S(2)}, u32[]{:S(2)}) collective-permute-start(bf16[2,256,256]{2,1,0:T(8,128)(2,1)S(1)} %slice_bitcast_fusion.12), channel_id=1, source_target_pairs={{0,8},{4,12},{8,0},{12,4},{16,24},{20,28},{24,16},{28,20},{1,9},{5... | collective-permute-start | bytes 786440 | tf_op jit(solution)/shard_map/ppermute | solution.py:195
  185.8 8.4 %collective-permute-start.57 = (bf16[2,256,256]{2,1,0:T(8,128)(2,1)S(1)}, bf16[2,256,256]{2,1,0:T(8,128)(2,1)S(1)}, u32[]{:S(2)}, u32[]{:S(2)}) collective-permute-start(bf16[2,256,256]{2,1,0:T(8,128)(2,1)S(1)} %slice_bitcast_fusion.10), channel_id=1, source_target_pairs={{0,16},{4,20},{8,24},{12,28},{16,0},{20,4},{24,8},{28,12},{1,17},{... | collective-permute-start | bytes 786440 | tf_op jit(solution)/shard_map/ppermute | solution.py:195
  192.9 18.9 %collective-permute-start.22 = (bf16[2,2,64,2048]{3,2,1,0:T(8,128)(2,1)S(1)}, bf16[2,2,64,2048]{3,2,1,0:T(8,128)(2,1)S(1)}, u32[]{:S(2)}, u32[]{:S(2)}) collective-permute-start(bf16[2,2,64,2048]{3,2,1,0:T(8,128)(2,1)S(1)} %slice_bitcast_fusion.8), channel_id=1, source_target_pairs={{0,4},{4,0},{8,12},{12,8},{16,20},{20,16},{24,28},{28,24},{1,5},{5... | collective-permute-start | bytes 3145736 | tf_op jit(solution)/shard_map/ppermute | solution.py:195
  194.4 5.0 %collective-permute-start.58 = (bf16[256,256]{1,0:T(8,128)(2,1)S(1)}, bf16[256,256]{1,0:T(8,128)(2,1)S(1)}, u32[]{:S(2)}, u32[]{:S(2)}) collective-permute-start(bf16[256,256]{1,0:T(8,128)(2,1)S(1)} %slice_bitcast_fusion.34), channel_id=1, source_target_pairs={{0,8},{4,12},{8,0},{12,4},{16,24},{20,28},{24,16},{28,20},{1,9},{5... | collective-permute-start | bytes 393224 | tf_op jit(solution)/shard_map/ppermute | solution.py:195
  199.4 5.0 %collective-permute-start.56 = (bf16[256,256]{1,0:T(8,128)(2,1)S(1)}, bf16[256,256]{1,0:T(8,128)(2,1)S(1)}, u32[]{:S(2)}, u32[]{:S(2)}) collective-permute-start(bf16[256,256]{1,0:T(8,128)(2,1)S(1)} %slice_bitcast_fusion.36), channel_id=1, source_target_pairs={{0,16},{4,20},{8,24},{12,28},{16,0},{20,4},{24,8},{28,12},{1,17},{... | collective-permute-start | bytes 393224 | tf_op jit(solution)/shard_map/ppermute | solution.py:195
  204.5 16.0 %collective-permute-start.59 = (bf16[256,512]{1,0:T(8,128)(2,1)S(1)}, bf16[256,512]{1,0:T(8,128)(2,1)S(1)}, u32[]{:S(2)}, u32[]{:S(2)}) collective-permute-start(bf16[256,512]{1,0:T(8,128)(2,1)S(1)} %pad_maximum_fusion.3), channel_id=1, source_target_pairs={{1,0},{2,1},{3,2},{0,3},{5,4},{6,5},{7,6},{4,7},{9,8},{10,9},{11,1... | collective-permute-start | bytes 786440 | tf_op jit(solution)/shard_map/ppermute | solution.py:200
  208.3 10.1 %collective-permute-start.61 = (bf16[256,512]{1,0:T(8,128)(2,1)S(1)}, bf16[256,512]{1,0:T(8,128)(2,1)S(1)}, u32[]{:S(2)}, u32[]{:S(2)}) collective-permute-start(bf16[256,512]{1,0:T(8,128)(2,1)S(1)} %pad_maximum_fusion.3), channel_id=1, source_target_pairs={{3,0},{0,1},{1,2},{2,3},{7,4},{4,5},{5,6},{6,7},{11,8},{8,9},{9,10... | collective-permute-start | bytes 786440 | tf_op jit(solution)/shard_map/ppermute | solution.py:200
  209.2 21.0 %collective-permute-start.50 = (bf16[2,64,1024]{2,1,0:T(8,128)(2,1)S(1)}, bf16[2,64,1024]{2,1,0:T(8,128)(2,1)S(1)}, u32[]{:S(2)}, u32[]{:S(2)}) collective-permute-start(bf16[2,64,1024]{2,1,0:T(8,128)(2,1)S(1)} %slice_bitcast_fusion.16), channel_id=1, source_target_pairs={{0,8},{4,12},{8,0},{12,4},{16,24},{20,28},{24,16},{28,20},{1,9},{5... | collective-permute-start | bytes 786440 | tf_op jit(solution)/shard_map/ppermute | solution.py:195
  210.5 20.5 %collective-permute-start.52 = (bf16[2,64,1024]{2,1,0:T(8,128)(2,1)S(1)}, bf16[2,64,1024]{2,1,0:T(8,128)(2,1)S(1)}, u32[]{:S(2)}, u32[]{:S(2)}) collective-permute-start(bf16[2,64,1024]{2,1,0:T(8,128)(2,1)S(1)} %slice_bitcast_fusion.14), channel_id=1, source_target_pairs={{0,16},{4,20},{8,24},{12,28},{16,0},{20,4},{24,8},{28,12},{1,17},{... | collective-permute-start | bytes 786440 | tf_op jit(solution)/shard_map/ppermute | solution.py:195
  211.8 21.2 %collective-permute-start.41 = (bf16[2,64,1024]{2,1,0:T(8,128)(2,1)S(1)}, bf16[2,64,1024]{2,1,0:T(8,128)(2,1)S(1)}, u32[]{:S(2)}, u32[]{:S(2)}) collective-permute-start(bf16[2,64,1024]{2,1,0:T(8,128)(2,1)S(1)} %slice_bitcast_fusion.21), channel_id=1, source_target_pairs={{0,8},{4,12},{8,0},{12,4},{16,24},{20,28},{24,16},{28,20},{1,9},{5... | collective-permute-start | bytes 786440 | tf_op jit(solution)/shard_map/ppermute | solution.py:195
  218.4 7.0 %collective-permute-start.62 = (bf16[128,512]{1,0:T(8,128)(2,1)S(1)}, bf16[128,512]{1,0:T(8,128)(2,1)S(1)}, u32[]{:S(2)}, u32[]{:S(2)}) collective-permute-start(bf16[128,512]{1,0:T(8,128)(2,1)S(1)} %slice.549), channel_id=1, source_target_pairs={{3,0},{0,1},{1,2},{2,3},{7,4},{4,5},{5,6},{6,7},{11,8},{8,9},{9,10... | collective-permute-start | bytes 393224 | tf_op jit(solution)/shard_map/ppermute | solution.py:200
  220.4 7.1 %collective-permute-start.60 = (bf16[128,512]{1,0:T(8,128)(2,1)S(1)}, bf16[128,512]{1,0:T(8,128)(2,1)S(1)}, u32[]{:S(2)}, u32[]{:S(2)}) collective-permute-start(bf16[128,512]{1,0:T(8,128)(2,1)S(1)} %slice.548), channel_id=1, source_target_pairs={{1,0},{2,1},{3,2},{0,3},{5,4},{6,5},{7,6},{4,7},{9,8},{10,9},{11,1... | collective-permute-start | bytes 393224 | tf_op jit(solution)/shard_map/ppermute | solution.py:200
  225.4 9.1 %collective-permute-start.43 = (bf16[2,64,1024]{2,1,0:T(8,128)(2,1)S(1)}, bf16[2,64,1024]{2,1,0:T(8,128)(2,1)S(1)}, u32[]{:S(2)}, u32[]{:S(2)}) collective-permute-start(bf16[2,64,1024]{2,1,0:T(8,128)(2,1)S(1)} %slice_bitcast_fusion.19), channel_id=1, source_target_pairs={{0,16},{4,20},{8,24},{12,28},{16,0},{20,4},{24,8},{28,12},{1,17},{... | collective-permute-start | bytes 786440 | tf_op jit(solution)/shard_map/ppermute | solution.py:195
  227.5 9.0 %collective-permute-start.32 = (bf16[2,64,1024]{2,1,0:T(8,128)(2,1)S(1)}, bf16[2,64,1024]{2,1,0:T(8,128)(2,1)S(1)}, u32[]{:S(2)}, u32[]{:S(2)}) collective-permute-start(bf16[2,64,1024]{2,1,0:T(8,128)(2,1)S(1)} %slice_bitcast_fusion.26), channel_id=1, source_target_pairs={{0,8},{4,12},{8,0},{12,4},{16,24},{20,28},{24,16},{28,20},{1,9},{5... | collective-permute-start | bytes 786440 | tf_op jit(solution)/shard_map/ppermute | solution.py:195
  230.3 9.9 %collective-permute-start.34 = (bf16[2,64,1024]{2,1,0:T(8,128)(2,1)S(1)}, bf16[2,64,1024]{2,1,0:T(8,128)(2,1)S(1)}, u32[]{:S(2)}, u32[]{:S(2)}) collective-permute-start(bf16[2,64,1024]{2,1,0:T(8,128)(2,1)S(1)} %slice_bitcast_fusion.24), channel_id=1, source_target_pairs={{0,16},{4,20},{8,24},{12,28},{16,0},{20,4},{24,8},{28,12},{1,17},{... | collective-permute-start | bytes 786440 | tf_op jit(solution)/shard_map/ppermute | solution.py:195
  231.0 11.0 %collective-permute-start.23 = (bf16[2,64,1024]{2,1,0:T(8,128)(2,1)S(1)}, bf16[2,64,1024]{2,1,0:T(8,128)(2,1)S(1)}, u32[]{:S(2)}, u32[]{:S(2)}) collective-permute-start(bf16[2,64,1024]{2,1,0:T(8,128)(2,1)S(1)} %slice_bitcast_fusion.31), channel_id=1, source_target_pairs={{0,8},{4,12},{8,0},{12,4},{16,24},{20,28},{24,16},{28,20},{1,9},{5... | collective-permute-start | bytes 786440 | tf_op jit(solution)/shard_map/ppermute | solution.py:195
  233.0 12.8 %collective-permute-start.25 = (bf16[2,64,1024]{2,1,0:T(8,128)(2,1)S(1)}, bf16[2,64,1024]{2,1,0:T(8,128)(2,1)S(1)}, u32[]{:S(2)}, u32[]{:S(2)}) collective-permute-start(bf16[2,64,1024]{2,1,0:T(8,128)(2,1)S(1)} %slice_bitcast_fusion.29), channel_id=1, source_target_pairs={{0,16},{4,20},{8,24},{12,28},{16,0},{20,4},{24,8},{28,12},{1,17},{... | collective-permute-start | bytes 786440 | tf_op jit(solution)/shard_map/ppermute | solution.py:195
  234.6 13.1 %collective-permute-start.53 = (bf16[64,1024]{1,0:T(8,128)(2,1)S(1)}, bf16[64,1024]{1,0:T(8,128)(2,1)S(1)}, u32[]{:S(2)}, u32[]{:S(2)}) collective-permute-start(bf16[64,1024]{1,0:T(8,128)(2,1)S(1)} %slice_bitcast_fusion.38), channel_id=1, source_target_pairs={{0,8},{4,12},{8,0},{12,4},{16,24},{20,28},{24,16},{28,20},{1,9},{5... | collective-permute-start | bytes 393224 | tf_op jit(solution)/shard_map/ppermute | solution.py:195
  236.6 12.1 %collective-permute-start.51 = (bf16[64,1024]{1,0:T(8,128)(2,1)S(1)}, bf16[64,1024]{1,0:T(8,128)(2,1)S(1)}, u32[]{:S(2)}, u32[]{:S(2)}) collective-permute-start(bf16[64,1024]{1,0:T(8,128)(2,1)S(1)} %slice_bitcast_fusion.40), channel_id=1, source_target_pairs={{0,16},{4,20},{8,24},{12,28},{16,0},{20,4},{24,8},{28,12},{1,17},{... | collective-permute-start | bytes 393224 | tf_op jit(solution)/shard_map/ppermute | solution.py:195
  240.2 10.3 %collective-permute-start.44 = (bf16[64,1024]{1,0:T(8,128)(2,1)S(1)}, bf16[64,1024]{1,0:T(8,128)(2,1)S(1)}, u32[]{:S(2)}, u32[]{:S(2)}) collective-permute-start(bf16[64,1024]{1,0:T(8,128)(2,1)S(1)} %slice_bitcast_fusion.42), channel_id=1, source_target_pairs={{0,8},{4,12},{8,0},{12,4},{16,24},{20,28},{24,16},{28,20},{1,9},{5... | collective-permute-start | bytes 393224 | tf_op jit(solution)/shard_map/ppermute | solution.py:195
  242.1 9.1 %collective-permute-start.42 = (bf16[64,1024]{1,0:T(8,128)(2,1)S(1)}, bf16[64,1024]{1,0:T(8,128)(2,1)S(1)}, u32[]{:S(2)}, u32[]{:S(2)}) collective-permute-start(bf16[64,1024]{1,0:T(8,128)(2,1)S(1)} %slice_bitcast_fusion.44), channel_id=1, source_target_pairs={{0,16},{4,20},{8,24},{12,28},{16,0},{20,4},{24,8},{28,12},{1,17},{... | collective-permute-start | bytes 393224 | tf_op jit(solution)/shard_map/ppermute | solution.py:195
  245.8 5.4 %collective-permute-start.35 = (bf16[64,1024]{1,0:T(8,128)(2,1)S(1)}, bf16[64,1024]{1,0:T(8,128)(2,1)S(1)}, u32[]{:S(2)}, u32[]{:S(2)}) collective-permute-start(bf16[64,1024]{1,0:T(8,128)(2,1)S(1)} %slice_bitcast_fusion.46), channel_id=1, source_target_pairs={{0,8},{4,12},{8,0},{12,4},{16,24},{20,28},{24,16},{28,20},{1,9},{5... | collective-permute-start | bytes 393224 | tf_op jit(solution)/shard_map/ppermute | solution.py:195
  247.7 5.0 %collective-permute-start.33 = (bf16[64,1024]{1,0:T(8,128)(2,1)S(1)}, bf16[64,1024]{1,0:T(8,128)(2,1)S(1)}, u32[]{:S(2)}, u32[]{:S(2)}) collective-permute-start(bf16[64,1024]{1,0:T(8,128)(2,1)S(1)} %slice_bitcast_fusion.48), channel_id=1, source_target_pairs={{0,16},{4,20},{8,24},{12,28},{16,0},{20,4},{24,8},{28,12},{1,17},{... | collective-permute-start | bytes 393224 | tf_op jit(solution)/shard_map/ppermute | solution.py:195
  248.6 5.0 %collective-permute-start.26 = (bf16[64,1024]{1,0:T(8,128)(2,1)S(1)}, bf16[64,1024]{1,0:T(8,128)(2,1)S(1)}, u32[]{:S(2)}, u32[]{:S(2)}) collective-permute-start(bf16[64,1024]{1,0:T(8,128)(2,1)S(1)} %slice_bitcast_fusion.50), channel_id=1, source_target_pairs={{0,8},{4,12},{8,0},{12,4},{16,24},{20,28},{24,16},{28,20},{1,9},{5... | collective-permute-start | bytes 393224 | tf_op jit(solution)/shard_map/ppermute | solution.py:195
  250.5 5.0 %collective-permute-start.24 = (bf16[64,1024]{1,0:T(8,128)(2,1)S(1)}, bf16[64,1024]{1,0:T(8,128)(2,1)S(1)}, u32[]{:S(2)}, u32[]{:S(2)}) collective-permute-start(bf16[64,1024]{1,0:T(8,128)(2,1)S(1)} %slice_bitcast_fusion.52), channel_id=1, source_target_pairs={{0,16},{4,20},{8,24},{12,28},{16,0},{20,4},{24,8},{28,12},{1,17},{... | collective-permute-start | bytes 393224 | tf_op jit(solution)/shard_map/ppermute | solution.py:195
  (3 other events, 8.9 us)

commit v2 on v0

v2 whole, which is shorter than its diff:
```python
import functools
import math

import jax
import jax.numpy as jnp
from jax import lax
from jax.experimental import pallas as pl
from jax.experimental.pallas import tpu as pltpu
from jax.sharding import PartitionSpec as P

H = 64
KVH = 8
HD = 128

NEG = -1e30


def attention_kernel(
    per_kv, rows, ranks, me_ref, seg_query, seg_key, q_ref, g_ref, kv_even, kv_odd,
    dq_ref, dkv_even, dkv_odd, q_rows, g_rows, q_cols, g_cols, s_all, d_all, p_low, d_low, top, total, dots,
):
    half = rows // 2
    inv_root = 1.0 / math.sqrt(HD)
    scale = inv_root * math.log2(math.e)
    me = me_ref[0]
    parity = me & 1
    contract_last = (((1,), (1,)), ((), ()))
    dkv_even[...] = jnp.zeros_like(dkv_even)
    dkv_odd[...] = jnp.zeros_like(dkv_odd)
    for side in range(2):
        here = slice(side * half, (side + 1) * half)
        blocks = me + 1 if side == 0 else ranks - me
        steps = (blocks + 1) // 2
        swap = parity if side == 0 else 1 - parity
        for p in range(per_kv):
            head = slice(p * HD, (p + 1) * HD)
            q_rows[p * half:(p + 1) * half, :] = q_ref[here, head]
            g_rows[p * half:(p + 1) * half, :] = g_ref[here, head]
        q_cols[...] = q_rows[...].T
        g_cols[...] = g_rows[...].T

        def slot(j):
            chip = j if side == 0 else ranks // 2 - 1 - j
            return chip ^ (me >> 1)

        def pair(j, first):
            at = slot(j)
            cols = slice(first, first + HD)
            return jnp.concatenate([kv_even[at, here, cols], kv_odd[at, here, cols]], axis=0)

        top[...] = jnp.full_like(top, NEG)
        total[...] = jnp.zeros_like(total)
        dots[...] = jnp.zeros_like(dots)

        def scores(j, carry):
            keys = pair(j, 0)
            vals = pair(j, HD)
            query_at = (blocks - 1) * half + lax.broadcasted_iota(jnp.int32, (half, half), 0)
            bias = []
            for block in (2 * j + swap, 2 * j + 1 - swap):
                key_at = block * half + lax.broadcasted_iota(jnp.int32, (half, half), 1)
                segs = seg_key[side * ranks + block]
                allowed = (key_at <= query_at) & (segs == seg_query[side])
                bias.append(jnp.where(allowed, 0.0, NEG))
            bias = jnp.concatenate(bias, axis=1)
            for p in range(per_kv):
                at = slice(p * half, (p + 1) * half)
                s = lax.dot_general(
                    q_rows[at, :], keys, contract_last, preferred_element_type=jnp.float32
                )
                s = s * scale + bias
                s_all[j, at, :] = s
                top[at, :] = jnp.maximum(top[at, :], jnp.maximum(s[:, :half], s[:, half:]))
                d_all[j, at, :] = lax.dot_general(
                    g_rows[at, :], vals, contract_last, preferred_element_type=jnp.float32
                )
            return carry

        lax.fori_loop(0, steps, scores, 0)
        top[...] = jnp.broadcast_to(jnp.max(top[...], axis=1, keepdims=True), top.shape)

        def sums(j, carry):
            for p in range(per_kv):
                at = slice(p * half, (p + 1) * half)
                high = top[at, :]
                s = s_all[j, at, :]
                e = jnp.exp2(s - jnp.concatenate([high, high], axis=1))
                s_all[j, at, :] = e
                total[at, :] += e[:, :half] + e[:, half:]
                ed = e * d_all[j, at, :]
                dots[at, :] += ed[:, :half] + ed[:, half:]
            return carry

        lax.fori_loop(0, steps, sums, 0)
        inverse = 1.0 / jnp.sum(total[...], axis=1, keepdims=True)
        delta = jnp.sum(dots[...], axis=1, keepdims=True) * inverse
        total[...] = jnp.broadcast_to(inverse, total.shape)
        dots[...] = jnp.broadcast_to(delta, dots.shape)
        top[...] = jnp.zeros_like(top)

        def grads(j, carry):
            keys = pair(j, 0)
            for p in range(per_kv):
                at = slice(p * half, (p + 1) * half)
                inv = total[at, :]
                dot = dots[at, :]
                prob = s_all[j, at, :] * jnp.concatenate([inv, inv], axis=1)
                p_low[at, :] = prob.astype(jnp.bfloat16)
                shifted = d_all[j, at, :] - jnp.concatenate([dot, dot], axis=1)
                d_low[at, :] = (prob * shifted).astype(jnp.bfloat16)
            top[...] += jnp.dot(d_low[...], keys, preferred_element_type=jnp.float32)
            key_part = jnp.dot(q_cols[...], d_low[...], preferred_element_type=jnp.float32)
            val_part = jnp.dot(g_cols[...], p_low[...], preferred_element_type=jnp.float32)
            key_part = (key_part * inv_root).T.astype(jnp.bfloat16)
            val_part = val_part.T.astype(jnp.bfloat16)
            at = slot(j)
            dkv_even[at, here, :HD] = key_part[:half, :]
            dkv_odd[at, here, :HD] = key_part[half:, :]
            dkv_even[at, here, HD:] = val_part[:half, :]
            dkv_odd[at, here, HD:] = val_part[half:, :]
            return carry

        lax.fori_loop(0, steps, grads, 0)
        grad = (top[...] * inv_root).astype(jnp.bfloat16)
        for p in range(per_kv):
            part, at = divmod(p, per_kv // 2)
            dq_ref[0, part, here, at * HD:(at + 1) * HD] = grad[p * half:(p + 1) * half, :]


def attention(me, seg_query, seg_key, queries, grad_attn, kv_even, kv_odd, kv_here, per_kv):
    pairs, rows, width = kv_even.shape
    ranks = 2 * pairs
    half = rows // 2
    stack = per_kv * half
    vmem = pl.BlockSpec(memory_space=pltpu.VMEM)
    heads = pl.BlockSpec((rows, per_kv * HD), lambda g: (0, g))
    kv_spec = pl.BlockSpec((pairs, rows, 2 * HD), lambda g: (0, 0, g))
    wide = per_kv // 2 * HD
    return pl.pallas_call(
        functools.partial(attention_kernel, per_kv, rows, ranks),
        out_shape=[jax.ShapeDtypeStruct((kv_here, 2, rows, wide), jnp.bfloat16)]
        + [jax.ShapeDtypeStruct((pairs, rows, width), jnp.bfloat16)] * 2,
        grid=(kv_here,),
        in_specs=[pl.BlockSpec(memory_space=pltpu.SMEM), vmem, vmem, heads, heads, kv_spec, kv_spec],
        out_specs=[pl.BlockSpec((1, 2, rows, wide), lambda g: (g, 0, 0, 0)), kv_spec, kv_spec],
        scratch_shapes=[
            pltpu.VMEM((stack, HD), jnp.bfloat16),
            pltpu.VMEM((stack, HD), jnp.bfloat16),
            pltpu.VMEM((HD, stack), jnp.bfloat16),
            pltpu.VMEM((HD, stack), jnp.bfloat16),
            pltpu.VMEM((pairs, stack, 2 * half), jnp.float32),
            pltpu.VMEM((pairs, stack, 2 * half), jnp.float32),
            pltpu.VMEM((stack, 2 * half), jnp.bfloat16),
            pltpu.VMEM((stack, 2 * half), jnp.bfloat16),
            pltpu.VMEM((stack, HD), jnp.float32),
            pltpu.VMEM((stack, HD), jnp.float32),
            pltpu.VMEM((stack, HD), jnp.float32),
        ],
        compiler_params=pltpu.CompilerParams(vmem_limit_bytes=32 << 20),
        cost_estimate=pl.CostEstimate(
            flops=14_000_000_000, bytes_accessed=8_000_000, transcendentals=3_000_000
        ),
        name="attention",
    )(me, seg_query, seg_key, queries, grad_attn, kv_even, kv_odd)


def project_kernel(slot_ref, *refs):
    even_ref, odd_ref, lhs = refs[-3:]
    count = lhs.shape[0]
    weights, parts = refs[:count], refs[count:-3]
    blocks, step, features = even_ref.shape
    for k in range(count):
        lhs[slot_ref[k]] = parts[k][...].reshape(lhs.shape[1:])
    tile = min(256, features)

    def columns(n, carry):
        at = pl.ds(pl.multiple_of(n * tile, tile), tile)
        out = jnp.dot(lhs[0], weights[0][:, at], preferred_element_type=jnp.float32)
        for k in range(1, count):
            out += jnp.dot(lhs[k], weights[k][:, at], preferred_element_type=jnp.float32)
        out = out.astype(jnp.bfloat16).reshape(2 * blocks, step, tile)
        for i in range(blocks):
            even_ref[i, :, at] = out[2 * i]
            odd_ref[i, :, at] = out[2 * i + 1]
        return carry

    lax.fori_loop(0, features // tile, columns, 0)


def project(slots, weights, parts):
    count = len(weights)
    group, step, depth = parts[0].shape
    features = weights[0].shape[1]
    smem = pl.BlockSpec(memory_space=pltpu.SMEM)
    vmem = pl.BlockSpec(memory_space=pltpu.VMEM)
    return pl.pallas_call(
        project_kernel,
        out_shape=[jax.ShapeDtypeStruct((group // 2, step, features), jnp.bfloat16)] * 2,
        in_specs=[smem] + [vmem] * (count + len(parts)),
        out_specs=[vmem, vmem],
        scratch_shapes=[pltpu.VMEM((count, group * step, depth), jnp.bfloat16)],
        compiler_params=pltpu.CompilerParams(vmem_limit_bytes=32 << 20),
        cost_estimate=pl.CostEstimate(
            flops=2 * group * step * depth * count * features,
            bytes_accessed=2 * (group * step * features + count * depth * features),
            transcendentals=0,
        ),
        name="project",
    )(slots, *weights, *parts)


def columns_kernel(col_ref, *refs):
    parts, outs = refs[:-2], refs[-2:]
    count = len(parts)
    heads = parts[0].shape[1] // (2 * HD)
    for k in range(count):
        where = lax.rem(col_ref[0] + k, count) * heads
        for i in range(2 * heads):
            at = pl.ds(pl.multiple_of((where + i // 2) * HD, HD), HD)
            outs[i % 2][:, at] = parts[k][:, i * HD:(i + 1) * HD]


def by_column(col, parts):
    rows, width = parts[0].shape
    vmem = pl.BlockSpec(memory_space=pltpu.VMEM)
    return pl.pallas_call(
        columns_kernel,
        out_shape=[jax.ShapeDtypeStruct((rows, len(parts) * width // 2), jnp.bfloat16)] * 2,
        in_specs=[pl.BlockSpec(memory_space=pltpu.SMEM)] + [vmem] * len(parts),
        out_specs=[vmem, vmem],
        name="by_column",
    )(col, *parts)


def across(block, mask):
    ranks = lax.axis_size("row")
    return lax.ppermute(block, "row", [(i, i ^ mask) for i in range(ranks)])


def turned(block, distance):
    count = lax.axis_size("col")
    return lax.ppermute(block, "col", [((i + distance) % count, i) for i in range(count)])


def opposite(ahead, behind):
    cut = ahead.shape[0] // 2
    return turned(ahead[:cut], 1), turned(behind[cut:], -1)


def added(one, two):
    return (one.astype(jnp.float32) + two.astype(jnp.float32)).astype(jnp.bfloat16)


def tied(*arrays):
    return lax.optimization_barrier(arrays)


def local(queries, keys, values, grad_attn, segment_ids, q_weight):
    rows = queries.shape[0]
    half = rows // 2
    ranks = lax.axis_size("row")
    count = lax.axis_size("col")
    heads_here = queries.shape[1] // HD
    group = H // KVH
    kv_here = max(1, heads_here // group)
    per_kv = heads_here // kv_here
    me = lax.axis_index("row")
    col = lax.axis_index("col")
    kv_first = col * heads_here // group

    mine = []
    for g in range(kv_here):
        for array in (keys, values):
            mine.append(lax.dynamic_slice_in_dim(array, (kv_first + g) * HD, HD, 1))
    mine = jnp.concatenate(mine, axis=1)
    kv_even = jnp.stack([mine] + [across(mine, d) for d in range(2, ranks, 2)])
    kv_odd = across(kv_even, 1)

    rows_w = q_weight.shape[0]
    key_segs = segment_ids.reshape(2 * ranks, 1, half)
    own = segment_ids.reshape(2 * ranks, half)
    query_segs = jnp.stack(
        [
            lax.dynamic_index_in_dim(own, me, 0, keepdims=False),
            lax.dynamic_index_in_dim(own, 2 * ranks - 1 - me, 0, keepdims=False),
        ]
    )[:, :, None]
    special = ranks == 8 and count == 4
    if special:
        cut = q_weight.reshape(4, rows_w // 4, -1)
        side = (me >> 1) & 1
        quarters = [
            lax.dynamic_index_in_dim(cut, 2 * at + i, 0, keepdims=False)
            for at in (side, 1 - side) for i in range(2)
        ]
        kv_even, kv_odd, *quarters = tied(kv_even, kv_odd, *quarters)
    dq, dkv_even, dkv_odd = attention(
        me.reshape(1), query_segs, key_segs, queries, grad_attn, kv_even, kv_odd, kv_here, per_kv
    )
    if special:
        input_grad, dkv_mine = paired(dq, dkv_even, dkv_odd, quarters, me, col)
    else:
        dq = dq.reshape(kv_here, 2, rows, -1).transpose(2, 0, 1, 3).reshape(rows, heads_here * HD)
        input_grad = jnp.dot(
            lax.all_gather(dq, "col", axis=1, tiled=True),
            lax.all_gather(q_weight, "row", axis=0, tiled=True),
            preferred_element_type=jnp.float32,
        ).astype(jnp.bfloat16)
        dkv_mine = chips_sum(added(dkv_even, across(dkv_odd, 1)))

    share = max(1, group // heads_here)
    if share == 1:
        key_grad, value_grad = by_column(
            col.reshape(1), [dkv_mine] + [turned(dkv_mine, k) for k in range(1, count)]
        )
        return (input_grad, key_grad, value_grad)
    whole = lax.all_gather(dkv_mine, "col")
    whole = whole.reshape(count // share, share, rows, -1).astype(jnp.float32)
    whole = whole.sum(axis=1).astype(jnp.bfloat16)
    key_grad = jnp.concatenate(list(whole[:, :, :HD]), axis=1)
    value_grad = jnp.concatenate(list(whole[:, :, HD:]), axis=1)
    return (input_grad, key_grad, value_grad)


def chips_sum(terms):
    total = terms[0].astype(jnp.float32)
    for i in range(1, terms.shape[0]):
        total += across(terms[i], 2 * i).astype(jnp.float32)
    return total.astype(jnp.bfloat16)


def paired(dq, dkv_even, dkv_odd, quarters, me, col):
    count = lax.axis_size("col")
    rows = dq.shape[2]
    core = me & 1
    side = (me >> 1) & 1

    keep_one, keep_two, send_one, send_two = quarters
    w_one = across(send_one, 2)
    keep_one_y = across(keep_one, 4)

    mine = lax.dynamic_index_in_dim(dq, core, 0, keepdims=False)
    theirs = across(lax.dynamic_index_in_dim(dq, 1 - core, 0, keepdims=False), 1)
    both = jnp.stack([mine, theirs], axis=1)
    keep = lax.dynamic_index_in_dim(both, side, 0, keepdims=False)
    send = lax.dynamic_index_in_dim(both, 1 - side, 0, keepdims=False)
    send, w_one, keep_one_y = tied(send, w_one, keep_one_y)
    keep_two_y = across(keep_two, 4)
    step = rows // 2
    blocks = [jnp.concatenate([keep[:, :step], across(send[:, :step], 2)], axis=0)]
    send_two, blocks[0] = tied(send_two, blocks[0])
    near = [[turned(blocks[0], 1), turned(blocks[0], -1)]]
    w_two = across(send_two, 2)
    w_one_y = across(w_one, 4)
    send, w_two = tied(send, w_two)
    blocks.append(jnp.concatenate([keep[:, step:], across(send[:, step:], 2)], axis=0))
    keep_two_y, *near[0] = tied(keep_two_y, *near[0])
    far = [opposite(*near[0])]
    blocks[1], *near[0] = tied(blocks[1], *near[0])
    near.append([turned(blocks[1], 1), turned(blocks[1], -1)])
    w_two_y = across(w_two, 4)
    dkv_terms = added(dkv_even, across(dkv_odd, 1))
    dkv_mine = chips_sum(dkv_terms)
    w_one_y, dkv_mine, *near[1] = tied(w_one_y, dkv_mine, *near[1])
    far.append(opposite(*near[1]))

    def joined(*parts):
        return jnp.concatenate(parts, axis=0)

    weights = [
        joined(keep_one, keep_two), joined(w_one, w_two),
        joined(keep_one_y, keep_two_y), joined(w_one_y, w_two_y),
    ]
    slots = ((me >> 1) ^ ((col + jnp.arange(count)) % count)).astype(jnp.int32)
    outs = []
    for c in range(2):
        parts = [blocks[c], near[c][0], jnp.concatenate(far[c], axis=0), near[c][1]]
        even, odd = project(slots, weights, parts)
        half_sum = added(even, across(odd, 1))
        outs.append(added(half_sum[0], across(half_sum[1], 2)))
    return jnp.concatenate(outs, axis=0), dkv_mine


def solution(mesh):
    placed = (
        P("row", "col"),
        P("row", None),
        P("row", None),
        P("row", "col"),
        P(),
        P("row", "col"),
    )
    return jax.shard_map(
        local,
        mesh=mesh,
        in_specs=placed,
        out_specs=(P("row", "col"), P("row", None), P("row", None)),
        check_vma=False,
    )
```

time: 566 us -> 194 us (0.34)
  waiting for transfers between devices: 302 us -> 103 us
  matrix products: 98.2 us -> 0 us
  local copies, waits for them, and re-layouts: 69 us -> 14.3 us
  other arithmetic: 43.8 us -> 4.14 us
  Pallas kernels: 0 us -> 31.3 us
  between operations: 13.9 us -> 1.05 us
    all_gather x2 -> x0, waiting for transfers between devices: 242 us -> none  [the longest x1 161 us: local(): lax.all_gather(q_weight, 'row', axis=0, tiled=True)]
    dot_general x57 -> x0, matrix products: 98.2 us -> none  [the longest x8 29.7 us: backward_block(): jnp.einsum('gpqk,kgh->qgph', dscore, key_split, preferred_element_type=jn...]
    ppermute x48 -> x32, waiting for transfers between devices: 12.1 us -> 103 us  [the longest x21 60.8 us: across(): return lax.ppermute(block, 'row', [(i, i ^ mask) for i in range(ranks)])]
    psum x1 -> x0, waiting for transfers between devices: 47.4 us -> none  [local(): lax.psum(key_wide.astype(jnp.bfloat16), 'col').astype(jnp.float32)]
    pallas_call x0 -> x4, Pallas kernels: none -> 31.3 us  [the longest x1 15.9 us: attention(): pl.pallas_call(functools.partial(attention_kernel, per_kv, rows, ranks),...]
    gather x17 -> x0, local copies, waits for them, and re-layouts: 29.5 us -> none  [the longest x16 27.6 us: block_mask(): key_segs = jnp.take(segment_ids, key_places)]
    add x24 -> x0, other arithmetic: 26.9 us -> none  [the longest x8 13.4 us: grad_turn(): key_acc + key_part]
    while x123 -> x0, local copies, waits for them, and re-layouts: 21.4 us -> none
  transfers between devices with their start and end apart: 51 -> 32, of which waited for: 12 -> 20; matrix products, arithmetic and copies ran while one was open for 30% -> 7% of each run, Pallas kernels for 0% -> 13%
where the time goes in v2:
time: 194 us; the launch traced here: 193 us
  waiting for transfers between devices  103 us (53%)
  starting transfers between devices  39.5 us (20%)
  Pallas kernels  31.3 us (16%)
  local copies, waits for them, and re-layouts  14.3 us (7%)
  other arithmetic  4.14 us (2%)
    ppermute x21, waiting for transfers between devices, across(): return lax.ppermute(block, 'row', [(i, i ^ mask) for i in range(ranks)])  60.8 us
    ppermute x11, waiting for transfers between devices, turned(): lax.ppermute(block, 'col', [((i + distance) % count, i) for i in range(co...  42.2 us
    ppermute x11, starting transfers between devices, turned(): lax.ppermute(block, 'col', [((i + distance) % count, i) for i in range(co...  20.8 us
    ppermute x21, starting transfers between devices, across(): return lax.ppermute(block, 'row', [(i, i ^ mask) for i in range(ranks)])  18.6 us
    pallas_call x1, Pallas kernels, attention(): pl.pallas_call(functools.partial(attention_kernel, per_kv, rows, ranks),...  15.9 us
    pallas_call x2, Pallas kernels, project(): pl.pallas_call(project_kernel, out_shape=[jax.ShapeDtypeStruct((group //...  13 us
    unnamed x24, local copies, waits for them, and re-layouts  6.37 us
    squeeze x1, local copies, waits for them, and re-layouts, local(): lax.dynamic_index_in_dim(cut, 2 * at + i, 0, keepdims=False)  4.53 us
  transfers between devices with their start and end apart: 32, of which 20 were waited for; matrix products, arithmetic and copies ran while one was open for 7% of the time, Pallas kernels for 13%

profile of v2, /device:TPU:0, one launch (start us, length us, event | category | flops | bytes accessed | tf_op | source)
XLA Modules:
  0.0 193.2 jit_solution(11078463027886921660)
XLA Ops:
  0.7 1.0 constant_dynamic-slice_fusion.4
  1.7 4.0 %collective-permute-start.2 = (bf16[256,512]{1,0:T(8,128)(2,1)S(1)}, bf16[256,512]{1,0:T(8,128)(2,1)S(1)}, u32[]{:S(2)}, u32[]{:S(2)}) collective-permute-start(bf16[256,512]{1,0:T(8,128)(2,1)S(1)} %get-tuple-element.85), channel_id=1, source_target_pairs={{0,24},{4,28},{8,16},{12,20},{16,8},{20,12},{24,0},{28,4},{1,25},{... | collective-permute-start | bytes 786440 | tf_op jit(solution)/shard_map/ppermute | solution.py:237
  5.6 0.5 collective-permute-start.1
  6.3 6.5 %collective-permute-done.2 = bf16[256,512]{1,0:T(8,128)(2,1)S(1)} collective-permute-done((bf16[256,512]{1,0:T(8,128)(2,1)S(1)}, bf16[256,512]{1,0:T(8,128)(2,1)S(1)}, u32[]{:S(2)}, u32[]{:S(2)}) %collective-permute-start.2) | collective-permute-done | bytes 262176 | tf_op jit(solution)/shard_map/ppermute | solution.py:237
  12.8 4.7 %collective-permute-done.1 = bf16[256,512]{1,0:T(8,128)(2,1)S(1)} collective-permute-done((bf16[256,512]{1,0:T(8,128)(2,1)S(1)}, bf16[256,512]{1,0:T(8,128)(2,1)S(1)}, u32[]{:S(2)}, u32[]{:S(2)}) %collective-permute-start.1) | collective-permute-done | bytes 262176 | tf_op jit(solution)/shard_map/ppermute | solution.py:237
  17.6 0.3 collective-permute-done
  18.3 4.5 %dynamic-slice_bitcast_fusion = (bf16[256,2048]{1,0:T(8,128)(2,1)}, bf16[256,2048]{1,0:T(8,128)(2,1)}, bf16[256,2048]{1,0:T(8,128)(2,1)}, bf16[256,2048]{1,0:T(8,128)(2,1)}) fusion(bf16[4,256,2048]{2,1,0:T(8,128)(2,1)} %bitcast.56, s32[]{:T(128)S(6)} %select_n.59, s32[]{:T(128)S(6)} %select_n.58, s32[]{:T(128)S(6)} %select_n.57, s32[]{:T(128)S(6)} %select_n.56), kind=kLoop, calls=%fused_computation.13 | loop fusion | bytes 8388624 | tf_op jit(solution)/shard_map/jit(dynamic_index_in_dim)/squeeze | solution.py:293
  22.8 1.5 collective-permute-start.5
  24.3 0.6 collective-permute-start.6
  24.9 15.9 %attention.1 = (bf16[2,2,256,512]{3,2,1,0:T(8,128)(2,1)S(1)}, bf16[4,256,512]{2,1,0:T(8,128)(2,1)S(1)}, bf16[4,256,512]{2,1,0:T(8,128)(2,1)S(1)}) custom-call(s32[1]{0:T(128)} %bitcast.9.me_ref, s32[2,128,1]{2,1,0:T(8,128)S(1)} %copy.9.seg_query, s32[16,1,128]{2,1,0:T(1,128)S(1)} %bitcast.55, bf16[256,2048]{1,0:T(8,128)(2,1)S(1)} %copy-done.1, ...), custom_call_target="tpu_custom_call" | custom-call | flops 14000000000 | bytes 8000000 | tf_op jit(solution)/shard_map/attention/pallas_call | solution.py:139
  40.9 0.9 copy-done.3
  41.8 0.5 collective-permute-start.13
  42.3 2.2 %collective-permute-done.4 = bf16[2,256,512]{2,1,0:T(8,128)(2,1)} collective-permute-done((bf16[2,256,512]{2,1,0:T(8,128)(2,1)S(1)}, bf16[2,256,512]{2,1,0:T(8,128)(2,1)}, u32[]{:S(2)}, u32[]{:S(2)}) %collective-permute-start.4) | collective-permute-done | bytes 524320 | tf_op jit(solution)/shard_map/ppermute | solution.py:237
  44.6 1.2 fusion.3
  45.8 2.9 %collective-permute-done.5 = bf16[256,2048]{1,0:T(8,128)(2,1)} collective-permute-done((bf16[256,2048]{1,0:T(8,128)(2,1)}, bf16[256,2048]{1,0:T(8,128)(2,1)}, u32[]{:S(2)}, u32[]{:S(2)}) %collective-permute-start.5) | collective-permute-done | bytes 1048608 | tf_op jit(solution)/shard_map/ppermute | solution.py:237
  48.7 1.2 collective-permute-done.6
  49.9 0.6 collective-permute-start.7
  50.5 1.5 collective-permute-start.9
  52.1 5.5 %collective-permute-done.7 = bf16[2,128,512]{2,1,0:T(8,128)(2,1)S(1)} collective-permute-done((bf16[2,128,512]{2,1,0:T(8,128)(2,1)S(1)}, bf16[2,128,512]{2,1,0:T(8,128)(2,1)S(1)}, u32[]{:S(2)}, u32[]{:S(2)}) %collective-permute-start.7) | collective-permute-done | bytes 262176 | tf_op jit(solution)/shard_map/ppermute | solution.py:237
  57.6 0.7 collective-permute-start.8
  58.3 1.3 constant_dynamic-update-slice_fusion.1
  59.7 1.4 collective-permute-start.12
  61.1 3.6 %collective-permute-start.10 = (bf16[4,128,512]{2,1,0:T(8,128)(2,1)S(1)}, bf16[4,128,512]{2,1,0:T(8,128)(2,1)S(1)}, u32[]{:S(2)}, u32[]{:S(2)}) collective-permute-start(bf16[4,128,512]{2,1,0:T(8,128)(2,1)S(1)} %pad_maximum_fusion.2.refs_4_), channel_id=1, source_target_pairs={{1,0},{2,1},{3,2},{0,3},{5,4},{6,5},{7,6},{4,7},{9,8},{10,9},{11,1... | collective-permute-start | bytes 1572872 | tf_op jit(solution)/shard_map/ppermute | solution.py:242
  64.7 0.3 add_convert_fusion.2
  65.0 1.3 constant_dynamic-update-slice_fusion.3
  66.4 14.8 %collective-permute-done.8 = bf16[256,2048]{1,0:T(8,128)(2,1)S(1)} collective-permute-done((bf16[256,2048]{1,0:T(8,128)(2,1)S(1)}, bf16[256,2048]{1,0:T(8,128)(2,1)S(1)}, u32[]{:S(2)}, u32[]{:S(2)}) %collective-permute-start.8) | collective-permute-done | bytes 1048608 | tf_op jit(solution)/shard_map/ppermute | solution.py:237
  81.2 0.7 collective-permute-start.17
  82.0 1.5 collective-permute-start.16
  83.5 1.4 collective-permute-start.15
  84.9 1.2 collective-permute-done.11.refs_7_
  86.1 0.8 collective-permute-start.14
  86.9 1.3 constant_dynamic-update-slice_fusion.5
  88.2 2.3 %collective-permute-done.17 = bf16[2,128,512]{2,1,0:T(8,128)(2,1)S(1)} collective-permute-done((bf16[2,128,512]{2,1,0:T(8,128)(2,1)S(1)}, bf16[2,128,512]{2,1,0:T(8,128)(2,1)S(1)}, u32[]{:S(2)}, u32[]{:S(2)}) %collective-permute-start.17) | collective-permute-done | bytes 262176 | tf_op jit(solution)/shard_map/ppermute | solution.py:237
  90.5 0.6 collective-permute-start.20
  91.2 4.4 %collective-permute-done.16 = bf16[256,512]{1,0:T(8,128)(2,1)S(1)} collective-permute-done((bf16[256,512]{1,0:T(8,128)(2,1)S(1)}, bf16[256,512]{1,0:T(8,128)(2,1)S(1)}, u32[]{:S(2)}, u32[]{:S(2)}) %collective-permute-start.16) | collective-permute-done | bytes 262176 | tf_op jit(solution)/shard_map/ppermute | solution.py:237
  95.6 3.7 %collective-permute-start.18 = (bf16[4,128,512]{2,1,0:T(8,128)(2,1)S(1)}, bf16[4,128,512]{2,1,0:T(8,128)(2,1)S(1)}, u32[]{:S(2)}, u32[]{:S(2)}) collective-permute-start(bf16[4,128,512]{2,1,0:T(8,128)(2,1)S(1)} %pad_maximum_fusion.3.refs_4_), channel_id=1, source_target_pairs={{1,0},{2,1},{3,2},{0,3},{5,4},{6,5},{7,6},{4,7},{9,8},{10,9},{11,1... | collective-permute-start | bytes 1572872 | tf_op jit(solution)/shard_map/ppermute | solution.py:242
  99.3 11.1 %collective-permute-done.15 = bf16[256,512]{1,0:T(8,128)(2,1)S(1)} collective-permute-done((bf16[256,512]{1,0:T(8,128)(2,1)S(1)}, bf16[256,512]{1,0:T(8,128)(2,1)S(1)}, u32[]{:S(2)}, u32[]{:S(2)}) %collective-permute-start.15) | collective-permute-done | bytes 262176 | tf_op jit(solution)/shard_map/ppermute | solution.py:237
  110.4 1.6 collective-permute-start.19
  112.4 10.2 %collective-permute-done.19.refs_7_ = bf16[4,128,512]{2,1,0:T(8,128)(2,1)S(1)} collective-permute-done((bf16[4,128,512]{2,1,0:T(8,128)(2,1)S(1)}, bf16[4,128,512]{2,1,0:T(8,128)(2,1)S(1)}, u32[]{:S(2)}, u32[]{:S(2)}) %collective-permute-start.19) | collective-permute-done | bytes 524320 | tf_op jit(solution)/shard_map/ppermute | solution.py:242
  122.6 0.8 collective-permute-start.26
  123.5 3.1 %collective-permute-start.25 = (bf16[2,128,512]{2,1,0:T(8,128)(2,1)S(1)}, bf16[2,128,512]{2,1,0:T(8,128)(2,1)S(1)}, u32[]{:S(2)}, u32[]{:S(2)}) collective-permute-start(bf16[2,128,512]{2,1,0:T(8,128)(2,1)S(1)} %slice.60), channel_id=1, source_target_pairs={{1,0},{2,1},{3,2},{0,3},{5,4},{6,5},{7,6},{4,7},{9,8},{10,9},{11,1... | collective-permute-start | bytes 786440 | tf_op jit(solution)/shard_map/ppermute | solution.py:242
  126.7 4.3 %collective-permute-done.20 = bf16[256,2048]{1,0:T(8,128)(2,1)S(1)} collective-permute-done((bf16[256,2048]{1,0:T(8,128)(2,1)S(1)}, bf16[256,2048]{1,0:T(8,128)(2,1)S(1)}, u32[]{:S(2)}, u32[]{:S(2)}) %collective-permute-start.20) | collective-permute-done | bytes 1048608 | tf_op jit(solution)/shard_map/ppermute | solution.py:237
  131.1 2.6 %collective-permute-done.25 = bf16[2,128,512]{2,1,0:T(8,128)(2,1)S(1)} collective-permute-done((bf16[2,128,512]{2,1,0:T(8,128)(2,1)S(1)}, bf16[2,128,512]{2,1,0:T(8,128)(2,1)S(1)}, u32[]{:S(2)}, u32[]{:S(2)}) %collective-permute-start.25) | collective-permute-done | bytes 262176 | tf_op jit(solution)/shard_map/ppermute | solution.py:242
  133.7 6.5 %project.3 = (bf16[2,128,2048]{2,1,0:T(8,128)(2,1)S(1)}, bf16[2,128,2048]{2,1,0:T(8,128)(2,1)S(1)}) custom-call(s32[4]{0:T(128)S(1)} %fusion.9.slot_ref, bf16[512,2048]{1,0:T(8,128)(2,1)S(1)} %constant_dynamic-update-slice_fusion.refs_0_, bf16[512,2048]{1,0:T(8,128)(2,1)S(1)} %constant_dynamic-update-slice_fusion.2.refs_1_, ...), custom_call_target="tpu_custom_call" | custom-call | flops 4294967296 | bytes 10485760 | tf_op jit(solution)/shard_map/project/pallas_call | solution.py:196
  140.3 0.7 collective-permute-start.22
  141.0 3.2 %collective-permute-start.21 = (bf16[2,128,512]{2,1,0:T(8,128)(2,1)S(1)}, bf16[2,128,512]{2,1,0:T(8,128)(2,1)S(1)}, u32[]{:S(2)}, u32[]{:S(2)}) collective-permute-start(bf16[2,128,512]{2,1,0:T(8,128)(2,1)S(1)} %slice.56), channel_id=1, source_target_pairs={{1,0},{2,1},{3,2},{0,3},{5,4},{6,5},{7,6},{4,7},{9,8},{10,9},{11,1... | collective-permute-start | bytes 786440 | tf_op jit(solution)/shard_map/ppermute | solution.py:242
  144.2 7.1 %collective-permute-done.22 = bf16[2,128,512]{2,1,0:T(8,128)(2,1)S(1)} collective-permute-done((bf16[2,128,512]{2,1,0:T(8,128)(2,1)S(1)}, bf16[2,128,512]{2,1,0:T(8,128)(2,1)S(1)}, u32[]{:S(2)}, u32[]{:S(2)}) %collective-permute-start.22) | collective-permute-done | bytes 262176 | tf_op jit(solution)/shard_map/ppermute | solution.py:242
  151.3 3.7 %collective-permute-done.21 = bf16[2,128,512]{2,1,0:T(8,128)(2,1)S(1)} collective-permute-done((bf16[2,128,512]{2,1,0:T(8,128)(2,1)S(1)}, bf16[2,128,512]{2,1,0:T(8,128)(2,1)S(1)}, u32[]{:S(2)}, u32[]{:S(2)}) %collective-permute-start.21) | collective-permute-done | bytes 262176 | tf_op jit(solution)/shard_map/ppermute | solution.py:242
  155.1 6.5 %project.2 = (bf16[2,128,2048]{2,1,0:T(8,128)(2,1)S(1)}, bf16[2,128,2048]{2,1,0:T(8,128)(2,1)S(1)}) custom-call(s32[4]{0:T(128)S(1)} %fusion.9.slot_ref, bf16[512,2048]{1,0:T(8,128)(2,1)S(1)} %constant_dynamic-update-slice_fusion.refs_0_, bf16[512,2048]{1,0:T(8,128)(2,1)S(1)} %constant_dynamic-update-slice_fusion.2.refs_1_, ...), custom_call_target="tpu_custom_call" | custom-call | flops 4294967296 | bytes 10485760 | tf_op jit(solution)/shard_map/project/pallas_call | solution.py:196
  161.7 2.1 %collective-permute-start.29 = (bf16[256,512]{1,0:T(8,128)(2,1)S(1)}, bf16[256,512]{1,0:T(8,128)(2,1)S(1)}, u32[]{:S(2)}, u32[]{:S(2)}) collective-permute-start(bf16[256,512]{1,0:T(8,128)(2,1)S(1)} %fusion.8.refs_0_), channel_id=1, source_target_pairs={{1,0},{2,1},{3,2},{0,3},{5,4},{6,5},{7,6},{4,7},{9,8},{10,9},{11,1... | collective-permute-start | bytes 786440 | tf_op jit(solution)/shard_map/ppermute | solution.py:242
  163.8 0.4 collective-permute-start.30
  164.2 1.6 collective-permute-start.31
  165.9 0.4 add_convert_fusion
  166.3 0.8 slice_bitcast_fusion
  167.1 1.4 collective-permute-start.28
  168.5 0.4 add_convert_fusion.1
  168.9 0.8 slice_bitcast_fusion.2
  169.7 0.7 collective-permute-start.24
  170.5 17.2 %collective-permute-done.30.refs_2_ = bf16[256,512]{1,0:T(8,128)(2,1)S(1)} collective-permute-done((bf16[256,512]{1,0:T(8,128)(2,1)S(1)}, bf16[256,512]{1,0:T(8,128)(2,1)S(1)}, u32[]{:S(2)}, u32[]{:S(2)}) %collective-permute-start.30) | collective-permute-done | bytes 262176 | tf_op jit(solution)/shard_map/ppermute | solution.py:242
  187.7 0.7 copy-done.8
  188.4 0.7 copy-done.9
  189.1 2.3 %by_column.1 = (bf16[256,1024]{1,0:T(8,128)(2,1)}, bf16[256,1024]{1,0:T(8,128)(2,1)}) custom-call(s32[1]{0:T(128)} %bitcast.26.col_ref, bf16[256,512]{1,0:T(8,128)(2,1)} %copy-done.6, bf16[256,512]{1,0:T(8,128)(2,1)} %copy-done.7, bf16[256,512]{1,0:T(8,128)(2,1)} %copy-done.8, bf16[256,512]{1,0:T(8,128)(2,1)} %copy-done.9), custom_call_target="tpu_custom_call" | custom-call | tf_op jit(solution)/shard_map/by_column/pallas_call | solution.py:226
  191.6 0.4 collective-permute-done.24
  192.1 1.1 pad_maximum_fusion.1
  (63 shorter events, 2.2 us)
Async XLA Ops:
  0.6 17.5 %copy-start = (s32[2048]{0:T(1024)S(1)}, s32[2048]{0:T(1024)}, u32[]{:S(2)}) copy-start(s32[2048]{0:T(1024)} %param.10) | copy-start | bytes 24580
  1.7 11.1 %collective-permute-start.2 = (bf16[256,512]{1,0:T(8,128)(2,1)S(1)}, bf16[256,512]{1,0:T(8,128)(2,1)S(1)}, u32[]{:S(2)}, u32[]{:S(2)}) collective-permute-start(bf16[256,512]{1,0:T(8,128)(2,1)S(1)} %get-tuple-element.85), channel_id=1, source_target_pairs={{0,24},{4,28},{8,16},{12,20},{16,8},{20,12},{24,0},{28,4},{1,25},{... | collective-permute-start | bytes 786440 | tf_op jit(solution)/shard_map/ppermute | solution.py:237
  5.6 11.9 %collective-permute-start.1 = (bf16[256,512]{1,0:T(8,128)(2,1)S(1)}, bf16[256,512]{1,0:T(8,128)(2,1)S(1)}, u32[]{:S(2)}, u32[]{:S(2)}) collective-permute-start(bf16[256,512]{1,0:T(8,128)(2,1)S(1)} %get-tuple-element.85), channel_id=1, source_target_pairs={{0,16},{4,20},{8,24},{12,28},{16,0},{20,4},{24,8},{28,12},{1,17},{... | collective-permute-start | bytes 786440 | tf_op jit(solution)/shard_map/ppermute | solution.py:237
  6.2 11.7 %collective-permute-start = (bf16[256,512]{1,0:T(8,128)(2,1)S(1)}, bf16[256,512]{1,0:T(8,128)(2,1)S(1)}, u32[]{:S(2)}, u32[]{:S(2)}) collective-permute-start(bf16[256,512]{1,0:T(8,128)(2,1)S(1)} %get-tuple-element.85), channel_id=1, source_target_pairs={{0,8},{4,12},{8,0},{12,4},{16,24},{20,28},{24,16},{28,20},{1,9},{5... | collective-permute-start | bytes 786440 | tf_op jit(solution)/shard_map/ppermute | solution.py:237
  18.0 4.8 %collective-permute-start.3 = (bf16[4,256,512]{2,1,0:T(8,128)(2,1)S(1)}, bf16[4,256,512]{2,1,0:T(8,128)(2,1)S(1)}, u32[]{:S(2)}, u32[]{:S(2)}) collective-permute-start(bf16[4,256,512]{2,1,0:T(8,128)(2,1)S(1)} %pad_maximum_fusion.kv_even), channel_id=1, source_target_pairs={{0,4},{4,0},{8,12},{12,8},{16,20},{20,16},{24,28},{28,24},{1,5},{5... | collective-permute-start | bytes 3145736 | tf_op jit(solution)/shard_map/ppermute | solution.py:237
  18.3 6.7 %copy-start.1 = (bf16[256,2048]{1,0:T(8,128)(2,1)S(1)}, bf16[256,2048]{1,0:T(8,128)(2,1)}, u32[]{:S(2)}) copy-start(bf16[256,2048]{1,0:T(8,128)(2,1)} %q_ref.1) | copy-start | bytes 3145732
  18.3 6.6 %copy-start.2 = (bf16[256,2048]{1,0:T(8,128)(2,1)S(1)}, bf16[256,2048]{1,0:T(8,128)(2,1)}, u32[]{:S(2)}) copy-start(bf16[256,2048]{1,0:T(8,128)(2,1)} %g_ref.1) | copy-start | bytes 3145732
  22.8 25.8 %collective-permute-start.5 = (bf16[256,2048]{1,0:T(8,128)(2,1)}, bf16[256,2048]{1,0:T(8,128)(2,1)}, u32[]{:S(2)}, u32[]{:S(2)}) collective-permute-start(bf16[256,2048]{1,0:T(8,128)(2,1)} %get-tuple-element.40), channel_id=1, source_target_pairs={{0,8},{4,12},{8,0},{12,4},{16,24},{20,28},{24,16},{28,20},{1,9},{5... | collective-permute-start | bytes 3145736 | tf_op jit(solution)/shard_map/ppermute | solution.py:237
  24.3 25.6 %collective-permute-start.6 = (bf16[256,2048]{1,0:T(8,128)(2,1)}, bf16[256,2048]{1,0:T(8,128)(2,1)}, u32[]{:S(2)}, u32[]{:S(2)}) collective-permute-start(bf16[256,2048]{1,0:T(8,128)(2,1)} %get-tuple-element.35), channel_id=1, source_target_pairs={{0,16},{4,20},{8,24},{12,28},{16,0},{20,4},{24,8},{28,12},{1,17},{... | collective-permute-start | bytes 3145736 | tf_op jit(solution)/shard_map/ppermute | solution.py:237
  40.8 1.0 copy-start.3
  40.8 9.7 %copy-start.4 = (bf16[256,2048]{1,0:T(8,128)(2,1)S(1)}, bf16[256,2048]{1,0:T(8,128)(2,1)}, u32[]{:S(2)}) copy-start(bf16[256,2048]{1,0:T(8,128)(2,1)} %get-tuple-element.36) | copy-start | bytes 3145732
  41.8 2.7 %collective-permute-start.4 = (bf16[2,256,512]{2,1,0:T(8,128)(2,1)S(1)}, bf16[2,256,512]{2,1,0:T(8,128)(2,1)}, u32[]{:S(2)}, u32[]{:S(2)}) collective-permute-start(bf16[2,256,512]{2,1,0:T(8,128)(2,1)S(1)} %get-tuple-element.76), channel_id=1, source_target_pairs={{0,4},{4,0},{8,12},{12,8},{16,20},{20,16},{24,28},{28,24},{1,5},{5... | collective-permute-start | bytes 1572872 | tf_op jit(solution)/shard_map/ppermute | solution.py:237
  41.8 22.9 %collective-permute-start.13 = (bf16[4,256,512]{2,1,0:T(8,128)(2,1)}, bf16[4,256,512]{2,1,0:T(8,128)(2,1)S(1)}, u32[]{:S(2)}, u32[]{:S(2)}) collective-permute-start(bf16[4,256,512]{2,1,0:T(8,128)(2,1)} %copy-done.3), channel_id=1, source_target_pairs={{0,4},{4,0},{8,12},{12,8},{16,20},{20,16},{24,28},{28,24},{1,5},{5... | collective-permute-start | bytes 3145736 | tf_op jit(solution)/shard_map/ppermute | solution.py:237
  44.6 13.0 %copy-start.5 = (bf16[256,2048]{1,0:T(8,128)(2,1)S(1)}, bf16[256,2048]{1,0:T(8,128)(2,1)}, u32[]{:S(2)}) copy-start(bf16[256,2048]{1,0:T(8,128)(2,1)} %get-tuple-element.44) | copy-start | bytes 3145732
  49.9 7.6 %collective-permute-start.7 = (bf16[2,128,512]{2,1,0:T(8,128)(2,1)S(1)}, bf16[2,128,512]{2,1,0:T(8,128)(2,1)S(1)}, u32[]{:S(2)}, u32[]{:S(2)}) collective-permute-start(bf16[2,128,512]{2,1,0:T(8,128)(2,1)S(1)} %slice.49), channel_id=1, source_target_pairs={{0,8},{4,12},{8,0},{12,4},{16,24},{20,28},{24,16},{28,20},{1,9},{5... | collective-permute-start | bytes 786440 | tf_op jit(solution)/shard_map/ppermute | solution.py:237
  50.5 31.5 %collective-permute-start.9 = (bf16[256,2048]{1,0:T(8,128)(2,1)S(1)}, bf16[256,2048]{1,0:T(8,128)(2,1)S(1)}, u32[]{:S(2)}, u32[]{:S(2)}) collective-permute-start(bf16[256,2048]{1,0:T(8,128)(2,1)S(1)} %copy-done.4), channel_id=1, source_target_pairs={{0,16},{4,20},{8,24},{12,28},{16,0},{20,4},{24,8},{28,12},{1,17},{... | collective-permute-start | bytes 3145736 | tf_op jit(solution)/shard_map/ppermute | solution.py:237
  57.6 23.6 %collective-permute-start.8 = (bf16[256,2048]{1,0:T(8,128)(2,1)S(1)}, bf16[256,2048]{1,0:T(8,128)(2,1)S(1)}, u32[]{:S(2)}, u32[]{:S(2)}) collective-permute-start(bf16[256,2048]{1,0:T(8,128)(2,1)S(1)} %copy-done.5), channel_id=1, source_target_pairs={{0,8},{4,12},{8,0},{12,4},{16,24},{20,28},{24,16},{28,20},{1,9},{5... | collective-permute-start | bytes 3145736 | tf_op jit(solution)/shard_map/ppermute | solution.py:237
  59.7 52.7 %collective-permute-start.12 = (bf16[256,2048]{1,0:T(8,128)(2,1)}, bf16[256,2048]{1,0:T(8,128)(2,1)S(1)}, u32[]{:S(2)}, u32[]{:S(2)}) collective-permute-start(bf16[256,2048]{1,0:T(8,128)(2,1)} %collective-permute-done.5), channel_id=1, source_target_pairs={{0,16},{4,20},{8,24},{12,28},{16,0},{20,4},{24,8},{28,12},{1,17},{... | collective-permute-start | bytes 3145736 | tf_op jit(solution)/shard_map/ppermute | solution.py:237
  61.1 22.4 %collective-permute-start.10 = (bf16[4,128,512]{2,1,0:T(8,128)(2,1)S(1)}, bf16[4,128,512]{2,1,0:T(8,128)(2,1)S(1)}, u32[]{:S(2)}, u32[]{:S(2)}) collective-permute-start(bf16[4,128,512]{2,1,0:T(8,128)(2,1)S(1)} %pad_maximum_fusion.2.refs_4_), channel_id=1, source_target_pairs={{1,0},{2,1},{3,2},{0,3},{5,4},{6,5},{7,6},{4,7},{9,8},{10,9},{11,1... | collective-permute-start | bytes 1572872 | tf_op jit(solution)/shard_map/ppermute | solution.py:242
  64.7 21.4 %collective-permute-start.11 = (bf16[4,128,512]{2,1,0:T(8,128)(2,1)S(1)}, bf16[4,128,512]{2,1,0:T(8,128)(2,1)S(1)}, u32[]{:S(2)}, u32[]{:S(2)}) collective-permute-start(bf16[4,128,512]{2,1,0:T(8,128)(2,1)S(1)} %pad_maximum_fusion.2.refs_4_), channel_id=1, source_target_pairs={{3,0},{0,1},{1,2},{2,3},{7,4},{4,5},{5,6},{6,7},{11,8},{8,9},{9,10... | collective-permute-start | bytes 1572872 | tf_op jit(solution)/shard_map/ppermute | solution.py:242
  81.2 9.3 %collective-permute-start.17 = (bf16[2,128,512]{2,1,0:T(8,128)(2,1)S(1)}, bf16[2,128,512]{2,1,0:T(8,128)(2,1)S(1)}, u32[]{:S(2)}, u32[]{:S(2)}) collective-permute-start(bf16[2,128,512]{2,1,0:T(8,128)(2,1)S(1)} %slice.55), channel_id=1, source_target_pairs={{0,8},{4,12},{8,0},{12,4},{16,24},{20,28},{24,16},{28,20},{1,9},{5... | collective-permute-start | bytes 786440 | tf_op jit(solution)/shard_map/ppermute | solution.py:237
  82.0 13.6 %collective-permute-start.16 = (bf16[256,512]{1,0:T(8,128)(2,1)S(1)}, bf16[256,512]{1,0:T(8,128)(2,1)S(1)}, u32[]{:S(2)}, u32[]{:S(2)}) collective-permute-start(bf16[256,512]{1,0:T(8,128)(2,1)S(1)} %get-tuple-element.72), channel_id=1, source_target_pairs={{0,24},{4,28},{8,16},{12,20},{16,8},{20,12},{24,0},{28,4},{1,25},{... | collective-permute-start | bytes 786440 | tf_op jit(solution)/shard_map/ppermute | solution.py:237
  83.5 26.9 %collective-permute-start.15 = (bf16[256,512]{1,0:T(8,128)(2,1)S(1)}, bf16[256,512]{1,0:T(8,128)(2,1)S(1)}, u32[]{:S(2)}, u32[]{:S(2)}) collective-permute-start(bf16[256,512]{1,0:T(8,128)(2,1)S(1)} %get-tuple-element.73), channel_id=1, source_target_pairs={{0,16},{4,20},{8,24},{12,28},{16,0},{20,4},{24,8},{28,12},{1,17},{... | collective-permute-start | bytes 786440 | tf_op jit(solution)/shard_map/ppermute | solution.py:237
  86.1 25.9 %collective-permute-start.14 = (bf16[256,512]{1,0:T(8,128)(2,1)S(1)}, bf16[256,512]{1,0:T(8,128)(2,1)S(1)}, u32[]{:S(2)}, u32[]{:S(2)}) collective-permute-start(bf16[256,512]{1,0:T(8,128)(2,1)S(1)} %get-tuple-element.71), channel_id=1, source_target_pairs={{0,8},{4,12},{8,0},{12,4},{16,24},{20,28},{24,16},{28,20},{1,9},{5... | collective-permute-start | bytes 786440 | tf_op jit(solution)/shard_map/ppermute | solution.py:237
  90.5 40.5 %collective-permute-start.20 = (bf16[256,2048]{1,0:T(8,128)(2,1)S(1)}, bf16[256,2048]{1,0:T(8,128)(2,1)S(1)}, u32[]{:S(2)}, u32[]{:S(2)}) collective-permute-start(bf16[256,2048]{1,0:T(8,128)(2,1)S(1)} %collective-permute-done.8), channel_id=1, source_target_pairs={{0,16},{4,20},{8,24},{12,28},{16,0},{20,4},{24,8},{28,12},{1,17},{... | collective-permute-start | bytes 3145736 | tf_op jit(solution)/shard_map/ppermute | solution.py:237
  95.6 16.8 %collective-permute-start.18 = (bf16[4,128,512]{2,1,0:T(8,128)(2,1)S(1)}, bf16[4,128,512]{2,1,0:T(8,128)(2,1)S(1)}, u32[]{:S(2)}, u32[]{:S(2)}) collective-permute-start(bf16[4,128,512]{2,1,0:T(8,128)(2,1)S(1)} %pad_maximum_fusion.3.refs_4_), channel_id=1, source_target_pairs={{1,0},{2,1},{3,2},{0,3},{5,4},{6,5},{7,6},{4,7},{9,8},{10,9},{11,1... | collective-permute-start | bytes 1572872 | tf_op jit(solution)/shard_map/ppermute | solution.py:242
  110.4 12.2 %collective-permute-start.19 = (bf16[4,128,512]{2,1,0:T(8,128)(2,1)S(1)}, bf16[4,128,512]{2,1,0:T(8,128)(2,1)S(1)}, u32[]{:S(2)}, u32[]{:S(2)}) collective-permute-start(bf16[4,128,512]{2,1,0:T(8,128)(2,1)S(1)} %pad_maximum_fusion.3.refs_4_), channel_id=1, source_target_pairs={{3,0},{0,1},{1,2},{2,3},{7,4},{4,5},{5,6},{6,7},{11,8},{8,9},{9,10... | collective-permute-start | bytes 1572872 | tf_op jit(solution)/shard_map/ppermute | solution.py:242
  112.1 52.1 %copy-start.6 = (bf16[256,512]{1,0:T(8,128)(2,1)}, bf16[256,512]{1,0:T(8,128)(2,1)S(1)}, u32[]{:S(2)}) copy-start(bf16[256,512]{1,0:T(8,128)(2,1)S(1)} %fusion.8.refs_0_) | copy-start | bytes 786436
  122.6 8.5 %collective-permute-start.26 = (bf16[2,128,512]{2,1,0:T(8,128)(2,1)S(1)}, bf16[2,128,512]{2,1,0:T(8,128)(2,1)S(1)}, u32[]{:S(2)}, u32[]{:S(2)}) collective-permute-start(bf16[2,128,512]{2,1,0:T(8,128)(2,1)S(1)} %slice.61), channel_id=1, source_target_pairs={{3,0},{0,1},{1,2},{2,3},{7,4},{4,5},{5,6},{6,7},{11,8},{8,9},{9,10... | collective-permute-start | bytes 786440 | tf_op jit(solution)/shard_map/ppermute | solution.py:242
  123.5 10.2 %collective-permute-start.25 = (bf16[2,128,512]{2,1,0:T(8,128)(2,1)S(1)}, bf16[2,128,512]{2,1,0:T(8,128)(2,1)S(1)}, u32[]{:S(2)}, u32[]{:S(2)}) collective-permute-start(bf16[2,128,512]{2,1,0:T(8,128)(2,1)S(1)} %slice.60), channel_id=1, source_target_pairs={{1,0},{2,1},{3,2},{0,3},{5,4},{6,5},{7,6},{4,7},{9,8},{10,9},{11,1... | collective-permute-start | bytes 786440 | tf_op jit(solution)/shard_map/ppermute | solution.py:242
  140.2 25.6 %collective-permute-start.27 = (bf16[2,128,2048]{2,1,0:T(8,128)(2,1)S(1)}, bf16[2,128,2048]{2,1,0:T(8,128)(2,1)S(1)}, u32[]{:S(2)}, u32[]{:S(2)}) collective-permute-start(bf16[2,128,2048]{2,1,0:T(8,128)(2,1)S(1)} %get-tuple-element.63), channel_id=1, source_target_pairs={{0,4},{4,0},{8,12},{12,8},{16,20},{20,16},{24,28},{28,24},{1,5},{5... | collective-permute-start | bytes 3145736 | tf_op jit(solution)/shard_map/ppermute | solution.py:237
  140.3 11.0 %collective-permute-start.22 = (bf16[2,128,512]{2,1,0:T(8,128)(2,1)S(1)}, bf16[2,128,512]{2,1,0:T(8,128)(2,1)S(1)}, u32[]{:S(2)}, u32[]{:S(2)}) collective-permute-start(bf16[2,128,512]{2,1,0:T(8,128)(2,1)S(1)} %slice.57), channel_id=1, source_target_pairs={{3,0},{0,1},{1,2},{2,3},{7,4},{4,5},{5,6},{6,7},{11,8},{8,9},{9,10... | collective-permute-start | bytes 786440 | tf_op jit(solution)/shard_map/ppermute | solution.py:242
  141.0 14.0 %collective-permute-start.21 = (bf16[2,128,512]{2,1,0:T(8,128)(2,1)S(1)}, bf16[2,128,512]{2,1,0:T(8,128)(2,1)S(1)}, u32[]{:S(2)}, u32[]{:S(2)}) collective-permute-start(bf16[2,128,512]{2,1,0:T(8,128)(2,1)S(1)} %slice.56), channel_id=1, source_target_pairs={{1,0},{2,1},{3,2},{0,3},{5,4},{6,5},{7,6},{4,7},{9,8},{10,9},{11,1... | collective-permute-start | bytes 786440 | tf_op jit(solution)/shard_map/ppermute | solution.py:242
  161.6 6.8 %collective-permute-start.23 = (bf16[2,128,2048]{2,1,0:T(8,128)(2,1)S(1)}, bf16[2,128,2048]{2,1,0:T(8,128)(2,1)S(1)}, u32[]{:S(2)}, u32[]{:S(2)}) collective-permute-start(bf16[2,128,2048]{2,1,0:T(8,128)(2,1)S(1)} %get-tuple-element.59), channel_id=1, source_target_pairs={{0,4},{4,0},{8,12},{12,8},{16,20},{20,16},{24,28},{28,24},{1,5},{5... | collective-permute-start | bytes 3145736 | tf_op jit(solution)/shard_map/ppermute | solution.py:237
  161.7 8.8 %collective-permute-start.29 = (bf16[256,512]{1,0:T(8,128)(2,1)S(1)}, bf16[256,512]{1,0:T(8,128)(2,1)S(1)}, u32[]{:S(2)}, u32[]{:S(2)}) collective-permute-start(bf16[256,512]{1,0:T(8,128)(2,1)S(1)} %fusion.8.refs_0_), channel_id=1, source_target_pairs={{1,0},{2,1},{3,2},{0,3},{5,4},{6,5},{7,6},{4,7},{9,8},{10,9},{11,1... | collective-permute-start | bytes 786440 | tf_op jit(solution)/shard_map/ppermute | solution.py:242
  163.8 23.9 %collective-permute-start.30 = (bf16[256,512]{1,0:T(8,128)(2,1)S(1)}, bf16[256,512]{1,0:T(8,128)(2,1)S(1)}, u32[]{:S(2)}, u32[]{:S(2)}) collective-permute-start(bf16[256,512]{1,0:T(8,128)(2,1)S(1)} %fusion.8.refs_0_), channel_id=1, source_target_pairs={{2,0},{3,1},{0,2},{1,3},{6,4},{7,5},{4,6},{5,7},{10,8},{11,9},{8,1... | collective-permute-start | bytes 786440 | tf_op jit(solution)/shard_map/ppermute | solution.py:242
  164.2 23.5 %collective-permute-start.31 = (bf16[256,512]{1,0:T(8,128)(2,1)S(1)}, bf16[256,512]{1,0:T(8,128)(2,1)S(1)}, u32[]{:S(2)}, u32[]{:S(2)}) collective-permute-start(bf16[256,512]{1,0:T(8,128)(2,1)S(1)} %fusion.8.refs_0_), channel_id=1, source_target_pairs={{3,0},{0,1},{1,2},{2,3},{7,4},{4,5},{5,6},{6,7},{11,8},{8,9},{9,10... | collective-permute-start | bytes 786440 | tf_op jit(solution)/shard_map/ppermute | solution.py:242
  167.1 24.3 %collective-permute-start.28 = (bf16[128,2048]{1,0:T(8,128)(2,1)}, bf16[128,2048]{1,0:T(8,128)(2,1)S(1)}, u32[]{:S(2)}, u32[]{:S(2)}) collective-permute-start(bf16[128,2048]{1,0:T(8,128)(2,1)} %slice_bitcast_fusion), channel_id=1, source_target_pairs={{0,8},{4,12},{8,0},{12,4},{16,24},{20,28},{24,16},{28,20},{1,9},{5... | collective-permute-start | bytes 1572872 | tf_op jit(solution)/shard_map/ppermute | solution.py:237
  169.7 22.3 %collective-permute-start.24 = (bf16[128,2048]{1,0:T(8,128)(2,1)}, bf16[128,2048]{1,0:T(8,128)(2,1)S(1)}, u32[]{:S(2)}, u32[]{:S(2)}) collective-permute-start(bf16[128,2048]{1,0:T(8,128)(2,1)} %slice_bitcast_fusion.2), channel_id=1, source_target_pairs={{0,8},{4,12},{8,0},{12,4},{16,24},{20,28},{24,16},{28,20},{1,9},{5... | collective-permute-start | bytes 1572872 | tf_op jit(solution)/shard_map/ppermute | solution.py:237
  170.5 17.2 %copy-start.7 = (bf16[256,512]{1,0:T(8,128)(2,1)}, bf16[256,512]{1,0:T(8,128)(2,1)S(1)}, u32[]{:S(2)}) copy-start(bf16[256,512]{1,0:T(8,128)(2,1)S(1)} %collective-permute-done.29.refs_1_) | copy-start | bytes 786436
  187.7 0.7 copy-start.8
  188.4 0.7 copy-start.9

commit v3 on v2

--- a/solution.py
+++ b/solution.py
@@ -70,31 +70,27 @@
                 )
                 s = s * scale + bias
                 s_all[j, at, :] = s
-                top[at, :] = jnp.maximum(top[at, :], jnp.maximum(s[:, :half], s[:, half:]))
-                d_all[j, at, :] = lax.dot_general(
+                d = lax.dot_general(
                     g_rows[at, :], vals, contract_last, preferred_element_type=jnp.float32
                 )
+                d_all[j, at, :] = d
+                old = top[at, :]
+                new = jnp.maximum(old, jnp.maximum(s[:, :half], s[:, half:]))
+                factor = jnp.exp2(old - new)
+                one = jnp.exp2(s[:, :half] - new)
+                two = jnp.exp2(s[:, half:] - new)
+                top[at, :] = new
+                total[at, :] = total[at, :] * factor + (one + two)
+                dots[at, :] = dots[at, :] * factor + (one * d[:, :half] + two * d[:, half:])
             return carry
 
         lax.fori_loop(0, steps, scores, 0)
-        top[...] = jnp.broadcast_to(jnp.max(top[...], axis=1, keepdims=True), top.shape)
-
-        def sums(j, carry):
-            for p in range(per_kv):
-                at = slice(p * half, (p + 1) * half)
-                high = top[at, :]
-                s = s_all[j, at, :]
-                e = jnp.exp2(s - jnp.concatenate([high, high], axis=1))
-                s_all[j, at, :] = e
-                total[at, :] += e[:, :half] + e[:, half:]
-                ed = e * d_all[j, at, :]
-                dots[at, :] += ed[:, :half] + ed[:, half:]
-            return carry
-
-        lax.fori_loop(0, steps, sums, 0)
-        inverse = 1.0 / jnp.sum(total[...], axis=1, keepdims=True)
-        delta = jnp.sum(dots[...], axis=1, keepdims=True) * inverse
-        total[...] = jnp.broadcast_to(inverse, total.shape)
+        lanes = top[...]
+        high = jnp.max(lanes, axis=1, keepdims=True)
+        factor = jnp.exp2(lanes - high)
+        sums = jnp.sum(total[...] * factor, axis=1, keepdims=True)
+        delta = jnp.sum(dots[...] * factor, axis=1, keepdims=True) / sums
+        total[...] = jnp.broadcast_to(high + jnp.log2(sums), total.shape)
         dots[...] = jnp.broadcast_to(delta, dots.shape)
         top[...] = jnp.zeros_like(top)
 
@@ -102,9 +98,9 @@
             keys = pair(j, 0)
             for p in range(per_kv):
                 at = slice(p * half, (p + 1) * half)
-                inv = total[at, :]
+                lse = total[at, :]
                 dot = dots[at, :]
-                prob = s_all[j, at, :] * jnp.concatenate([inv, inv], axis=1)
+                prob = jnp.exp2(s_all[j, at, :] - jnp.concatenate([lse, lse], axis=1))
                 p_low[at, :] = prob.astype(jnp.bfloat16)
                 shifted = d_all[j, at, :] - jnp.concatenate([dot, dot], axis=1)
                 d_low[at, :] = (prob * shifted).astype(jnp.bfloat16)
@@ -158,47 +154,52 @@
         ],
         compiler_params=pltpu.CompilerParams(vmem_limit_bytes=32 << 20),
         cost_estimate=pl.CostEstimate(
-            flops=14_000_000_000, bytes_accessed=8_000_000, transcendentals=3_000_000
+            flops=3_400_000_000, bytes_accessed=8_000_000, transcendentals=2_600_000
         ),
         name="attention",
     )(me, seg_query, seg_key, queries, grad_attn, kv_even, kv_odd)
 
 
-def project_kernel(slot_ref, *refs):
-    even_ref, odd_ref, lhs = refs[-3:]
-    count = lhs.shape[0]
-    weights, parts = refs[:count], refs[count:-3]
-    blocks, step, features = even_ref.shape
+def project_kernel(pieces_here, places, slot_ref, *refs):
+    group = len(places[0])
+    count = len(places)
+    outs, lhs = refs[-1 - group:-1], refs[-1]
+    pieces, sources = refs[:pieces_here], refs[pieces_here:-1 - group]
+    step, features = outs[0].shape
+    depth = sources[0].shape[1]
     for k in range(count):
-        lhs[slot_ref[k]] = parts[k][...].reshape(lhs.shape[1:])
+        at = pl.ds(pl.multiple_of(slot_ref[k] * depth, depth), depth)
+        for i in range(group):
+            source, first = places[k][i]
+            lhs[i * step:(i + 1) * step, at] = sources[source][first:first + step, :]
     tile = min(256, features)
 
     def columns(n, carry):
         at = pl.ds(pl.multiple_of(n * tile, tile), tile)
-        out = jnp.dot(lhs[0], weights[0][:, at], preferred_element_type=jnp.float32)
-        for k in range(1, count):
-            out += jnp.dot(lhs[k], weights[k][:, at], preferred_element_type=jnp.float32)
-        out = out.astype(jnp.bfloat16).reshape(2 * blocks, step, tile)
-        for i in range(blocks):
-            even_ref[i, :, at] = out[2 * i]
-            odd_ref[i, :, at] = out[2 * i + 1]
+        weight = jnp.concatenate([piece[:, at] for piece in pieces], axis=0)
+        for i in range(group):
+            rows = slice(i * step, (i + 1) * step)
+            out = jnp.dot(lhs[rows, :], weight, preferred_element_type=jnp.float32)
+            outs[i][:, at] = out.astype(jnp.bfloat16)
         return carry
 
     lax.fori_loop(0, features // tile, columns, 0)
 
 
-def project(slots, weights, parts):
+def project(slots, weights, sources, places, step):
     count = len(weights)
-    group, step, depth = parts[0].shape
-    features = weights[0].shape[1]
+    group = len(places[0])
+    depth = sources[0].shape[1]
+    pieces = [piece for weight in weights for piece in weight]
+    features = pieces[0].shape[1]
     smem = pl.BlockSpec(memory_space=pltpu.SMEM)
     vmem = pl.BlockSpec(memory_space=pltpu.VMEM)
     return pl.pallas_call(
-        project_kernel,
-        out_shape=[jax.ShapeDtypeStruct((group // 2, step, features), jnp.bfloat16)] * 2,
-        in_specs=[smem] + [vmem] * (count + len(parts)),
-        out_specs=[vmem, vmem],
-        scratch_shapes=[pltpu.VMEM((count, group * step, depth), jnp.bfloat16)],
+        functools.partial(project_kernel, len(pieces), places),
+        out_shape=[jax.ShapeDtypeStruct((step, features), jnp.bfloat16)] * group,
+        in_specs=[smem] + [vmem] * (len(pieces) + len(sources)),
+        out_specs=[vmem] * group,
+        scratch_shapes=[pltpu.VMEM((group * step, count * depth), jnp.bfloat16)],
         compiler_params=pltpu.CompilerParams(vmem_limit_bytes=32 << 20),
         cost_estimate=pl.CostEstimate(
             flops=2 * group * step * depth * count * features,
@@ -206,7 +207,7 @@
             transcendentals=0,
         ),
         name="project",
-    )(slots, *weights, *parts)
+    )(slots, *pieces, *sources)
 
 
 def columns_kernel(col_ref, *refs):
@@ -274,9 +275,20 @@
             mine.append(lax.dynamic_slice_in_dim(array, (kv_first + g) * HD, HD, 1))
     mine = jnp.concatenate(mine, axis=1)
     kv_even = jnp.stack([mine] + [across(mine, d) for d in range(2, ranks, 2)])
+    rows_w = q_weight.shape[0]
+    special = ranks == 8 and count == 4
+    if special:
+        side = (me >> 1) & 1
+        wide = rows_w // 2
+        pieces = []
+        for start, size in (
+            (side * wide, wide // 2), (side * wide + wide // 2, wide // 2),
+            ((1 - side) * wide, wide // 2), ((1 - side) * wide + wide // 2, wide // 2),
+        ):
+            pieces.append(lax.dynamic_slice_in_dim(q_weight, start, size, 0))
+        kv_even, *pieces = tied(kv_even, *pieces)
     kv_odd = across(kv_even, 1)
 
-    rows_w = q_weight.shape[0]
     key_segs = segment_ids.reshape(2 * ranks, 1, half)
     own = segment_ids.reshape(2 * ranks, half)
     query_segs = jnp.stack(
@@ -285,20 +297,11 @@
             lax.dynamic_index_in_dim(own, 2 * ranks - 1 - me, 0, keepdims=False),
         ]
     )[:, :, None]
-    special = ranks == 8 and count == 4
-    if special:
-        cut = q_weight.reshape(4, rows_w // 4, -1)
-        side = (me >> 1) & 1
-        quarters = [
-            lax.dynamic_index_in_dim(cut, 2 * at + i, 0, keepdims=False)
-            for at in (side, 1 - side) for i in range(2)
-        ]
-        kv_even, kv_odd, *quarters = tied(kv_even, kv_odd, *quarters)
     dq, dkv_even, dkv_odd = attention(
         me.reshape(1), query_segs, key_segs, queries, grad_attn, kv_even, kv_odd, kv_here, per_kv
     )
     if special:
-        input_grad, dkv_mine = paired(dq, dkv_even, dkv_odd, quarters, me, col)
+        input_grad, dkv_mine = paired(dq, dkv_even, dkv_odd, pieces, me, col)
     else:
         dq = dq.reshape(kv_here, 2, rows, -1).transpose(2, 0, 1, 3).reshape(rows, heads_here * HD)
         input_grad = jnp.dot(
@@ -310,9 +313,8 @@
 
     share = max(1, group // heads_here)
     if share == 1:
-        key_grad, value_grad = by_column(
-            col.reshape(1), [dkv_mine] + [turned(dkv_mine, k) for k in range(1, count)]
-        )
+        parts = dkv_mine if special else [dkv_mine] + [turned(dkv_mine, k) for k in range(1, count)]
+        key_grad, value_grad = by_column(col.reshape(1), parts)
         return (input_grad, key_grad, value_grad)
     whole = lax.all_gather(dkv_mine, "col")
     whole = whole.reshape(count // share, share, rows, -1).astype(jnp.float32)
@@ -329,15 +331,22 @@
     return total.astype(jnp.bfloat16)
 
 
-def paired(dq, dkv_even, dkv_odd, quarters, me, col):
+def paired(dq, dkv_even, dkv_odd, pieces, me, col):
     count = lax.axis_size("col")
     rows = dq.shape[2]
     core = me & 1
     side = (me >> 1) & 1
 
-    keep_one, keep_two, send_one, send_two = quarters
-    w_one = across(send_one, 2)
-    keep_one_y = across(keep_one, 4)
+    keep_w, (send_one, send_two) = pieces[:2], pieces[2:]
+
+    def x(block):
+        return across(block, 2)
+
+    def y(block):
+        return across(block, 4)
+
+    w_one = x(send_one)
+    keep_one_y = y(keep_w[0])
 
     mine = lax.dynamic_index_in_dim(dq, core, 0, keepdims=False)
     theirs = across(lax.dynamic_index_in_dim(dq, 1 - core, 0, keepdims=False), 1)
@@ -345,40 +354,41 @@
     keep = lax.dynamic_index_in_dim(both, side, 0, keepdims=False)
     send = lax.dynamic_index_in_dim(both, 1 - side, 0, keepdims=False)
     send, w_one, keep_one_y = tied(send, w_one, keep_one_y)
-    keep_two_y = across(keep_two, 4)
-    step = rows // 2
-    blocks = [jnp.concatenate([keep[:, :step], across(send[:, :step], 2)], axis=0)]
-    send_two, blocks[0] = tied(send_two, blocks[0])
-    near = [[turned(blocks[0], 1), turned(blocks[0], -1)]]
-    w_two = across(send_two, 2)
-    w_one_y = across(w_one, 4)
-    send, w_two = tied(send, w_two)
-    blocks.append(jnp.concatenate([keep[:, step:], across(send[:, step:], 2)], axis=0))
-    keep_two_y, *near[0] = tied(keep_two_y, *near[0])
-    far = [opposite(*near[0])]
-    blocks[1], *near[0] = tied(blocks[1], *near[0])
-    near.append([turned(blocks[1], 1), turned(blocks[1], -1)])
-    w_two_y = across(w_two, 4)
+    keep_two_y = y(keep_w[1])
+    tokens = jnp.concatenate([keep, x(send)], axis=0)
+    tokens = tokens.reshape(4 * rows, -1)
+    send_two, tokens = tied(send_two, tokens)
+    near = [turned(tokens, 1), turned(tokens, -1)]
+    w_two = x(send_two)
+    w_one_y = y(w_one)
     dkv_terms = added(dkv_even, across(dkv_odd, 1))
-    dkv_mine = chips_sum(dkv_terms)
-    w_one_y, dkv_mine, *near[1] = tied(w_one_y, dkv_mine, *near[1])
-    far.append(opposite(*near[1]))
-
-    def joined(*parts):
-        return jnp.concatenate(parts, axis=0)
-
-    weights = [
-        joined(keep_one, keep_two), joined(w_one, w_two),
-        joined(keep_one_y, keep_two_y), joined(w_one_y, w_two_y),
-    ]
+    dkv_terms, w_two = tied(dkv_terms, w_two)
+    dkv_x = x(dkv_terms[1::2])
+    w_two_y = y(w_two)
+    keep_two_y, w_one_y, dkv_x, near[0], near[1] = tied(keep_two_y, w_one_y, dkv_x, *near)
+    cut = 2 * rows
+    far = [turned(near[0][:cut], 1), turned(near[1][cut:], -1)]
+    dkv_terms = added(dkv_terms[0::2], dkv_x)
+    dkv_y = y(dkv_terms[1])
+    w_two_y, dkv_y = tied(w_two_y, dkv_y)
+
+    weights = [keep_w, [w_one, w_two], [keep_one_y, keep_two_y], [w_one_y, w_two_y]]
     slots = ((me >> 1) ^ ((col + jnp.arange(count)) % count)).astype(jnp.int32)
-    outs = []
-    for c in range(2):
-        parts = [blocks[c], near[c][0], jnp.concatenate(far[c], axis=0), near[c][1]]
-        even, odd = project(slots, weights, parts)
-        half_sum = added(even, across(odd, 1))
-        outs.append(added(half_sum[0], across(half_sum[1], 2)))
-    return jnp.concatenate(outs, axis=0), dkv_mine
+
+    def partial(devices):
+        places = [[(k, d * rows) for d in devices] for k in (0, 1)]
+        places.append([(3 + d // 2, d % 2 * rows) for d in devices])
+        places.append([(2, d * rows) for d in devices])
+        return project(slots, weights, [tokens, *near, *far], places, rows)
+
+    zero, one, two, three = partial(range(4))
+    there = added(two, across(three, 1))
+    found = across(one, 1)
+    got = x(there)
+    dkv_mine = added(dkv_terms[0], dkv_y)
+    dkv_all = [dkv_mine] + [turned(dkv_mine, k) for k in range(1, count)]
+    total = zero.astype(jnp.float32) + found.astype(jnp.float32) + got.astype(jnp.float32)
+    return total.astype(jnp.bfloat16), dkv_all
 
 
 def solution(mesh):

time: 194 us -> 188 us (0.969); the launches traced: 193 us -> 185 us
  starting transfers between devices: 39.5 us -> 28.4 us
  waiting for transfers between devices: 103 us -> 106 us
  other arithmetic: 4.14 us -> 6.7 us
    ppermute x21 -> x18, waiting for transfers between devices: 60.8 us -> 87.8 us  [across(): return lax.ppermute(block, 'row', [(i, i ^ mask) for i in range(ranks)])]
    ppermute x11 -> x7, waiting for transfers between devices: 42.2 us -> 18 us  [turned(): lax.ppermute(block, 'col', [((i + distance) % count, i) for i in range(co...]
    ppermute x11 -> x7, starting transfers between devices: 20.8 us -> 12.5 us  [turned(): lax.ppermute(block, 'col', [((i + distance) % count, i) for i in range(co...]
    squeeze x4 -> x1, local copies, waits for them, and re-layouts: 6.24 us -> 0.02 us  [paired(): dkv_y = y(dkv_terms[1])]
    dynamic_slice x0 -> x1, local copies, waits for them, and re-layouts: none -> 3.97 us  [local(): pieces.append(lax.dynamic_slice_in_dim(q_weight, start, size, 0))]
    convert_element_type x1, other arithmetic: 0.14 us -> 3.06 us  [paired(): return (total.astype(jnp.bfloat16), dkv_all)]
    ppermute x21 -> x18, starting transfers between devices: 18.6 us -> 15.8 us  [across(): return lax.ppermute(block, 'row', [(i, i ^ mask) for i in range(ranks)])]
    pallas_call x2 -> x1, Pallas kernels: 13 us -> 12.5 us  [project(): pl.pallas_call(functools.partial(project_kernel, len(pieces), places), ou...]
  transfers between devices with their start and end apart: 32 -> 25, of which waited for: 20 -> 14; matrix products, arithmetic and copies ran while one was open for 7% -> 4% of each run, Pallas kernels for 13% -> 10%
where the time goes in v3:
time: 188 us; the launch traced here: 185 us
  waiting for transfers between devices  106 us (56%)
  Pallas kernels  30.5 us (16%)
  starting transfers between devices  28.4 us (15%)
  local copies, waits for them, and re-layouts  12.7 us (7%)
  other arithmetic  6.7 us (4%)
    ppermute x18, waiting for transfers between devices, across(): return lax.ppermute(block, 'row', [(i, i ^ mask) for i in range(ranks)])  87.8 us
    ppermute x7, waiting for transfers between devices, turned(): lax.ppermute(block, 'col', [((i + distance) % count, i) for i in range(co...  18 us
    ppermute x18, starting transfers between devices, across(): return lax.ppermute(block, 'row', [(i, i ^ mask) for i in range(ranks)])  15.8 us
    pallas_call x1, Pallas kernels, attention(): pl.pallas_call(functools.partial(attention_kernel, per_kv, rows, ranks),...  15.7 us
    ppermute x7, starting transfers between devices, turned(): lax.ppermute(block, 'col', [((i + distance) % count, i) for i in range(co...  12.5 us
    pallas_call x1, Pallas kernels, project(): pl.pallas_call(functools.partial(project_kernel, len(pieces), places), ou...  12.5 us
    unnamed x30, local copies, waits for them, and re-layouts  6.38 us
    dynamic_slice x1, local copies, waits for them, and re-layouts, local(): pieces.append(lax.dynamic_slice_in_dim(q_weight, start, size, 0))  3.97 us
  transfers between devices with their start and end apart: 25, of which 14 were waited for; matrix products, arithmetic and copies ran while one was open for 4% of the time, Pallas kernels for 10%

profile of v3, /device:TPU:0, one launch (start us, length us, event | category | flops | bytes accessed | tf_op | source)
XLA Modules:
  0.0 185.0 jit_solution(16964585806742752256)
XLA Ops:
  0.7 1.0 constant_dynamic-slice_fusion.8
  1.7 3.0 %collective-permute-start.1 = (bf16[256,512]{1,0:T(8,128)(2,1)S(1)}, bf16[256,512]{1,0:T(8,128)(2,1)S(1)}, u32[]{:S(2)}, u32[]{:S(2)}) collective-permute-start(bf16[256,512]{1,0:T(8,128)(2,1)S(1)} %get-tuple-element.72), channel_id=1, source_target_pairs={{0,16},{4,20},{8,24},{12,28},{16,0},{20,4},{24,8},{28,12},{1,17},{... | collective-permute-start | bytes 786440 | tf_op jit(solution)/shard_map/ppermute | solution.py:238
  4.7 1.5 collective-permute-start
  6.2 0.0 collective-permute-start.2
  6.2 4.0 %constant_dynamic-slice_fusion.2 = (bf16[256,2048]{1,0:T(8,128)(2,1)}, bf16[256,2048]{1,0:T(8,128)(2,1)S(1)}, bf16[256,2048]{1,0:T(8,128)(2,1)S(1)}, bf16[256,2048]{1,0:T(8,128)(2,1)}) fusion(bf16[1024,2048]{1,0:T(8,128)(2,1)} %param.11, s32[]{:T(128)S(6)} %select_n.58, s32[]{:T(128)S(6)} %select_n.56, s32[]{:T(128)S(6)} %select_n.55, s32[]{:T(128)S(6)} %select_n.57), kind=kLoop, calls=%fused_computation.23 | loop fusion | bytes 8388624 | tf_op jit(solution)/shard_map/dynamic_slice | solution.py:288
  10.2 0.8 collective-permute-done.1
  11.0 2.9 %collective-permute-done = bf16[256,512]{1,0:T(8,128)(2,1)S(1)} collective-permute-done((bf16[256,512]{1,0:T(8,128)(2,1)S(1)}, bf16[256,512]{1,0:T(8,128)(2,1)S(1)}, u32[]{:S(2)}, u32[]{:S(2)}) %collective-permute-start) | collective-permute-done | bytes 262176 | tf_op jit(solution)/shard_map/ppermute | solution.py:238
  13.9 3.9 %collective-permute-done.2 = bf16[256,512]{1,0:T(8,128)(2,1)S(1)} collective-permute-done((bf16[256,512]{1,0:T(8,128)(2,1)S(1)}, bf16[256,512]{1,0:T(8,128)(2,1)S(1)}, u32[]{:S(2)}, u32[]{:S(2)}) %collective-permute-start.2) | collective-permute-done | bytes 262176 | tf_op jit(solution)/shard_map/ppermute | solution.py:238
  17.9 0.7 copy-done.14
  18.6 1.2 pad_maximum_fusion.kv_even
  19.8 0.1 collective-permute-start.3
  19.9 1.0 copy-done
  20.9 0.1 copy.9.seg_query
  21.1 1.7 collective-permute-start.5
  22.8 1.5 collective-permute-start.6
  24.3 0.0 collective-permute-done.3.kv_odd
  24.3 1.2 copy-done.1
  25.5 1.2 copy-done.3
  26.8 1.2 copy-done.4
  28.0 15.7 %attention.1 = (bf16[2,2,256,512]{3,2,1,0:T(8,128)(2,1)S(1)}, bf16[4,256,512]{2,1,0:T(8,128)(2,1)S(1)}, bf16[4,256,512]{2,1,0:T(8,128)(2,1)S(1)}) custom-call(s32[1]{0:T(128)} %bitcast.4.me_ref, s32[2,128,1]{2,1,0:T(8,128)S(1)} %copy.9.seg_query, s32[16,1,128]{2,1,0:T(1,128)S(1)} %bitcast.32, bf16[256,2048]{1,0:T(8,128)(2,1)S(1)} %copy-done.3, ...), custom_call_target="tpu_custom_call" | custom-call | flops 3400000000 | bytes 8000000 | tf_op jit(solution)/shard_map/attention/pallas_call | solution.py:135
  43.7 1.2 dynamic-slice_bitcast_fusion
  44.9 0.2 copy-done.5
  45.1 0.0 collective-permute-start.4
  45.1 2.2 %collective-permute-done.4 = bf16[2,256,512]{2,1,0:T(8,128)(2,1)} collective-permute-done((bf16[2,256,512]{2,1,0:T(8,128)(2,1)}, bf16[2,256,512]{2,1,0:T(8,128)(2,1)}, u32[]{:S(2)}, u32[]{:S(2)}) %collective-permute-start.4) | collective-permute-done | bytes 524320 | tf_op jit(solution)/shard_map/ppermute | solution.py:238
  47.3 1.4 fusion.1
  48.7 0.0 collective-permute-done.5.refs_2_
  48.7 0.0 collective-permute-done.6.refs_4_
  48.7 0.6 collective-permute-start.8
  49.3 13.4 %collective-permute-done.8 = bf16[2,256,512]{2,1,0:T(8,128)(2,1)S(1)} collective-permute-done((bf16[2,256,512]{2,1,0:T(8,128)(2,1)S(1)}, bf16[2,256,512]{2,1,0:T(8,128)(2,1)S(1)}, u32[]{:S(2)}, u32[]{:S(2)}) %collective-permute-start.8) | collective-permute-done | bytes 524320 | tf_op jit(solution)/shard_map/ppermute | solution.py:238
  62.7 0.1 pad_maximum_fusion.1
  62.8 0.6 collective-permute-start.9
  63.4 1.0 collective-permute-start.10
  64.5 1.0 collective-permute-start.11
  65.5 1.6 collective-permute-start.14
  67.0 2.2 %collective-permute-start.13 = (bf16[1024,512]{1,0:T(8,128)(2,1)S(1)}, bf16[1024,512]{1,0:T(8,128)(2,1)S(1)}, u32[]{:S(2)}, u32[]{:S(2)}) collective-permute-start(bf16[1024,512]{1,0:T(8,128)(2,1)S(1)} %bitcast.29), channel_id=1, source_target_pairs={{1,0},{2,1},{3,2},{0,3},{5,4},{6,5},{7,6},{4,7},{9,8},{10,9},{11,1... | collective-permute-start | bytes 3145736 | tf_op jit(solution)/shard_map/ppermute | solution.py:243
  69.3 0.3 add_convert_fusion.2
  69.6 17.7 %collective-permute-done.9.refs_3_ = bf16[256,2048]{1,0:T(8,128)(2,1)S(1)} collective-permute-done((bf16[256,2048]{1,0:T(8,128)(2,1)S(1)}, bf16[256,2048]{1,0:T(8,128)(2,1)S(1)}, u32[]{:S(2)}, u32[]{:S(2)}) %collective-permute-start.9) | collective-permute-done | bytes 1048608 | tf_op jit(solution)/shard_map/ppermute | solution.py:238
  87.3 0.6 collective-permute-start.12
  87.9 1.6 collective-permute-done.10.refs_5_
  89.5 1.0 collective-permute-start.15
  90.5 21.4 %collective-permute-done.11.refs_6_ = bf16[256,2048]{1,0:T(8,128)(2,1)S(1)} collective-permute-done((bf16[256,2048]{1,0:T(8,128)(2,1)}, bf16[256,2048]{1,0:T(8,128)(2,1)S(1)}, u32[]{:S(2)}, u32[]{:S(2)}) %collective-permute-start.11) | collective-permute-done | bytes 1048608 | tf_op jit(solution)/shard_map/ppermute | solution.py:238
  112.0 0.0 collective-permute-done.14.refs_10_
  112.0 0.8 collective-permute-done.13.refs_9_
  112.9 1.2 collective-permute-start.18
  114.0 2.7 %collective-permute-start.17 = (bf16[512,512]{1,0:T(8,128)(2,1)S(1)}, bf16[512,512]{1,0:T(8,128)(2,1)S(1)}, u32[]{:S(2)}, u32[]{:S(2)}) collective-permute-start(bf16[512,512]{1,0:T(8,128)(2,1)S(1)} %slice.21), channel_id=1, source_target_pairs={{1,0},{2,1},{3,2},{0,3},{5,4},{6,5},{7,6},{4,7},{9,8},{10,9},{11,1... | collective-permute-start | bytes 1572872 | tf_op jit(solution)/shard_map/ppermute | solution.py:243
  116.7 0.1 add_convert_fusion.3
  116.9 1.1 collective-permute-start.16
  118.0 20.1 %collective-permute-done.16 = bf16[256,512]{1,0:T(8,128)(2,1)S(1)} collective-permute-done((bf16[256,512]{1,0:T(8,128)(2,1)S(1)}, bf16[256,512]{1,0:T(8,128)(2,1)S(1)}, u32[]{:S(2)}, u32[]{:S(2)}) %collective-permute-start.16) | collective-permute-done | bytes 262176 | tf_op jit(solution)/shard_map/ppermute | solution.py:238
  138.1 0.7 collective-permute-done.17.refs_11_
  138.8 12.5 %project.1 = (bf16[256,2048]{1,0:T(8,128)(2,1)S(1)}, bf16[256,2048]{1,0:T(8,128)(2,1)}, bf16[256,2048]{1,0:T(8,128)(2,1)S(1)}, bf16[256,2048]{1,0:T(8,128)(2,1)S(1)}) custom-call(s32[4]{0:T(128)S(1)} %fusion.5.slot_ref, bf16[256,2048]{1,0:T(8,128)(2,1)S(1)} %get-tuple-element.31.refs_0_, bf16[256,2048]{1,0:T(8,128)(2,1)S(1)} %get-tuple-element.32.refs_1_, ...), custom_call_target="tpu_custom_call" | custom-call | flops 8589934592 | bytes 12582912 | tf_op jit(solution)/shard_map/project/pallas_call | solution.py:197
  151.3 0.5 collective-permute-start.19
  151.8 3.6 %collective-permute-done.20 = bf16[256,2048]{1,0:T(8,128)(2,1)S(1)} collective-permute-done((bf16[256,2048]{1,0:T(8,128)(2,1)S(1)}, bf16[256,2048]{1,0:T(8,128)(2,1)S(1)}, u32[]{:S(2)}, u32[]{:S(2)}) %collective-permute-start.20) | collective-permute-done | bytes 1048608 | tf_op jit(solution)/shard_map/ppermute | solution.py:238
  155.4 0.4 add_convert_fusion.1
  155.8 1.5 collective-permute-start.21
  157.3 0.1 fusion.4.refs_0_
  157.4 0.9 collective-permute-start.24
  158.3 2.6 %collective-permute-start.23 = (bf16[256,512]{1,0:T(8,128)(2,1)S(1)}, bf16[256,512]{1,0:T(8,128)(2,1)S(1)}, u32[]{:S(2)}, u32[]{:S(2)}) collective-permute-start(bf16[256,512]{1,0:T(8,128)(2,1)S(1)} %fusion.4.refs_0_), channel_id=1, source_target_pairs={{2,0},{3,1},{0,2},{1,3},{6,4},{7,5},{4,6},{5,7},{10,8},{11,9},{8,1... | collective-permute-start | bytes 786440 | tf_op jit(solution)/shard_map/ppermute | solution.py:243
  160.9 1.3 collective-permute-start.22
  162.3 6.3 %collective-permute-done.24.refs_3_ = bf16[256,512]{1,0:T(8,128)(2,1)S(1)} collective-permute-done((bf16[256,512]{1,0:T(8,128)(2,1)S(1)}, bf16[256,512]{1,0:T(8,128)(2,1)S(1)}, u32[]{:S(2)}, u32[]{:S(2)}) %collective-permute-start.24) | collective-permute-done | bytes 262176 | tf_op jit(solution)/shard_map/ppermute | solution.py:243
  168.6 10.2 %collective-permute-done.23.refs_2_ = bf16[256,512]{1,0:T(8,128)(2,1)S(1)} collective-permute-done((bf16[256,512]{1,0:T(8,128)(2,1)S(1)}, bf16[256,512]{1,0:T(8,128)(2,1)S(1)}, u32[]{:S(2)}, u32[]{:S(2)}) %collective-permute-start.23) | collective-permute-done | bytes 262176 | tf_op jit(solution)/shard_map/ppermute | solution.py:243
  178.8 0.7 copy-done.10
  179.5 0.1 copy-done.11
  179.6 2.3 %by_column.1 = (bf16[256,1024]{1,0:T(8,128)(2,1)}, bf16[256,1024]{1,0:T(8,128)(2,1)}) custom-call(s32[1]{0:T(128)} %bitcast.15.col_ref, bf16[256,512]{1,0:T(8,128)(2,1)} %copy-done.8, bf16[256,512]{1,0:T(8,128)(2,1)} %copy-done.11, bf16[256,512]{1,0:T(8,128)(2,1)} %copy-done.10, bf16[256,512]{1,0:T(8,128)(2,1)} %copy-done.9), custom_call_target="tpu_custom_call" | custom-call | tf_op jit(solution)/shard_map/by_column/pallas_call | solution.py:227
  182.0 3.1 %add_convert_fusion = bf16[256,2048]{1,0:T(8,128)(2,1)} fusion(bf16[256,2048]{1,0:T(8,128)(2,1)} %collective-permute-done.21, bf16[256,2048]{1,0:T(8,128)(2,1)} %collective-permute-done.19, bf16[256,2048]{1,0:T(8,128)(2,1)S(1)} %get-tuple-element.52), kind=kLoop, calls=%fused_computation | loop fusion | flops 3145728 | bytes 4194304 | tf_op jit(solution)/shard_map/convert_element_type | solution.py:391
  (39 shorter events, 0.3 us)
Async XLA Ops:
  1.7 9.3 %collective-permute-start.1 = (bf16[256,512]{1,0:T(8,128)(2,1)S(1)}, bf16[256,512]{1,0:T(8,128)(2,1)S(1)}, u32[]{:S(2)}, u32[]{:S(2)}) collective-permute-start(bf16[256,512]{1,0:T(8,128)(2,1)S(1)} %get-tuple-element.72), channel_id=1, source_target_pairs={{0,16},{4,20},{8,24},{12,28},{16,0},{20,4},{24,8},{28,12},{1,17},{... | collective-permute-start | bytes 786440 | tf_op jit(solution)/shard_map/ppermute | solution.py:238
  4.7 9.2 %collective-permute-start = (bf16[256,512]{1,0:T(8,128)(2,1)S(1)}, bf16[256,512]{1,0:T(8,128)(2,1)S(1)}, u32[]{:S(2)}, u32[]{:S(2)}) collective-permute-start(bf16[256,512]{1,0:T(8,128)(2,1)S(1)} %get-tuple-element.72), channel_id=1, source_target_pairs={{0,8},{4,12},{8,0},{12,4},{16,24},{20,28},{24,16},{28,20},{1,9},{5... | collective-permute-start | bytes 786440 | tf_op jit(solution)/shard_map/ppermute | solution.py:238
  6.2 11.7 %collective-permute-start.2 = (bf16[256,512]{1,0:T(8,128)(2,1)S(1)}, bf16[256,512]{1,0:T(8,128)(2,1)S(1)}, u32[]{:S(2)}, u32[]{:S(2)}) collective-permute-start(bf16[256,512]{1,0:T(8,128)(2,1)S(1)} %get-tuple-element.72), channel_id=1, source_target_pairs={{0,24},{4,28},{8,16},{12,20},{16,8},{20,12},{24,0},{28,4},{1,25},{... | collective-permute-start | bytes 786440 | tf_op jit(solution)/shard_map/ppermute | solution.py:238
  10.2 10.7 %copy-start.2 = (s32[2048]{0:T(1024)S(1)}, s32[2048]{0:T(1024)}, u32[]{:S(2)}) copy-start(s32[2048]{0:T(1024)} %param.10) | copy-start | bytes 24580
  11.0 6.9 %copy-start.12 = (bf16[256,512]{1,0:T(8,128)(2,1)}, bf16[256,512]{1,0:T(8,128)(2,1)S(1)}, u32[]{:S(2)}) copy-start(bf16[256,512]{1,0:T(8,128)(2,1)S(1)} %collective-permute-done.1) | copy-start | bytes 786436
  13.9 4.0 %copy-start.13 = (bf16[256,512]{1,0:T(8,128)(2,1)}, bf16[256,512]{1,0:T(8,128)(2,1)S(1)}, u32[]{:S(2)}) copy-start(bf16[256,512]{1,0:T(8,128)(2,1)S(1)} %collective-permute-done) | copy-start | bytes 786436
  17.9 0.7 copy-start.14
  19.8 4.5 %collective-permute-start.3 = (bf16[4,256,512]{2,1,0:T(8,128)(2,1)S(1)}, bf16[4,256,512]{2,1,0:T(8,128)(2,1)}, u32[]{:S(2)}, u32[]{:S(2)}) collective-permute-start(bf16[4,256,512]{2,1,0:T(8,128)(2,1)S(1)} %pad_maximum_fusion.kv_even), channel_id=1, source_target_pairs={{0,4},{4,0},{8,12},{12,8},{16,20},{20,16},{24,28},{28,24},{1,5},{5... | collective-permute-start | bytes 3145736 | tf_op jit(solution)/shard_map/ppermute | solution.py:238
  19.9 1.0 copy-start
  21.1 27.6 %collective-permute-start.5 = (bf16[256,2048]{1,0:T(8,128)(2,1)}, bf16[256,2048]{1,0:T(8,128)(2,1)}, u32[]{:S(2)}, u32[]{:S(2)}) collective-permute-start(bf16[256,2048]{1,0:T(8,128)(2,1)} %get-tuple-element.35), channel_id=1, source_target_pairs={{0,8},{4,12},{8,0},{12,4},{16,24},{20,28},{24,16},{28,20},{1,9},{5... | collective-permute-start | bytes 3145736 | tf_op jit(solution)/shard_map/ppermute | solution.py:238
  22.8 25.9 %collective-permute-start.6 = (bf16[256,2048]{1,0:T(8,128)(2,1)S(1)}, bf16[256,2048]{1,0:T(8,128)(2,1)}, u32[]{:S(2)}, u32[]{:S(2)}) collective-permute-start(bf16[256,2048]{1,0:T(8,128)(2,1)S(1)} %get-tuple-element.31.refs_0_), channel_id=1, source_target_pairs={{0,16},{4,20},{8,24},{12,28},{16,0},{20,4},{24,8},{28,12},{1,17},{... | collective-permute-start | bytes 3145736 | tf_op jit(solution)/shard_map/ppermute | solution.py:238
  24.3 1.2 copy-start.1
  25.5 1.2 copy-start.3
  26.8 1.2 copy-start.4
  43.7 1.4 copy-start.5
  45.1 2.3 %collective-permute-start.4 = (bf16[2,256,512]{2,1,0:T(8,128)(2,1)}, bf16[2,256,512]{2,1,0:T(8,128)(2,1)}, u32[]{:S(2)}, u32[]{:S(2)}) collective-permute-start(bf16[2,256,512]{2,1,0:T(8,128)(2,1)} %get-tuple-element.65), channel_id=1, source_target_pairs={{0,4},{4,0},{8,12},{12,8},{16,20},{20,16},{24,28},{28,24},{1,5},{5... | collective-permute-start | bytes 1572872 | tf_op jit(solution)/shard_map/ppermute | solution.py:238
  45.1 4.2 %copy-start.6 = (bf16[4,256,512]{2,1,0:T(8,128)(2,1)S(1)}, bf16[4,256,512]{2,1,0:T(8,128)(2,1)}, u32[]{:S(2)}) copy-start(bf16[4,256,512]{2,1,0:T(8,128)(2,1)} %copy-done.5) | copy-start | bytes 3145732
  47.3 15.5 %copy-start.7 = (bf16[256,2048]{1,0:T(8,128)(2,1)S(1)}, bf16[256,2048]{1,0:T(8,128)(2,1)}, u32[]{:S(2)}) copy-start(bf16[256,2048]{1,0:T(8,128)(2,1)} %get-tuple-element.41) | copy-start | bytes 3145732
  48.7 14.0 %collective-permute-start.8 = (bf16[2,256,512]{2,1,0:T(8,128)(2,1)S(1)}, bf16[2,256,512]{2,1,0:T(8,128)(2,1)S(1)}, u32[]{:S(2)}, u32[]{:S(2)}) collective-permute-start(bf16[2,256,512]{2,1,0:T(8,128)(2,1)S(1)} %get-tuple-element.40), channel_id=1, source_target_pairs={{0,8},{4,12},{8,0},{12,4},{16,24},{20,28},{24,16},{28,20},{1,9},{5... | collective-permute-start | bytes 1572872 | tf_op jit(solution)/shard_map/ppermute | solution.py:238
  49.3 17.7 %collective-permute-start.7 = (bf16[4,256,512]{2,1,0:T(8,128)(2,1)S(1)}, bf16[4,256,512]{2,1,0:T(8,128)(2,1)S(1)}, u32[]{:S(2)}, u32[]{:S(2)}) collective-permute-start(bf16[4,256,512]{2,1,0:T(8,128)(2,1)S(1)} %copy-done.6), channel_id=1, source_target_pairs={{0,4},{4,0},{8,12},{12,8},{16,20},{20,16},{24,28},{28,24},{1,5},{5... | collective-permute-start | bytes 3145736 | tf_op jit(solution)/shard_map/ppermute | solution.py:238
  62.8 24.4 %collective-permute-start.9 = (bf16[256,2048]{1,0:T(8,128)(2,1)S(1)}, bf16[256,2048]{1,0:T(8,128)(2,1)S(1)}, u32[]{:S(2)}, u32[]{:S(2)}) collective-permute-start(bf16[256,2048]{1,0:T(8,128)(2,1)S(1)} %copy-done.7), channel_id=1, source_target_pairs={{0,8},{4,12},{8,0},{12,4},{16,24},{20,28},{24,16},{28,20},{1,9},{5... | collective-permute-start | bytes 3145736 | tf_op jit(solution)/shard_map/ppermute | solution.py:238
  63.4 26.1 %collective-permute-start.10 = (bf16[256,2048]{1,0:T(8,128)(2,1)S(1)}, bf16[256,2048]{1,0:T(8,128)(2,1)S(1)}, u32[]{:S(2)}, u32[]{:S(2)}) collective-permute-start(bf16[256,2048]{1,0:T(8,128)(2,1)S(1)} %get-tuple-element.32.refs_1_), channel_id=1, source_target_pairs={{0,16},{4,20},{8,24},{12,28},{16,0},{20,4},{24,8},{28,12},{1,17},{... | collective-permute-start | bytes 3145736 | tf_op jit(solution)/shard_map/ppermute | solution.py:238
  64.5 47.5 %collective-permute-start.11 = (bf16[256,2048]{1,0:T(8,128)(2,1)}, bf16[256,2048]{1,0:T(8,128)(2,1)S(1)}, u32[]{:S(2)}, u32[]{:S(2)}) collective-permute-start(bf16[256,2048]{1,0:T(8,128)(2,1)} %collective-permute-done.5.refs_2_), channel_id=1, source_target_pairs={{0,16},{4,20},{8,24},{12,28},{16,0},{20,4},{24,8},{28,12},{1,17},{... | collective-permute-start | bytes 3145736 | tf_op jit(solution)/shard_map/ppermute | solution.py:238
  65.5 46.5 %collective-permute-start.14 = (bf16[1024,512]{1,0:T(8,128)(2,1)S(1)}, bf16[1024,512]{1,0:T(8,128)(2,1)S(1)}, u32[]{:S(2)}, u32[]{:S(2)}) collective-permute-start(bf16[1024,512]{1,0:T(8,128)(2,1)S(1)} %bitcast.28), channel_id=1, source_target_pairs={{3,0},{0,1},{1,2},{2,3},{7,4},{4,5},{5,6},{6,7},{11,8},{8,9},{9,10... | collective-permute-start | bytes 3145736 | tf_op jit(solution)/shard_map/ppermute | solution.py:243
  67.0 45.7 %collective-permute-start.13 = (bf16[1024,512]{1,0:T(8,128)(2,1)S(1)}, bf16[1024,512]{1,0:T(8,128)(2,1)S(1)}, u32[]{:S(2)}, u32[]{:S(2)}) collective-permute-start(bf16[1024,512]{1,0:T(8,128)(2,1)S(1)} %bitcast.29), channel_id=1, source_target_pairs={{1,0},{2,1},{3,2},{0,3},{5,4},{6,5},{7,6},{4,7},{9,8},{10,9},{11,1... | collective-permute-start | bytes 3145736 | tf_op jit(solution)/shard_map/ppermute | solution.py:243
  87.3 25.5 %collective-permute-start.12 = (bf16[2,256,512]{2,1,0:T(8,128)(2,1)S(1)}, bf16[2,256,512]{2,1,0:T(8,128)(2,1)S(1)}, u32[]{:S(2)}, u32[]{:S(2)}) collective-permute-start(bf16[2,256,512]{2,1,0:T(8,128)(2,1)S(1)} %slice.18), channel_id=1, source_target_pairs={{0,8},{4,12},{8,0},{12,4},{16,24},{20,28},{24,16},{28,20},{1,9},{5... | collective-permute-start | bytes 1572872 | tf_op jit(solution)/shard_map/ppermute | solution.py:238
  89.5 48.6 %collective-permute-start.15 = (bf16[256,2048]{1,0:T(8,128)(2,1)S(1)}, bf16[256,2048]{1,0:T(8,128)(2,1)S(1)}, u32[]{:S(2)}, u32[]{:S(2)}) collective-permute-start(bf16[256,2048]{1,0:T(8,128)(2,1)S(1)} %collective-permute-done.9.refs_3_), channel_id=1, source_target_pairs={{0,16},{4,20},{8,24},{12,28},{16,0},{20,4},{24,8},{28,12},{1,17},{... | collective-permute-start | bytes 3145736 | tf_op jit(solution)/shard_map/ppermute | solution.py:238
  112.9 25.2 %collective-permute-start.18 = (bf16[512,512]{1,0:T(8,128)(2,1)S(1)}, bf16[512,512]{1,0:T(8,128)(2,1)S(1)}, u32[]{:S(2)}, u32[]{:S(2)}) collective-permute-start(bf16[512,512]{1,0:T(8,128)(2,1)S(1)} %slice.22), channel_id=1, source_target_pairs={{3,0},{0,1},{1,2},{2,3},{7,4},{4,5},{5,6},{6,7},{11,8},{8,9},{9,10... | collective-permute-start | bytes 1572872 | tf_op jit(solution)/shard_map/ppermute | solution.py:243
  114.0 24.8 %collective-permute-start.17 = (bf16[512,512]{1,0:T(8,128)(2,1)S(1)}, bf16[512,512]{1,0:T(8,128)(2,1)S(1)}, u32[]{:S(2)}, u32[]{:S(2)}) collective-permute-start(bf16[512,512]{1,0:T(8,128)(2,1)S(1)} %slice.21), channel_id=1, source_target_pairs={{1,0},{2,1},{3,2},{0,3},{5,4},{6,5},{7,6},{4,7},{9,8},{10,9},{11,1... | collective-permute-start | bytes 1572872 | tf_op jit(solution)/shard_map/ppermute | solution.py:243
  116.9 21.2 %collective-permute-start.16 = (bf16[256,512]{1,0:T(8,128)(2,1)S(1)}, bf16[256,512]{1,0:T(8,128)(2,1)S(1)}, u32[]{:S(2)}, u32[]{:S(2)}) collective-permute-start(bf16[256,512]{1,0:T(8,128)(2,1)S(1)} %slice_bitcast_fusion.1), channel_id=1, source_target_pairs={{0,16},{4,20},{8,24},{12,28},{16,0},{20,4},{24,8},{28,12},{1,17},{... | collective-permute-start | bytes 786440 | tf_op jit(solution)/shard_map/ppermute | solution.py:238
  151.3 4.1 %collective-permute-start.20 = (bf16[256,2048]{1,0:T(8,128)(2,1)S(1)}, bf16[256,2048]{1,0:T(8,128)(2,1)S(1)}, u32[]{:S(2)}, u32[]{:S(2)}) collective-permute-start(bf16[256,2048]{1,0:T(8,128)(2,1)S(1)} %get-tuple-element.55), channel_id=1, source_target_pairs={{0,4},{4,0},{8,12},{12,8},{16,20},{20,16},{24,28},{28,24},{1,5},{5... | collective-permute-start | bytes 3145736 | tf_op jit(solution)/shard_map/ppermute | solution.py:238
  151.3 30.7 %collective-permute-start.19 = (bf16[256,2048]{1,0:T(8,128)(2,1)}, bf16[256,2048]{1,0:T(8,128)(2,1)}, u32[]{:S(2)}, u32[]{:S(2)}) collective-permute-start(bf16[256,2048]{1,0:T(8,128)(2,1)} %get-tuple-element.53), channel_id=1, source_target_pairs={{0,4},{4,0},{8,12},{12,8},{16,20},{20,16},{24,28},{28,24},{1,5},{5... | collective-permute-start | bytes 3145736 | tf_op jit(solution)/shard_map/ppermute | solution.py:238
  155.8 26.1 %collective-permute-start.21 = (bf16[256,2048]{1,0:T(8,128)(2,1)S(1)}, bf16[256,2048]{1,0:T(8,128)(2,1)}, u32[]{:S(2)}, u32[]{:S(2)}) collective-permute-start(bf16[256,2048]{1,0:T(8,128)(2,1)S(1)} %add_convert_fusion.1), channel_id=1, source_target_pairs={{0,8},{4,12},{8,0},{12,4},{16,24},{20,28},{24,16},{28,20},{1,9},{5... | collective-permute-start | bytes 3145736 | tf_op jit(solution)/shard_map/ppermute | solution.py:238
  157.4 21.4 %copy-start.8 = (bf16[256,512]{1,0:T(8,128)(2,1)}, bf16[256,512]{1,0:T(8,128)(2,1)S(1)}, u32[]{:S(2)}) copy-start(bf16[256,512]{1,0:T(8,128)(2,1)S(1)} %fusion.4.refs_0_) | copy-start | bytes 786436
  157.4 11.1 %collective-permute-start.24 = (bf16[256,512]{1,0:T(8,128)(2,1)S(1)}, bf16[256,512]{1,0:T(8,128)(2,1)S(1)}, u32[]{:S(2)}, u32[]{:S(2)}) collective-permute-start(bf16[256,512]{1,0:T(8,128)(2,1)S(1)} %fusion.4.refs_0_), channel_id=1, source_target_pairs={{3,0},{0,1},{1,2},{2,3},{7,4},{4,5},{5,6},{6,7},{11,8},{8,9},{9,10... | collective-permute-start | bytes 786440 | tf_op jit(solution)/shard_map/ppermute | solution.py:243
  158.3 20.4 %collective-permute-start.23 = (bf16[256,512]{1,0:T(8,128)(2,1)S(1)}, bf16[256,512]{1,0:T(8,128)(2,1)S(1)}, u32[]{:S(2)}, u32[]{:S(2)}) collective-permute-start(bf16[256,512]{1,0:T(8,128)(2,1)S(1)} %fusion.4.refs_0_), channel_id=1, source_target_pairs={{2,0},{3,1},{0,2},{1,3},{6,4},{7,5},{4,6},{5,7},{10,8},{11,9},{8,1... | collective-permute-start | bytes 786440 | tf_op jit(solution)/shard_map/ppermute | solution.py:243
  160.9 17.9 %collective-permute-start.22 = (bf16[256,512]{1,0:T(8,128)(2,1)S(1)}, bf16[256,512]{1,0:T(8,128)(2,1)S(1)}, u32[]{:S(2)}, u32[]{:S(2)}) collective-permute-start(bf16[256,512]{1,0:T(8,128)(2,1)S(1)} %fusion.4.refs_0_), channel_id=1, source_target_pairs={{1,0},{2,1},{3,2},{0,3},{5,4},{6,5},{7,6},{4,7},{9,8},{10,9},{11,1... | collective-permute-start | bytes 786440 | tf_op jit(solution)/shard_map/ppermute | solution.py:243
  168.6 10.2 %copy-start.9 = (bf16[256,512]{1,0:T(8,128)(2,1)}, bf16[256,512]{1,0:T(8,128)(2,1)S(1)}, u32[]{:S(2)}) copy-start(bf16[256,512]{1,0:T(8,128)(2,1)S(1)} %collective-permute-done.24.refs_3_) | copy-start | bytes 786436
  178.8 0.7 copy-start.10
  178.8 0.8 copy-start.11

commit v4 on v3

--- a/solution.py
+++ b/solution.py
@@ -160,54 +160,64 @@
     )(me, seg_query, seg_key, queries, grad_attn, kv_even, kv_odd)
 
 
-def project_kernel(pieces_here, places, slot_ref, *refs):
+def project_kernel(pieces_here, weights, places, rest, last_ref, slot_ref, *refs):
     group = len(places[0])
-    count = len(places)
     outs, lhs = refs[-1 - group:-1], refs[-1]
     pieces, sources = refs[:pieces_here], refs[pieces_here:-1 - group]
+    former = None
+    if rest:
+        sources, former = sources[:-group], sources[-group:]
     step, features = outs[0].shape
     depth = sources[0].shape[1]
-    for k in range(count):
-        at = pl.ds(pl.multiple_of(slot_ref[k] * depth, depth), depth)
+    last = last_ref[0]
+    for k, place in enumerate(places):
+        slot = slot_ref[k]
+        at = pl.multiple_of(0 if rest else jnp.where(slot > last, slot - 1, slot) * depth, depth)
         for i in range(group):
-            source, first = places[k][i]
-            lhs[i * step:(i + 1) * step, at] = sources[source][first:first + step, :]
+            source, first = place[i]
+            lhs[i * step:(i + 1) * step, pl.ds(at, depth)] = sources[source][first:first + step, :]
     tile = min(256, features)
-
-    def columns(n, carry):
-        at = pl.ds(pl.multiple_of(n * tile, tile), tile)
-        weight = jnp.concatenate([piece[:, at] for piece in pieces], axis=0)
-        for i in range(group):
-            rows = slice(i * step, (i + 1) * step)
-            out = jnp.dot(lhs[rows, :], weight, preferred_element_type=jnp.float32)
-            outs[i][:, at] = out.astype(jnp.bfloat16)
-        return carry
-
-    lax.fori_loop(0, features // tile, columns, 0)
-
-
-def project(slots, weights, sources, places, step):
-    count = len(weights)
+    for e in range(len(weights)):
+        used = weights[e] if rest else sum(weights[:e] + weights[e + 1:], [])
+
+        @pl.when(last == e)
+        def _(used=used):
+            def columns(n, carry):
+                at = pl.ds(pl.multiple_of(n * tile, tile), tile)
+                weight = [pieces[i][first:first + size, at] for i, first, size in used]
+                weight = jnp.concatenate(weight, axis=0)
+                for i in range(group):
+                    rows = slice(i * step, (i + 1) * step)
+                    out = jnp.dot(lhs[rows, :], weight, preferred_element_type=jnp.float32)
+                    if former is not None:
+                        out += former[i][:, at].astype(jnp.float32)
+                    outs[i][:, at] = out.astype(jnp.bfloat16)
+                return carry
+
+            lax.fori_loop(0, features // tile, columns, 0)
+
+
+def project(last, slots, pieces, weights, sources, places, step, former=()):
     group = len(places[0])
     depth = sources[0].shape[1]
-    pieces = [piece for weight in weights for piece in weight]
     features = pieces[0].shape[1]
     smem = pl.BlockSpec(memory_space=pltpu.SMEM)
     vmem = pl.BlockSpec(memory_space=pltpu.VMEM)
+    operands = [*pieces, *sources, *former]
     return pl.pallas_call(
-        functools.partial(project_kernel, len(pieces), places),
+        functools.partial(project_kernel, len(pieces), weights, places, bool(former)),
         out_shape=[jax.ShapeDtypeStruct((step, features), jnp.bfloat16)] * group,
-        in_specs=[smem] + [vmem] * (len(pieces) + len(sources)),
+        in_specs=[smem, smem] + [vmem] * len(operands),
         out_specs=[vmem] * group,
-        scratch_shapes=[pltpu.VMEM((group * step, count * depth), jnp.bfloat16)],
+        scratch_shapes=[pltpu.VMEM((group * step, len(places) * depth), jnp.bfloat16)],
         compiler_params=pltpu.CompilerParams(vmem_limit_bytes=32 << 20),
         cost_estimate=pl.CostEstimate(
-            flops=2 * group * step * depth * count * features,
-            bytes_accessed=2 * (group * step * features + count * depth * features),
+            flops=2 * group * step * depth * len(places) * features,
+            bytes_accessed=2 * (group * step * features + len(places) * depth * features),
             transcendentals=0,
         ),
         name="project",
-    )(slots, *pieces, *sources)
+    )(last, slots, *operands)
 
 
 def columns_kernel(col_ref, *refs):
@@ -282,7 +292,8 @@
         wide = rows_w // 2
         pieces = []
         for start, size in (
-            (side * wide, wide // 2), (side * wide + wide // 2, wide // 2),
+            (side * wide, wide // 2), (side * wide + wide // 2, wide // 4),
+            (side * wide + wide * 3 // 4, wide // 4),
             ((1 - side) * wide, wide // 2), ((1 - side) * wide + wide // 2, wide // 2),
         ):
             pieces.append(lax.dynamic_slice_in_dim(q_weight, start, size, 0))
@@ -337,7 +348,7 @@
     core = me & 1
     side = (me >> 1) & 1
 
-    keep_w, (send_one, send_two) = pieces[:2], pieces[2:]
+    keep_w, (send_one, send_two) = pieces[:3], pieces[3:]
 
     def x(block):
         return across(block, 2)
@@ -354,41 +365,48 @@
     keep = lax.dynamic_index_in_dim(both, side, 0, keepdims=False)
     send = lax.dynamic_index_in_dim(both, 1 - side, 0, keepdims=False)
     send, w_one, keep_one_y = tied(send, w_one, keep_one_y)
+    keep_w[1], send = tied(keep_w[1], send)
     keep_two_y = y(keep_w[1])
     tokens = jnp.concatenate([keep, x(send)], axis=0)
     tokens = tokens.reshape(4 * rows, -1)
-    send_two, tokens = tied(send_two, tokens)
+    last_one = jnp.concatenate([keep_w[2], w_one], axis=0)
+    dkv_terms = added(dkv_even, across(dkv_odd, 1))
+    send_two, last_one, keep_two_y, dkv_terms, tokens = tied(
+        send_two, last_one, keep_two_y, dkv_terms, tokens
+    )
     near = [turned(tokens, 1), turned(tokens, -1)]
+    last_one_y = y(last_one)
     w_two = x(send_two)
-    w_one_y = y(w_one)
-    dkv_terms = added(dkv_even, across(dkv_odd, 1))
-    dkv_terms, w_two = tied(dkv_terms, w_two)
     dkv_x = x(dkv_terms[1::2])
     w_two_y = y(w_two)
-    keep_two_y, w_one_y, dkv_x, near[0], near[1] = tied(keep_two_y, w_one_y, dkv_x, *near)
+    last_one_y, near[0], near[1] = tied(last_one_y, *near)
     cut = 2 * rows
     far = [turned(near[0][:cut], 1), turned(near[1][cut:], -1)]
     dkv_terms = added(dkv_terms[0::2], dkv_x)
     dkv_y = y(dkv_terms[1])
-    w_two_y, dkv_y = tied(w_two_y, dkv_y)
-
-    weights = [keep_w, [w_one, w_two], [keep_one_y, keep_two_y], [w_one_y, w_two_y]]
+
+    pieces = [*keep_w, w_one, w_two, keep_one_y, keep_two_y, last_one_y, w_two_y]
+    sizes = [piece.shape[0] for piece in pieces]
+    last = sizes[2]
+    weights = [
+        [(i, 0, sizes[i]) for i in (0, 1, 2)], [(i, 0, sizes[i]) for i in (3, 4)],
+        [(5, 0, sizes[5]), (6, 0, sizes[6]), (7, 0, last)], [(7, last, sizes[7] - last), (8, 0, sizes[8])],
+    ]
     slots = ((me >> 1) ^ ((col + jnp.arange(count)) % count)).astype(jnp.int32)
-
-    def partial(devices):
-        places = [[(k, d * rows) for d in devices] for k in (0, 1)]
-        places.append([(3 + d // 2, d % 2 * rows) for d in devices])
-        places.append([(2, d * rows) for d in devices])
-        return project(slots, weights, [tokens, *near, *far], places, rows)
-
-    zero, one, two, three = partial(range(4))
+    devices = range(4)
+    places = [[(k, d * rows) for d in devices] for k in range(3)]
+    most = project(slots[2:3], slots[jnp.array([0, 1, 3])], pieces, weights, [tokens, *near], places, rows)
+    *most, dkv_y = tied(*most, dkv_y)
+    places = [[(d // 2, d % 2 * rows) for d in devices]]
+    zero, one, two, three = project(slots[2:3], slots[2:3], pieces, weights, far, places, rows, most)
     there = added(two, across(three, 1))
     found = across(one, 1)
     got = x(there)
     dkv_mine = added(dkv_terms[0], dkv_y)
     dkv_all = [dkv_mine] + [turned(dkv_mine, k) for k in range(1, count)]
-    total = zero.astype(jnp.float32) + found.astype(jnp.float32) + got.astype(jnp.float32)
-    return total.astype(jnp.bfloat16), dkv_all
+    mine = added(zero, found)
+    mine, *dkv_all = tied(mine, *dkv_all)
+    return added(mine, got), dkv_all
 
 
 def solution(mesh):

time: 188 us -> 182 us (0.968)
  waiting for transfers between devices: 106 us -> 83.4 us
  Pallas kernels: 30.5 us -> 38.2 us
  local copies, waits for them, and re-layouts: 12.7 us -> 16.9 us
  other arithmetic: 6.7 us -> 9.98 us
  starting transfers between devices: 28.4 us -> 30.4 us
    ppermute x18, waiting for transfers between devices: 87.8 us -> 51.3 us  [across(): return lax.ppermute(block, 'row', [(i, i ^ mask) for i in range(ranks)])]
    ppermute x7, waiting for transfers between devices: 18 us -> 32.1 us  [turned(): lax.ppermute(block, 'col', [((i + distance) % count, i) for i in range(co...]
    pallas_call x1 -> x2, Pallas kernels: 12.5 us -> 19.3 us  [project(): pl.pallas_call(functools.partial(project_kernel, len(pieces), weights, pl...]
    convert_element_type x4 -> x6, other arithmetic: 0.89 us -> 5.15 us  [added(): (one.astype(jnp.float32) + two.astype(jnp.float32)).astype(jnp.bfloat16)]
    convert_element_type x1 -> x0, other arithmetic: 3.06 us -> none  [paired(): return (total.astype(jnp.bfloat16), dkv_all)]
    ppermute x18, starting transfers between devices: 15.8 us -> 18.8 us  [across(): return lax.ppermute(block, 'row', [(i, i ^ mask) for i in range(ranks)])]
    slice x2, local copies, waits for them, and re-layouts: 0.07 us -> 2.15 us  [paired(): far = [turned(near[0][:cut], 1), turned(near[1][cut:], -1)]]
    dynamic_slice x1 -> x2, local copies, waits for them, and re-layouts: 3.97 us -> 4.89 us  [local(): pieces.append(lax.dynamic_slice_in_dim(q_weight, start, size, 0))]
  transfers between devices with their start and end apart: 25 -> 25, of which waited for: 14 -> 12; matrix products, arithmetic and copies ran while one was open for 4% -> 10% of each run, Pallas kernels for 10% -> 17%
where the time goes in v4:
time: 182 us; the launch traced here: 180 us
  waiting for transfers between devices  83.4 us (46%)
  Pallas kernels  38.2 us (21%)
  starting transfers between devices  30.4 us (17%)
  local copies, waits for them, and re-layouts  16.9 us (9%)
  other arithmetic  9.98 us (5%)
    ppermute x18, waiting for transfers between devices, across(): return lax.ppermute(block, 'row', [(i, i ^ mask) for i in range(ranks)])  51.3 us
    ppermute x7, waiting for transfers between devices, turned(): lax.ppermute(block, 'col', [((i + distance) % count, i) for i in range(co...  32.1 us
    pallas_call x2, Pallas kernels, project(): pl.pallas_call(functools.partial(project_kernel, len(pieces), weights, pl...  19.3 us
    ppermute x18, starting transfers between devices, across(): return lax.ppermute(block, 'row', [(i, i ^ mask) for i in range(ranks)])  18.8 us
    pallas_call x1, Pallas kernels, attention(): pl.pallas_call(functools.partial(attention_kernel, per_kv, rows, ranks),...  16.6 us
    ppermute x7, starting transfers between devices, turned(): lax.ppermute(block, 'col', [((i + distance) % count, i) for i in range(co...  11.6 us
    unnamed x28, local copies, waits for them, and re-layouts  5.67 us
    convert_element_type x6, other arithmetic, added(): (one.astype(jnp.float32) + two.astype(jnp.float32)).astype(jnp.bfloat16)  5.15 us
  transfers between devices with their start and end apart: 25, of which 12 were waited for; matrix products, arithmetic and copies ran while one was open for 10% of the time, Pallas kernels for 17%

profile of v4, /device:TPU:0, one launch (start us, length us, event | category | flops | bytes accessed | tf_op | source)
XLA Modules:
  0.0 179.8 jit_solution(10568516984201162925)
XLA Ops:
  0.7 1.0 constant_dynamic-slice_fusion.9
  1.7 3.0 %collective-permute-start.1 = (bf16[256,512]{1,0:T(8,128)(2,1)S(1)}, bf16[256,512]{1,0:T(8,128)(2,1)S(1)}, u32[]{:S(2)}, u32[]{:S(2)}) collective-permute-start(bf16[256,512]{1,0:T(8,128)(2,1)S(1)} %get-tuple-element.101), channel_id=1, source_target_pairs={{0,16},{4,20},{8,24},{12,28},{16,0},{20,4},{24,8},{28,12},{1,17},{... | collective-permute-start | bytes 786440 | tf_op jit(solution)/shard_map/ppermute | solution.py:248
  4.7 1.5 collective-permute-start
  6.2 3.6 %constant_dynamic-slice_fusion.2 = (bf16[256,2048]{1,0:T(8,128)(2,1)}, bf16[256,2048]{1,0:T(8,128)(2,1)S(1)}, bf16[256,2048]{1,0:T(8,128)(2,1)}) fusion(bf16[1024,2048]{1,0:T(8,128)(2,1)} %param.12, s32[]{:T(128)S(6)} %select_n.65, s32[]{:T(128)S(6)} %select_n.61, s32[]{:T(128)S(6)} %select_n.64), kind=kLoop, calls=%fused_computation.26 | loop fusion | bytes 6291468 | tf_op jit(solution)/shard_map/dynamic_slice | solution.py:299
  9.9 1.3 constant_dynamic-slice_fusion.4
  11.2 2.8 %collective-permute-done = bf16[256,512]{1,0:T(8,128)(2,1)S(1)} collective-permute-done((bf16[256,512]{1,0:T(8,128)(2,1)S(1)}, bf16[256,512]{1,0:T(8,128)(2,1)S(1)}, u32[]{:S(2)}, u32[]{:S(2)}) %collective-permute-start) | collective-permute-done | bytes 262176 | tf_op jit(solution)/shard_map/ppermute | solution.py:248
  13.9 3.9 %collective-permute-done.2 = bf16[256,512]{1,0:T(8,128)(2,1)S(1)} collective-permute-done((bf16[256,512]{1,0:T(8,128)(2,1)S(1)}, bf16[256,512]{1,0:T(8,128)(2,1)S(1)}, u32[]{:S(2)}, u32[]{:S(2)}) %collective-permute-start.2) | collective-permute-done | bytes 262176 | tf_op jit(solution)/shard_map/ppermute | solution.py:248
  17.9 1.1 pad_maximum_fusion.1.kv_even
  19.0 0.1 copy.10.seg_query
  19.2 1.7 collective-permute-start.5
  20.9 1.5 collective-permute-start.6
  22.4 1.2 copy-done.5
  23.6 1.2 copy-done.6
  24.9 16.6 %attention.1 = (bf16[2,2,256,512]{3,2,1,0:T(8,128)(2,1)S(1)}, bf16[4,256,512]{2,1,0:T(8,128)(2,1)S(1)}, bf16[4,256,512]{2,1,0:T(8,128)(2,1)}) custom-call(s32[1]{0:T(128)} %bitcast.4.me_ref, s32[2,128,1]{2,1,0:T(8,128)S(1)} %copy.10.seg_query, s32[16,1,128]{2,1,0:T(1,128)S(1)} %bitcast.29, bf16[256,2048]{1,0:T(8,128)(2,1)S(1)} %copy-done.5, ...), custom_call_target="tpu_custom_call" | custom-call | flops 3400000000 | bytes 8000000 | tf_op jit(solution)/shard_map/attention/pallas_call | solution.py:135
  41.4 1.0 copy-done
  42.4 1.0 dynamic-slice_bitcast_fusion
  43.4 0.5 collective-permute-start.4
  44.0 2.2 %collective-permute-done.4 = bf16[2,256,512]{2,1,0:T(8,128)(2,1)} collective-permute-done((bf16[2,256,512]{2,1,0:T(8,128)(2,1)}, bf16[2,256,512]{2,1,0:T(8,128)(2,1)}, u32[]{:S(2)}, u32[]{:S(2)}) %collective-permute-start.4) | collective-permute-done | bytes 524320 | tf_op jit(solution)/shard_map/ppermute | solution.py:248
  46.2 1.3 fusion.1
  47.5 1.3 collective-permute-start.9
  48.8 1.5 collective-permute-start.7
  50.3 1.3 pad_maximum_fusion
  51.6 1.6 add_convert_fusion.3
  53.2 8.3 %collective-permute-done.9 = bf16[2,256,512]{2,1,0:T(8,128)(2,1)S(1)} collective-permute-done((bf16[2,256,512]{2,1,0:T(8,128)(2,1)S(1)}, bf16[2,256,512]{2,1,0:T(8,128)(2,1)S(1)}, u32[]{:S(2)}, u32[]{:S(2)}) %collective-permute-start.9) | collective-permute-done | bytes 524320 | tf_op jit(solution)/shard_map/ppermute | solution.py:248
  61.5 1.1 pad_maximum_fusion.2
  62.6 0.8 copy-done.2
  63.4 1.3 collective-permute-start.10
  64.6 1.5 collective-permute-start.11
  66.1 1.6 collective-permute-start.13
  67.7 2.3 %collective-permute-start.12 = (bf16[1024,512]{1,0:T(8,128)(2,1)}, bf16[1024,512]{1,0:T(8,128)(2,1)}, u32[]{:S(2)}, u32[]{:S(2)}) collective-permute-start(bf16[1024,512]{1,0:T(8,128)(2,1)} %bitcast.13.refs_9_), channel_id=1, source_target_pairs={{1,0},{2,1},{3,2},{0,3},{5,4},{6,5},{7,6},{4,7},{9,8},{10,9},{11,1... | collective-permute-start | bytes 3145736 | tf_op jit(solution)/shard_map/ppermute | solution.py:253
  70.0 17.9 %collective-permute-done.10.refs_4_ = bf16[256,2048]{1,0:T(8,128)(2,1)} collective-permute-done((bf16[256,2048]{1,0:T(8,128)(2,1)S(1)}, bf16[256,2048]{1,0:T(8,128)(2,1)}, u32[]{:S(2)}, u32[]{:S(2)}) %collective-permute-start.10) | collective-permute-done | bytes 1048608 | tf_op jit(solution)/shard_map/ppermute | solution.py:248
  87.8 1.3 collective-permute-start.14
  89.1 0.8 slice.27
  90.0 1.5 collective-permute-start.17
  91.5 0.6 slice.23.last_ref.slot_ref
  92.1 0.6 gather_fusion
  92.7 9.4 %collective-permute-done.17 = bf16[2,256,512]{2,1,0:T(8,128)(2,1)} collective-permute-done((bf16[2,256,512]{2,1,0:T(8,128)(2,1)}, bf16[2,256,512]{2,1,0:T(8,128)(2,1)}, u32[]{:S(2)}, u32[]{:S(2)}) %collective-permute-start.17) | collective-permute-done | bytes 524320 | tf_op jit(solution)/shard_map/ppermute | solution.py:248
  102.1 1.3 add_convert_fusion.4
  103.4 0.9 collective-permute-start.18
  104.4 9.6 %collective-permute-done.12.refs_10_ = bf16[1024,512]{1,0:T(8,128)(2,1)} collective-permute-done((bf16[1024,512]{1,0:T(8,128)(2,1)}, bf16[1024,512]{1,0:T(8,128)(2,1)}, u32[]{:S(2)}, u32[]{:S(2)}) %collective-permute-start.12) | collective-permute-done | bytes 1048608 | tf_op jit(solution)/shard_map/ppermute | solution.py:253
  114.0 1.1 slice.24
  115.1 1.1 slice.25
  116.2 1.2 collective-permute-start.16
  117.4 2.7 %collective-permute-start.15 = (bf16[512,512]{1,0:T(8,128)(2,1)S(1)}, bf16[512,512]{1,0:T(8,128)(2,1)S(1)}, u32[]{:S(2)}, u32[]{:S(2)}) collective-permute-start(bf16[512,512]{1,0:T(8,128)(2,1)S(1)} %slice.24), channel_id=1, source_target_pairs={{1,0},{2,1},{3,2},{0,3},{5,4},{6,5},{7,6},{4,7},{9,8},{10,9},{11,1... | collective-permute-start | bytes 1572872 | tf_op jit(solution)/shard_map/ppermute | solution.py:253
  120.1 4.7 %collective-permute-done.14.refs_8_ = bf16[256,2048]{1,0:T(8,128)(2,1)} collective-permute-done((bf16[256,2048]{1,0:T(8,128)(2,1)}, bf16[256,2048]{1,0:T(8,128)(2,1)}, u32[]{:S(2)}, u32[]{:S(2)}) %collective-permute-start.14) | collective-permute-done | bytes 1048608 | tf_op jit(solution)/shard_map/ppermute | solution.py:248
  124.7 12.0 %project.2 = (bf16[256,2048]{1,0:T(8,128)(2,1)S(1)}, bf16[256,2048]{1,0:T(8,128)(2,1)S(1)}, bf16[256,2048]{1,0:T(8,128)(2,1)S(1)}, bf16[256,2048]{1,0:T(8,128)(2,1)S(1)}) custom-call(s32[1]{0:T(128)} %slice.23.last_ref.slot_ref, s32[3]{0:T(128)S(1)} %gather_fusion, bf16[256,2048]{1,0:T(8,128)(2,1)S(1)} %get-tuple-element.45.refs_0_, ...), custom_call_target="tpu_custom_call" | custom-call | flops 6442450944 | bytes 10485760 | tf_op jit(solution)/shard_map/project/pallas_call | solution.py:207
  136.8 5.4 %collective-permute-done.15.refs_9_ = bf16[512,512]{1,0:T(8,128)(2,1)S(1)} collective-permute-done((bf16[512,512]{1,0:T(8,128)(2,1)S(1)}, bf16[512,512]{1,0:T(8,128)(2,1)S(1)}, u32[]{:S(2)}, u32[]{:S(2)}) %collective-permute-start.15) | collective-permute-done | bytes 524320 | tf_op jit(solution)/shard_map/ppermute | solution.py:253
  142.2 7.3 %project.3 = (bf16[256,2048]{1,0:T(8,128)(2,1)S(1)}, bf16[256,2048]{1,0:T(8,128)(2,1)S(1)}, bf16[256,2048]{1,0:T(8,128)(2,1)S(1)}, bf16[256,2048]{1,0:T(8,128)(2,1)S(1)}) custom-call(s32[1]{0:T(128)} %slice.23.last_ref.slot_ref, s32[1]{0:T(128)} %slice.23.last_ref.slot_ref, bf16[256,2048]{1,0:T(8,128)(2,1)S(1)} %get-tuple-element.45.refs_0_, ...), custom_call_target="tpu_custom_call" | custom-call | flops 2147483648 | bytes 6291456 | tf_op jit(solution)/shard_map/project/pallas_call | solution.py:207
  149.5 0.1 collective-permute-start.23
  149.6 0.5 collective-permute-start.19
  150.1 2.1 %collective-permute-done.23 = bf16[256,2048]{1,0:T(8,128)(2,1)S(1)} collective-permute-done((bf16[256,2048]{1,0:T(8,128)(2,1)S(1)}, bf16[256,2048]{1,0:T(8,128)(2,1)S(1)}, u32[]{:S(2)}, u32[]{:S(2)}) %collective-permute-start.23) | collective-permute-done | bytes 1048608 | tf_op jit(solution)/shard_map/ppermute | solution.py:248
  152.2 0.4 add_convert_fusion.1
  152.6 0.6 collective-permute-start.24
  153.2 0.1 fusion.4.refs_0_
  153.3 0.4 collective-permute-start.22
  153.7 2.3 %collective-permute-start.21 = (bf16[256,512]{1,0:T(8,128)(2,1)S(1)}, bf16[256,512]{1,0:T(8,128)(2,1)S(1)}, u32[]{:S(2)}, u32[]{:S(2)}) collective-permute-start(bf16[256,512]{1,0:T(8,128)(2,1)S(1)} %fusion.4.refs_0_), channel_id=1, source_target_pairs={{2,0},{3,1},{0,2},{1,3},{6,4},{7,5},{4,6},{5,7},{10,8},{11,9},{8,1... | collective-permute-start | bytes 786440 | tf_op jit(solution)/shard_map/ppermute | solution.py:253
  156.0 1.2 collective-permute-start.20
  157.2 0.4 add_convert_fusion.2
  157.6 6.8 %collective-permute-done.22.refs_3_ = bf16[256,512]{1,0:T(8,128)(2,1)S(1)} collective-permute-done((bf16[256,512]{1,0:T(8,128)(2,1)S(1)}, bf16[256,512]{1,0:T(8,128)(2,1)S(1)}, u32[]{:S(2)}, u32[]{:S(2)}) %collective-permute-start.22) | collective-permute-done | bytes 262176 | tf_op jit(solution)/shard_map/ppermute | solution.py:253
  164.4 10.2 %collective-permute-done.21.refs_2_ = bf16[256,512]{1,0:T(8,128)(2,1)S(1)} collective-permute-done((bf16[256,512]{1,0:T(8,128)(2,1)S(1)}, bf16[256,512]{1,0:T(8,128)(2,1)S(1)}, u32[]{:S(2)}, u32[]{:S(2)}) %collective-permute-start.21) | collective-permute-done | bytes 262176 | tf_op jit(solution)/shard_map/ppermute | solution.py:253
  174.7 0.7 copy-done.11
  175.4 0.7 copy-done.12
  176.1 2.3 %by_column.1 = (bf16[256,1024]{1,0:T(8,128)(2,1)}, bf16[256,1024]{1,0:T(8,128)(2,1)}) custom-call(s32[1]{0:T(128)} %bitcast.16.col_ref, bf16[256,512]{1,0:T(8,128)(2,1)} %copy-done.8, bf16[256,512]{1,0:T(8,128)(2,1)} %copy-done.12, bf16[256,512]{1,0:T(8,128)(2,1)} %copy-done.11, bf16[256,512]{1,0:T(8,128)(2,1)} %copy-done.10), custom_call_target="tpu_custom_call" | custom-call | tf_op jit(solution)/shard_map/by_column/pallas_call | solution.py:237
  178.4 1.4 add_convert_fusion
  (44 shorter events, 0.2 us)
Async XLA Ops:
  1.7 9.5 %collective-permute-start.1 = (bf16[256,512]{1,0:T(8,128)(2,1)S(1)}, bf16[256,512]{1,0:T(8,128)(2,1)S(1)}, u32[]{:S(2)}, u32[]{:S(2)}) collective-permute-start(bf16[256,512]{1,0:T(8,128)(2,1)S(1)} %get-tuple-element.101), channel_id=1, source_target_pairs={{0,16},{4,20},{8,24},{12,28},{16,0},{20,4},{24,8},{28,12},{1,17},{... | collective-permute-start | bytes 786440 | tf_op jit(solution)/shard_map/ppermute | solution.py:248
  4.7 9.2 %collective-permute-start = (bf16[256,512]{1,0:T(8,128)(2,1)S(1)}, bf16[256,512]{1,0:T(8,128)(2,1)S(1)}, u32[]{:S(2)}, u32[]{:S(2)}) collective-permute-start(bf16[256,512]{1,0:T(8,128)(2,1)S(1)} %get-tuple-element.101), channel_id=1, source_target_pairs={{0,8},{4,12},{8,0},{12,4},{16,24},{20,28},{24,16},{28,20},{1,9},{5... | collective-permute-start | bytes 786440 | tf_op jit(solution)/shard_map/ppermute | solution.py:248
  6.2 11.7 %collective-permute-start.2 = (bf16[256,512]{1,0:T(8,128)(2,1)S(1)}, bf16[256,512]{1,0:T(8,128)(2,1)S(1)}, u32[]{:S(2)}, u32[]{:S(2)}) collective-permute-start(bf16[256,512]{1,0:T(8,128)(2,1)S(1)} %get-tuple-element.101), channel_id=1, source_target_pairs={{0,24},{4,28},{8,16},{12,20},{16,8},{20,12},{24,0},{28,4},{1,25},{... | collective-permute-start | bytes 786440 | tf_op jit(solution)/shard_map/ppermute | solution.py:248
  9.9 9.2 %copy-start.4 = (s32[2048]{0:T(1024)S(1)}, s32[2048]{0:T(1024)}, u32[]{:S(2)}) copy-start(s32[2048]{0:T(1024)} %param.11) | copy-start | bytes 24580
  19.0 3.4 %collective-permute-start.3 = (bf16[4,256,512]{2,1,0:T(8,128)(2,1)}, bf16[4,256,512]{2,1,0:T(8,128)(2,1)}, u32[]{:S(2)}, u32[]{:S(2)}) collective-permute-start(bf16[4,256,512]{2,1,0:T(8,128)(2,1)} %pad_maximum_fusion.1.kv_even), channel_id=1, source_target_pairs={{0,4},{4,0},{8,12},{12,8},{16,20},{20,16},{24,28},{28,24},{1,5},{5... | collective-permute-start | bytes 3145736 | tf_op jit(solution)/shard_map/ppermute | solution.py:248
  19.2 28.3 %collective-permute-start.5 = (bf16[256,2048]{1,0:T(8,128)(2,1)}, bf16[256,2048]{1,0:T(8,128)(2,1)S(1)}, u32[]{:S(2)}, u32[]{:S(2)}) collective-permute-start(bf16[256,2048]{1,0:T(8,128)(2,1)} %get-tuple-element.49), channel_id=1, source_target_pairs={{0,8},{4,12},{8,0},{12,4},{16,24},{20,28},{24,16},{28,20},{1,9},{5... | collective-permute-start | bytes 3145736 | tf_op jit(solution)/shard_map/ppermute | solution.py:248
  20.9 26.6 %collective-permute-start.6 = (bf16[256,2048]{1,0:T(8,128)(2,1)S(1)}, bf16[256,2048]{1,0:T(8,128)(2,1)}, u32[]{:S(2)}, u32[]{:S(2)}) collective-permute-start(bf16[256,2048]{1,0:T(8,128)(2,1)S(1)} %get-tuple-element.45.refs_0_), channel_id=1, source_target_pairs={{0,16},{4,20},{8,24},{12,28},{16,0},{20,4},{24,8},{28,12},{1,17},{... | collective-permute-start | bytes 3145736 | tf_op jit(solution)/shard_map/ppermute | solution.py:248
  22.4 1.2 copy-start.5
  23.6 1.2 copy-start.6
  41.4 1.0 copy-start
  42.4 9.2 %collective-permute-start.8 = (bf16[4,256,512]{2,1,0:T(8,128)(2,1)}, bf16[4,256,512]{2,1,0:T(8,128)(2,1)}, u32[]{:S(2)}, u32[]{:S(2)}) collective-permute-start(bf16[4,256,512]{2,1,0:T(8,128)(2,1)} %get-tuple-element.56), channel_id=1, source_target_pairs={{0,4},{4,0},{8,12},{12,8},{16,20},{20,16},{24,28},{28,24},{1,5},{5... | collective-permute-start | bytes 3145736 | tf_op jit(solution)/shard_map/ppermute | solution.py:248
  43.4 2.7 %collective-permute-start.4 = (bf16[2,256,512]{2,1,0:T(8,128)(2,1)}, bf16[2,256,512]{2,1,0:T(8,128)(2,1)}, u32[]{:S(2)}, u32[]{:S(2)}) collective-permute-start(bf16[2,256,512]{2,1,0:T(8,128)(2,1)} %get-tuple-element.94), channel_id=1, source_target_pairs={{0,4},{4,0},{8,12},{12,8},{16,20},{20,16},{24,28},{28,24},{1,5},{5... | collective-permute-start | bytes 1572872 | tf_op jit(solution)/shard_map/ppermute | solution.py:248
  47.4 4.2 %copy-start.1 = (bf16[4,256,512]{2,1,0:T(8,128)(2,1)S(1)}, bf16[4,256,512]{2,1,0:T(8,128)(2,1)}, u32[]{:S(2)}) copy-start(bf16[4,256,512]{2,1,0:T(8,128)(2,1)} %copy-done) | copy-start | bytes 3145732
  47.5 14.0 %collective-permute-start.9 = (bf16[2,256,512]{2,1,0:T(8,128)(2,1)S(1)}, bf16[2,256,512]{2,1,0:T(8,128)(2,1)S(1)}, u32[]{:S(2)}, u32[]{:S(2)}) collective-permute-start(bf16[2,256,512]{2,1,0:T(8,128)(2,1)S(1)} %get-tuple-element.57), channel_id=1, source_target_pairs={{0,8},{4,12},{8,0},{12,4},{16,24},{20,28},{24,16},{28,20},{1,9},{5... | collective-permute-start | bytes 1572872 | tf_op jit(solution)/shard_map/ppermute | solution.py:248
  48.8 13.8 %collective-permute-start.7 = (bf16[128,2048]{1,0:T(8,128)(2,1)S(1)}, bf16[128,2048]{1,0:T(8,128)(2,1)S(1)}, u32[]{:S(2)}, u32[]{:S(2)}) collective-permute-start(bf16[128,2048]{1,0:T(8,128)(2,1)S(1)} %get-tuple-element.51.refs_1_), channel_id=1, source_target_pairs={{0,16},{4,20},{8,24},{12,28},{16,0},{20,4},{24,8},{28,12},{1,17},{... | collective-permute-start | bytes 1572872 | tf_op jit(solution)/shard_map/ppermute | solution.py:248
  51.6 11.8 %copy-start.9 = (bf16[256,2048]{1,0:T(8,128)(2,1)S(1)}, bf16[256,2048]{1,0:T(8,128)(2,1)}, u32[]{:S(2)}) copy-start(bf16[256,2048]{1,0:T(8,128)(2,1)} %get-tuple-element.58) | copy-start | bytes 3145732
  53.2 38.8 %copy-start.7 = (bf16[4,256,512]{2,1,0:T(8,128)(2,1)}, bf16[4,256,512]{2,1,0:T(8,128)(2,1)S(1)}, u32[]{:S(2)}) copy-start(bf16[4,256,512]{2,1,0:T(8,128)(2,1)S(1)} %add_convert_fusion.3) | copy-start | bytes 3145732
  53.2 38.8 %copy-start.13 = (s32[3]{0:T(128)S(1)}, s32[3]{0:T(128)}, u32[]{:S(2)}) copy-start(s32[3]{0:T(128)} %constant.89) | copy-start | bytes 40
  62.6 0.8 copy-start.2
  63.4 24.5 %collective-permute-start.10 = (bf16[256,2048]{1,0:T(8,128)(2,1)S(1)}, bf16[256,2048]{1,0:T(8,128)(2,1)}, u32[]{:S(2)}, u32[]{:S(2)}) collective-permute-start(bf16[256,2048]{1,0:T(8,128)(2,1)S(1)} %copy-done.9), channel_id=1, source_target_pairs={{0,8},{4,12},{8,0},{12,4},{16,24},{20,28},{24,16},{28,20},{1,9},{5... | collective-permute-start | bytes 3145736 | tf_op jit(solution)/shard_map/ppermute | solution.py:248
  64.6 49.4 %collective-permute-start.11 = (bf16[384,2048]{1,0:T(8,128)(2,1)}, bf16[384,2048]{1,0:T(8,128)(2,1)}, u32[]{:S(2)}, u32[]{:S(2)}) collective-permute-start(bf16[384,2048]{1,0:T(8,128)(2,1)} %pad_maximum_fusion), channel_id=1, source_target_pairs={{0,16},{4,20},{8,24},{12,28},{16,0},{20,4},{24,8},{28,12},{1,17},{... | collective-permute-start | bytes 4718600 | tf_op jit(solution)/shard_map/ppermute | solution.py:248
  66.1 38.2 %collective-permute-start.13 = (bf16[1024,512]{1,0:T(8,128)(2,1)}, bf16[1024,512]{1,0:T(8,128)(2,1)}, u32[]{:S(2)}, u32[]{:S(2)}) collective-permute-start(bf16[1024,512]{1,0:T(8,128)(2,1)} %bitcast.13.refs_9_), channel_id=1, source_target_pairs={{3,0},{0,1},{1,2},{2,3},{7,4},{4,5},{5,6},{6,7},{11,8},{8,9},{9,10... | collective-permute-start | bytes 3145736 | tf_op jit(solution)/shard_map/ppermute | solution.py:253
  67.7 46.3 %collective-permute-start.12 = (bf16[1024,512]{1,0:T(8,128)(2,1)}, bf16[1024,512]{1,0:T(8,128)(2,1)}, u32[]{:S(2)}, u32[]{:S(2)}) collective-permute-start(bf16[1024,512]{1,0:T(8,128)(2,1)} %bitcast.13.refs_9_), channel_id=1, source_target_pairs={{1,0},{2,1},{3,2},{0,3},{5,4},{6,5},{7,6},{4,7},{9,8},{10,9},{11,1... | collective-permute-start | bytes 3145736 | tf_op jit(solution)/shard_map/ppermute | solution.py:253
  87.8 36.9 %collective-permute-start.14 = (bf16[256,2048]{1,0:T(8,128)(2,1)}, bf16[256,2048]{1,0:T(8,128)(2,1)}, u32[]{:S(2)}, u32[]{:S(2)}) collective-permute-start(bf16[256,2048]{1,0:T(8,128)(2,1)} %collective-permute-done.10.refs_4_), channel_id=1, source_target_pairs={{0,16},{4,20},{8,24},{12,28},{16,0},{20,4},{24,8},{28,12},{1,17},{... | collective-permute-start | bytes 3145736 | tf_op jit(solution)/shard_map/ppermute | solution.py:248
  90.0 12.1 %collective-permute-start.17 = (bf16[2,256,512]{2,1,0:T(8,128)(2,1)}, bf16[2,256,512]{2,1,0:T(8,128)(2,1)}, u32[]{:S(2)}, u32[]{:S(2)}) collective-permute-start(bf16[2,256,512]{2,1,0:T(8,128)(2,1)} %slice.27), channel_id=1, source_target_pairs={{0,8},{4,12},{8,0},{12,4},{16,24},{20,28},{24,16},{28,20},{1,9},{5... | collective-permute-start | bytes 1572872 | tf_op jit(solution)/shard_map/ppermute | solution.py:248
  92.7 32.0 %copy-start.3 = (bf16[128,2048]{1,0:T(8,128)(2,1)S(1)}, bf16[128,2048]{1,0:T(8,128)(2,1)}, u32[]{:S(2)}) copy-start(bf16[128,2048]{1,0:T(8,128)(2,1)} %copy-done.2) | copy-start | bytes 1572868
  103.4 33.3 %collective-permute-start.18 = (bf16[256,512]{1,0:T(8,128)(2,1)S(1)}, bf16[256,512]{1,0:T(8,128)(2,1)S(1)}, u32[]{:S(2)}, u32[]{:S(2)}) collective-permute-start(bf16[256,512]{1,0:T(8,128)(2,1)S(1)} %slice_bitcast_fusion.1), channel_id=1, source_target_pairs={{0,16},{4,20},{8,24},{12,28},{16,0},{20,4},{24,8},{28,12},{1,17},{... | collective-permute-start | bytes 786440 | tf_op jit(solution)/shard_map/ppermute | solution.py:248
  116.2 20.6 %collective-permute-start.16 = (bf16[512,512]{1,0:T(8,128)(2,1)S(1)}, bf16[512,512]{1,0:T(8,128)(2,1)S(1)}, u32[]{:S(2)}, u32[]{:S(2)}) collective-permute-start(bf16[512,512]{1,0:T(8,128)(2,1)S(1)} %slice.25), channel_id=1, source_target_pairs={{3,0},{0,1},{1,2},{2,3},{7,4},{4,5},{5,6},{6,7},{11,8},{8,9},{9,10... | collective-permute-start | bytes 1572872 | tf_op jit(solution)/shard_map/ppermute | solution.py:253
  117.4 24.8 %collective-permute-start.15 = (bf16[512,512]{1,0:T(8,128)(2,1)S(1)}, bf16[512,512]{1,0:T(8,128)(2,1)S(1)}, u32[]{:S(2)}, u32[]{:S(2)}) collective-permute-start(bf16[512,512]{1,0:T(8,128)(2,1)S(1)} %slice.24), channel_id=1, source_target_pairs={{1,0},{2,1},{3,2},{0,3},{5,4},{6,5},{7,6},{4,7},{9,8},{10,9},{11,1... | collective-permute-start | bytes 1572872 | tf_op jit(solution)/shard_map/ppermute | solution.py:253
  149.5 2.7 %collective-permute-start.23 = (bf16[256,2048]{1,0:T(8,128)(2,1)S(1)}, bf16[256,2048]{1,0:T(8,128)(2,1)S(1)}, u32[]{:S(2)}, u32[]{:S(2)}) collective-permute-start(bf16[256,2048]{1,0:T(8,128)(2,1)S(1)} %get-tuple-element.80), channel_id=1, source_target_pairs={{0,4},{4,0},{8,12},{12,8},{16,20},{20,16},{24,28},{28,24},{1,5},{5... | collective-permute-start | bytes 3145736 | tf_op jit(solution)/shard_map/ppermute | solution.py:248
  149.6 7.6 %collective-permute-start.19 = (bf16[256,2048]{1,0:T(8,128)(2,1)S(1)}, bf16[256,2048]{1,0:T(8,128)(2,1)S(1)}, u32[]{:S(2)}, u32[]{:S(2)}) collective-permute-start(bf16[256,2048]{1,0:T(8,128)(2,1)S(1)} %get-tuple-element.76), channel_id=1, source_target_pairs={{0,4},{4,0},{8,12},{12,8},{16,20},{20,16},{24,28},{28,24},{1,5},{5... | collective-permute-start | bytes 3145736 | tf_op jit(solution)/shard_map/ppermute | solution.py:248
  152.6 25.8 %collective-permute-start.24 = (bf16[256,2048]{1,0:T(8,128)(2,1)S(1)}, bf16[256,2048]{1,0:T(8,128)(2,1)S(1)}, u32[]{:S(2)}, u32[]{:S(2)}) collective-permute-start(bf16[256,2048]{1,0:T(8,128)(2,1)S(1)} %add_convert_fusion.1), channel_id=1, source_target_pairs={{0,8},{4,12},{8,0},{12,4},{16,24},{20,28},{24,16},{28,20},{1,9},{5... | collective-permute-start | bytes 3145736 | tf_op jit(solution)/shard_map/ppermute | solution.py:248
  153.3 22.8 %copy-start.8 = (bf16[256,512]{1,0:T(8,128)(2,1)}, bf16[256,512]{1,0:T(8,128)(2,1)S(1)}, u32[]{:S(2)}) copy-start(bf16[256,512]{1,0:T(8,128)(2,1)S(1)} %fusion.4.refs_0_) | copy-start | bytes 786436
  153.3 11.1 %collective-permute-start.22 = (bf16[256,512]{1,0:T(8,128)(2,1)S(1)}, bf16[256,512]{1,0:T(8,128)(2,1)S(1)}, u32[]{:S(2)}, u32[]{:S(2)}) collective-permute-start(bf16[256,512]{1,0:T(8,128)(2,1)S(1)} %fusion.4.refs_0_), channel_id=1, source_target_pairs={{3,0},{0,1},{1,2},{2,3},{7,4},{4,5},{5,6},{6,7},{11,8},{8,9},{9,10... | collective-permute-start | bytes 786440 | tf_op jit(solution)/shard_map/ppermute | solution.py:253
  153.7 20.9 %collective-permute-start.21 = (bf16[256,512]{1,0:T(8,128)(2,1)S(1)}, bf16[256,512]{1,0:T(8,128)(2,1)S(1)}, u32[]{:S(2)}, u32[]{:S(2)}) collective-permute-start(bf16[256,512]{1,0:T(8,128)(2,1)S(1)} %fusion.4.refs_0_), channel_id=1, source_target_pairs={{2,0},{3,1},{0,2},{1,3},{6,4},{7,5},{4,6},{5,7},{10,8},{11,9},{8,1... | collective-permute-start | bytes 786440 | tf_op jit(solution)/shard_map/ppermute | solution.py:253
  156.0 18.6 %collective-permute-start.20 = (bf16[256,512]{1,0:T(8,128)(2,1)S(1)}, bf16[256,512]{1,0:T(8,128)(2,1)S(1)}, u32[]{:S(2)}, u32[]{:S(2)}) collective-permute-start(bf16[256,512]{1,0:T(8,128)(2,1)S(1)} %fusion.4.refs_0_), channel_id=1, source_target_pairs={{1,0},{2,1},{3,2},{0,3},{5,4},{6,5},{7,6},{4,7},{9,8},{10,9},{11,1... | collective-permute-start | bytes 786440 | tf_op jit(solution)/shard_map/ppermute | solution.py:253
  164.4 10.2 %copy-start.10 = (bf16[256,512]{1,0:T(8,128)(2,1)}, bf16[256,512]{1,0:T(8,128)(2,1)S(1)}, u32[]{:S(2)}) copy-start(bf16[256,512]{1,0:T(8,128)(2,1)S(1)} %collective-permute-done.22.refs_3_) | copy-start | bytes 786436
  174.6 0.7 copy-start.11
  175.4 0.7 copy-start.12

commit v5 on v4

--- a/solution.py
+++ b/solution.py
@@ -160,55 +160,79 @@
     )(me, seg_query, seg_key, queries, grad_attn, kv_even, kv_odd)
 
 
-def project_kernel(pieces_here, weights, places, rest, last_ref, slot_ref, *refs):
+def gather_rows(places, sources, lhs, step, at):
+    depth = sources[0].shape[1]
+    for i, (source, first) in enumerate(places):
+        lhs[i * step:(i + 1) * step, pl.ds(at, depth)] = sources[source][first:first + step, :]
+
+
+def most_kernel(pieces_here, weights, places, last_ref, slot_ref, *refs):
     group = len(places[0])
-    outs, lhs = refs[-1 - group:-1], refs[-1]
-    pieces, sources = refs[:pieces_here], refs[pieces_here:-1 - group]
-    former = None
-    if rest:
-        sources, former = sources[:-group], sources[-group:]
+    outs, last_out, lhs = refs[-2 - group:-2], refs[-2], refs[-1]
+    pieces, sources = refs[:pieces_here], refs[pieces_here:-2 - group]
     step, features = outs[0].shape
     depth = sources[0].shape[1]
     last = last_ref[0]
     for k, place in enumerate(places):
         slot = slot_ref[k]
-        at = pl.multiple_of(0 if rest else jnp.where(slot > last, slot - 1, slot) * depth, depth)
-        for i in range(group):
-            source, first = place[i]
-            lhs[i * step:(i + 1) * step, pl.ds(at, depth)] = sources[source][first:first + step, :]
+        at = pl.multiple_of(jnp.where(slot > last, slot - 1, slot) * depth, depth)
+        gather_rows(place, sources, lhs, step, at)
     tile = min(256, features)
+
+    def joined(used, at):
+        return jnp.concatenate([pieces[i][first:first + size, at] for i, first, size in used], axis=0)
+
     for e in range(len(weights)):
-        used = weights[e] if rest else sum(weights[:e] + weights[e + 1:], [])
+        used = sum(weights[:e] + weights[e + 1:], [])
 
         @pl.when(last == e)
-        def _(used=used):
+        def _(e=e, used=used):
             def columns(n, carry):
                 at = pl.ds(pl.multiple_of(n * tile, tile), tile)
-                weight = [pieces[i][first:first + size, at] for i, first, size in used]
-                weight = jnp.concatenate(weight, axis=0)
+                last_out[:, at] = joined(weights[e], at)
+                weight = joined(used, at)
                 for i in range(group):
                     rows = slice(i * step, (i + 1) * step)
                     out = jnp.dot(lhs[rows, :], weight, preferred_element_type=jnp.float32)
-                    if former is not None:
-                        out += former[i][:, at].astype(jnp.float32)
                     outs[i][:, at] = out.astype(jnp.bfloat16)
                 return carry
 
             lax.fori_loop(0, features // tile, columns, 0)
 
 
-def project(last, slots, pieces, weights, sources, places, step, former=()):
+def rest_kernel(places, weight_ref, *refs):
+    group = len(places)
+    outs, lhs = refs[-1 - group:-1], refs[-1]
+    sources, former = refs[:-1 - 2 * group], refs[-1 - 2 * group:-1 - group]
+    step, features = outs[0].shape
+    gather_rows(places, sources, lhs, step, 0)
+    tile = min(256, features)
+
+    def columns(n, carry):
+        at = pl.ds(pl.multiple_of(n * tile, tile), tile)
+        weight = weight_ref[:, at]
+        for i in range(group):
+            rows = slice(i * step, (i + 1) * step)
+            out = jnp.dot(lhs[rows, :], weight, preferred_element_type=jnp.float32)
+            outs[i][:, at] = (out + former[i][:, at].astype(jnp.float32)).astype(jnp.bfloat16)
+        return carry
+
+    lax.fori_loop(0, features // tile, columns, 0)
+
+
+def project(last, slots, pieces, weights, sources, places, step):
     group = len(places[0])
     depth = sources[0].shape[1]
     features = pieces[0].shape[1]
     smem = pl.BlockSpec(memory_space=pltpu.SMEM)
     vmem = pl.BlockSpec(memory_space=pltpu.VMEM)
-    operands = [*pieces, *sources, *former]
+    operands = [*pieces, *sources]
     return pl.pallas_call(
-        functools.partial(project_kernel, len(pieces), weights, places, bool(former)),
-        out_shape=[jax.ShapeDtypeStruct((step, features), jnp.bfloat16)] * group,
+        functools.partial(most_kernel, len(pieces), weights, places),
+        out_shape=[jax.ShapeDtypeStruct((step, features), jnp.bfloat16)] * group
+        + [jax.ShapeDtypeStruct((depth, features), jnp.bfloat16)],
         in_specs=[smem, smem] + [vmem] * len(operands),
-        out_specs=[vmem] * group,
+        out_specs=[vmem] * (group + 1),
         scratch_shapes=[pltpu.VMEM((group * step, len(places) * depth), jnp.bfloat16)],
         compiler_params=pltpu.CompilerParams(vmem_limit_bytes=32 << 20),
         cost_estimate=pl.CostEstimate(
@@ -216,8 +240,29 @@
             bytes_accessed=2 * (group * step * features + len(places) * depth * features),
             transcendentals=0,
         ),
-        name="project",
+        name="project_most",
     )(last, slots, *operands)
+
+
+def project_rest(weight, sources, places, step, former):
+    depth, features = weight.shape
+    group = len(places)
+    vmem = pl.BlockSpec(memory_space=pltpu.VMEM)
+    operands = [*sources, *former]
+    return pl.pallas_call(
+        functools.partial(rest_kernel, places),
+        out_shape=[jax.ShapeDtypeStruct((step, features), jnp.bfloat16)] * group,
+        in_specs=[vmem] * (1 + len(operands)),
+        out_specs=[vmem] * group,
+        scratch_shapes=[pltpu.VMEM((group * step, depth), jnp.bfloat16)],
+        compiler_params=pltpu.CompilerParams(vmem_limit_bytes=32 << 20),
+        cost_estimate=pl.CostEstimate(
+            flops=2 * group * step * depth * features,
+            bytes_accessed=2 * (2 * group * step * features + depth * features),
+            transcendentals=0,
+        ),
+        name="project_rest",
+    )(weight, *operands)
 
 
 def columns_kernel(col_ref, *refs):
@@ -395,10 +440,10 @@
     slots = ((me >> 1) ^ ((col + jnp.arange(count)) % count)).astype(jnp.int32)
     devices = range(4)
     places = [[(k, d * rows) for d in devices] for k in range(3)]
-    most = project(slots[2:3], slots[jnp.array([0, 1, 3])], pieces, weights, [tokens, *near], places, rows)
+    *most, last_weight = project(slots[2:3], slots[jnp.array([0, 1, 3])], pieces, weights, [tokens, *near], places, rows)
     *most, dkv_y = tied(*most, dkv_y)
-    places = [[(d // 2, d % 2 * rows) for d in devices]]
-    zero, one, two, three = project(slots[2:3], slots[2:3], pieces, weights, far, places, rows, most)
+    places = [(d // 2, d % 2 * rows) for d in devices]
+    zero, one, two, three = project_rest(last_weight, far, places, rows, most)
     there = added(two, across(three, 1))
     found = across(one, 1)
     got = x(there)

time: 182 us -> 176 us (0.967)
  Pallas kernels: 38.2 us -> 34.6 us
  starting transfers between devices: 30.4 us -> 27.3 us
  other arithmetic: 9.98 us -> 7.99 us
    ppermute x18, waiting for transfers between devices: 51.3 us -> 56.7 us  [across(): return lax.ppermute(block, 'row', [(i, i ^ mask) for i in range(ranks)])]
    ppermute x7, waiting for transfers between devices: 32.1 us -> 27.7 us  [turned(): lax.ppermute(block, 'col', [((i + distance) % count, i) for i in range(co...]
    pallas_call x2, Pallas kernels: 19.3 us -> 15.8 us  [the longest x1 12.1 us: project(): pl.pallas_call(functools.partial(most_kernel, len(pieces), weights, place...]
    unnamed x28 -> x30, local copies, waits for them, and re-layouts: 5.67 us -> 6.09 us
  transfers between devices with their start and end apart: 25 -> 25, of which waited for: 12 -> 13; matrix products, arithmetic and copies ran while one was open for 10% -> 10% of each run, Pallas kernels for 17% -> 18%
where the time goes in v5:
time: 176 us; the launch traced here: 173 us
  waiting for transfers between devices  84.4 us (48%)
  Pallas kernels  34.6 us (20%)
  starting transfers between devices  27.3 us (16%)
  local copies, waits for them, and re-layouts  17.4 us (10%)
  other arithmetic  7.99 us (5%)
    ppermute x18, waiting for transfers between devices, across(): return lax.ppermute(block, 'row', [(i, i ^ mask) for i in range(ranks)])  56.7 us
    ppermute x7, waiting for transfers between devices, turned(): lax.ppermute(block, 'col', [((i + distance) % count, i) for i in range(co...  27.7 us
    ppermute x18, starting transfers between devices, across(): return lax.ppermute(block, 'row', [(i, i ^ mask) for i in range(ranks)])  17 us
    pallas_call x1, Pallas kernels, attention(): pl.pallas_call(functools.partial(attention_kernel, per_kv, rows, ranks),...  16.4 us
    pallas_call x1, Pallas kernels, project(): pl.pallas_call(functools.partial(most_kernel, len(pieces), weights, place...  12.1 us
    ppermute x7, starting transfers between devices, turned(): lax.ppermute(block, 'col', [((i + distance) % count, i) for i in range(co...  10.3 us
    unnamed x30, local copies, waits for them, and re-layouts  6.09 us
    convert_element_type x6, other arithmetic, added(): (one.astype(jnp.float32) + two.astype(jnp.float32)).astype(jnp.bfloat16)  5.14 us
  transfers between devices with their start and end apart: 25, of which 13 were waited for; matrix products, arithmetic and copies ran while one was open for 10% of the time, Pallas kernels for 18%

profile of v5, /device:TPU:0, one launch (start us, length us, event | category | flops | bytes accessed | tf_op | source)
XLA Modules:
  0.0 172.5 jit_solution(17809131509530770519)
XLA Ops:
  0.7 1.0 constant_dynamic-slice_fusion.9
  1.7 3.0 %collective-permute-start.1 = (bf16[256,512]{1,0:T(8,128)(2,1)S(1)}, bf16[256,512]{1,0:T(8,128)(2,1)S(1)}, u32[]{:S(2)}, u32[]{:S(2)}) collective-permute-start(bf16[256,512]{1,0:T(8,128)(2,1)S(1)} %get-tuple-element.103), channel_id=1, source_target_pairs={{0,16},{4,20},{8,24},{12,28},{16,0},{20,4},{24,8},{28,12},{1,17},{... | collective-permute-start | bytes 786440 | tf_op jit(solution)/shard_map/ppermute | solution.py:293
  4.7 1.5 collective-permute-start
  6.2 3.6 %constant_dynamic-slice_fusion.2 = (bf16[256,2048]{1,0:T(8,128)(2,1)}, bf16[256,2048]{1,0:T(8,128)(2,1)}, bf16[256,2048]{1,0:T(8,128)(2,1)}) fusion(bf16[1024,2048]{1,0:T(8,128)(2,1)} %param.12, s32[]{:T(128)S(6)} %select_n.66, s32[]{:T(128)S(6)} %select_n.62, s32[]{:T(128)S(6)} %select_n.65), kind=kLoop, calls=%fused_computation.26 | loop fusion | bytes 6291468 | tf_op jit(solution)/shard_map/dynamic_slice | solution.py:344
  9.9 1.3 constant_dynamic-slice_fusion.4
  11.2 2.7 %collective-permute-done = bf16[256,512]{1,0:T(8,128)(2,1)S(1)} collective-permute-done((bf16[256,512]{1,0:T(8,128)(2,1)S(1)}, bf16[256,512]{1,0:T(8,128)(2,1)S(1)}, u32[]{:S(2)}, u32[]{:S(2)}) %collective-permute-start) | collective-permute-done | bytes 262176 | tf_op jit(solution)/shard_map/ppermute | solution.py:293
  13.9 3.9 %collective-permute-done.2 = bf16[256,512]{1,0:T(8,128)(2,1)S(1)} collective-permute-done((bf16[256,512]{1,0:T(8,128)(2,1)S(1)}, bf16[256,512]{1,0:T(8,128)(2,1)S(1)}, u32[]{:S(2)}, u32[]{:S(2)}) %collective-permute-start.2) | collective-permute-done | bytes 262176 | tf_op jit(solution)/shard_map/ppermute | solution.py:293
  17.9 0.1 pad_maximum_fusion.1.kv_even
  18.0 0.1 collective-permute-start.3
  18.1 1.0 copy-done
  19.1 0.1 copy.10.seg_query
  19.3 1.7 collective-permute-start.5
  21.0 1.5 collective-permute-start.6
  22.5 1.2 copy-done.1
  23.7 1.2 copy-done.4
  24.9 1.2 copy-done.5
  26.2 16.4 %attention.1 = (bf16[2,2,256,512]{3,2,1,0:T(8,128)(2,1)S(1)}, bf16[4,256,512]{2,1,0:T(8,128)(2,1)S(1)}, bf16[4,256,512]{2,1,0:T(8,128)(2,1)}) custom-call(s32[1]{0:T(128)} %bitcast.4.me_ref, s32[2,128,1]{2,1,0:T(8,128)S(1)} %copy.10.seg_query, s32[16,1,128]{2,1,0:T(1,128)S(1)} %bitcast.32, bf16[256,2048]{1,0:T(8,128)(2,1)S(1)} %copy-done.4, ...), custom_call_target="tpu_custom_call" | custom-call | flops 3400000000 | bytes 8000000 | tf_op jit(solution)/shard_map/attention/pallas_call | solution.py:135
  42.6 1.0 dynamic-slice_bitcast_fusion
  43.7 0.5 collective-permute-start.4
  44.2 2.2 %collective-permute-done.4 = bf16[2,256,512]{2,1,0:T(8,128)(2,1)} collective-permute-done((bf16[2,256,512]{2,1,0:T(8,128)(2,1)}, bf16[2,256,512]{2,1,0:T(8,128)(2,1)}, u32[]{:S(2)}, u32[]{:S(2)}) %collective-permute-start.4) | collective-permute-done | bytes 524320 | tf_op jit(solution)/shard_map/ppermute | solution.py:293
  46.4 1.3 fusion.1
  47.7 0.6 collective-permute-start.9
  48.3 1.0 collective-permute-start.7
  49.3 1.3 pad_maximum_fusion
  50.6 1.6 add_convert_fusion.3
  52.2 9.5 %collective-permute-done.9 = bf16[2,256,512]{2,1,0:T(8,128)(2,1)S(1)} collective-permute-done((bf16[2,256,512]{2,1,0:T(8,128)(2,1)S(1)}, bf16[2,256,512]{2,1,0:T(8,128)(2,1)S(1)}, u32[]{:S(2)}, u32[]{:S(2)}) %collective-permute-start.9) | collective-permute-done | bytes 524320 | tf_op jit(solution)/shard_map/ppermute | solution.py:293
  61.7 0.1 pad_maximum_fusion.2
  61.8 0.2 collective-permute-done.7.refs_6_
  62.0 1.5 collective-permute-start.10
  63.5 0.5 collective-permute-start.11
  64.0 1.6 collective-permute-start.13
  65.5 2.3 %collective-permute-start.12 = (bf16[1024,512]{1,0:T(8,128)(2,1)S(1)}, bf16[1024,512]{1,0:T(8,128)(2,1)}, u32[]{:S(2)}, u32[]{:S(2)}) collective-permute-start(bf16[1024,512]{1,0:T(8,128)(2,1)S(1)} %bitcast.29), channel_id=1, source_target_pairs={{1,0},{2,1},{3,2},{0,3},{5,4},{6,5},{7,6},{4,7},{9,8},{10,9},{11,1... | collective-permute-start | bytes 3145736 | tf_op jit(solution)/shard_map/ppermute | solution.py:298
  67.8 18.6 %collective-permute-done.10.refs_4_ = bf16[256,2048]{1,0:T(8,128)(2,1)} collective-permute-done((bf16[256,2048]{1,0:T(8,128)(2,1)S(1)}, bf16[256,2048]{1,0:T(8,128)(2,1)}, u32[]{:S(2)}, u32[]{:S(2)}) %collective-permute-start.10) | collective-permute-done | bytes 1048608 | tf_op jit(solution)/shard_map/ppermute | solution.py:293
  86.4 0.8 collective-permute-start.14
  87.1 0.8 slice.25
  88.0 1.0 collective-permute-start.17
  89.0 0.6 slice.21.last_ref
  89.6 0.6 gather_fusion
  90.2 9.7 %collective-permute-done.17 = bf16[2,256,512]{2,1,0:T(8,128)(2,1)} collective-permute-done((bf16[2,256,512]{2,1,0:T(8,128)(2,1)}, bf16[2,256,512]{2,1,0:T(8,128)(2,1)}, u32[]{:S(2)}, u32[]{:S(2)}) %collective-permute-start.17) | collective-permute-done | bytes 524320 | tf_op jit(solution)/shard_map/ppermute | solution.py:293
  99.9 1.3 add_convert_fusion.4
  101.3 1.6 collective-permute-start.18
  102.8 8.5 %collective-permute-done.12.refs_10_ = bf16[1024,512]{1,0:T(8,128)(2,1)} collective-permute-done((bf16[1024,512]{1,0:T(8,128)(2,1)S(1)}, bf16[1024,512]{1,0:T(8,128)(2,1)}, u32[]{:S(2)}, u32[]{:S(2)}) %collective-permute-start.12) | collective-permute-done | bytes 1048608 | tf_op jit(solution)/shard_map/ppermute | solution.py:298
  111.3 1.1 slice.23
  112.4 1.1 slice.22
  113.5 2.4 %collective-permute-start.15 = (bf16[512,512]{1,0:T(8,128)(2,1)S(1)}, bf16[512,512]{1,0:T(8,128)(2,1)S(1)}, u32[]{:S(2)}, u32[]{:S(2)}) collective-permute-start(bf16[512,512]{1,0:T(8,128)(2,1)S(1)} %slice.22), channel_id=1, source_target_pairs={{1,0},{2,1},{3,2},{0,3},{5,4},{6,5},{7,6},{4,7},{9,8},{10,9},{11,1... | collective-permute-start | bytes 1572872 | tf_op jit(solution)/shard_map/ppermute | solution.py:298
  115.8 7.7 %collective-permute-done.14.refs_8_ = bf16[256,2048]{1,0:T(8,128)(2,1)} collective-permute-done((bf16[256,2048]{1,0:T(8,128)(2,1)}, bf16[256,2048]{1,0:T(8,128)(2,1)}, u32[]{:S(2)}, u32[]{:S(2)}) %collective-permute-start.14) | collective-permute-done | bytes 1048608 | tf_op jit(solution)/shard_map/ppermute | solution.py:293
  123.6 12.1 %project_most.1 = (bf16[256,2048]{1,0:T(8,128)(2,1)S(1)}, bf16[256,2048]{1,0:T(8,128)(2,1)S(1)}, bf16[256,2048]{1,0:T(8,128)(2,1)S(1)}, bf16[256,2048]{1,0:T(8,128)(2,1)S(1)}, bf16[512,2048]{1,0:T(8,128)(2,1)S(1)}) custom-call(s32[1]{0:T(128)} %slice.21.last_ref, s32[3]{0:T(128)S(1)} %gather_fusion, bf16[256,2048]{1,0:T(8,128)(2,1)S(1)} %copy-done.2, ...), custom_call_target="tpu_custom_call" | custom-call | flops 6442450944 | bytes 10485760 | tf_op jit(solution)/shard_map/project_most/pallas_call | solution.py:230
  135.7 2.4 %collective-permute-done.16.refs_1_ = bf16[512,512]{1,0:T(8,128)(2,1)S(1)} collective-permute-done((bf16[512,512]{1,0:T(8,128)(2,1)S(1)}, bf16[512,512]{1,0:T(8,128)(2,1)S(1)}, u32[]{:S(2)}, u32[]{:S(2)}) %collective-permute-start.16) | collective-permute-done | bytes 524320 | tf_op jit(solution)/shard_map/ppermute | solution.py:298
  138.2 3.7 %project_rest.1 = (bf16[256,2048]{1,0:T(8,128)(2,1)S(1)}, bf16[256,2048]{1,0:T(8,128)(2,1)S(1)}, bf16[256,2048]{1,0:T(8,128)(2,1)S(1)}, bf16[256,2048]{1,0:T(8,128)(2,1)S(1)}) custom-call(bf16[512,2048]{1,0:T(8,128)(2,1)S(1)} %get-tuple-element.67.weight_ref, bf16[512,512]{1,0:T(8,128)(2,1)S(1)} %collective-permute-done.15.refs_0_, ...), custom_call_target="tpu_custom_call" | custom-call | flops 2147483648 | bytes 10485760 | tf_op jit(solution)/shard_map/project_rest/pallas_call | solution.py:252
  141.8 0.1 collective-permute-start.23
  141.9 0.5 collective-permute-start.19
  142.4 2.1 %collective-permute-done.23 = bf16[256,2048]{1,0:T(8,128)(2,1)S(1)} collective-permute-done((bf16[256,2048]{1,0:T(8,128)(2,1)S(1)}, bf16[256,2048]{1,0:T(8,128)(2,1)S(1)}, u32[]{:S(2)}, u32[]{:S(2)}) %collective-permute-start.23) | collective-permute-done | bytes 1048608 | tf_op jit(solution)/shard_map/ppermute | solution.py:293
  144.6 0.4 add_convert_fusion.1
  144.9 1.1 collective-permute-start.24
  146.1 1.6 collective-permute-start.22
  147.8 0.9 collective-permute-start.21
  148.7 1.6 collective-permute-start.20
  150.2 0.4 add_convert_fusion.2
  150.6 6.7 %collective-permute-done.22.refs_3_ = bf16[256,512]{1,0:T(8,128)(2,1)S(1)} collective-permute-done((bf16[256,512]{1,0:T(8,128)(2,1)S(1)}, bf16[256,512]{1,0:T(8,128)(2,1)S(1)}, u32[]{:S(2)}, u32[]{:S(2)}) %collective-permute-start.22) | collective-permute-done | bytes 262176 | tf_op jit(solution)/shard_map/ppermute | solution.py:298
  157.3 10.1 %collective-permute-done.21.refs_2_ = bf16[256,512]{1,0:T(8,128)(2,1)S(1)} collective-permute-done((bf16[256,512]{1,0:T(8,128)(2,1)S(1)}, bf16[256,512]{1,0:T(8,128)(2,1)S(1)}, u32[]{:S(2)}, u32[]{:S(2)}) %collective-permute-start.21) | collective-permute-done | bytes 262176 | tf_op jit(solution)/shard_map/ppermute | solution.py:298
  167.4 0.7 copy-done.12
  168.1 0.7 copy-done.13
  168.8 2.3 %by_column.1 = (bf16[256,1024]{1,0:T(8,128)(2,1)}, bf16[256,1024]{1,0:T(8,128)(2,1)}) custom-call(s32[1]{0:T(128)} %bitcast.16.col_ref, bf16[256,512]{1,0:T(8,128)(2,1)} %copy-done.9, bf16[256,512]{1,0:T(8,128)(2,1)} %copy-done.13, bf16[256,512]{1,0:T(8,128)(2,1)} %copy-done.12, bf16[256,512]{1,0:T(8,128)(2,1)} %copy-done.11), custom_call_target="tpu_custom_call" | custom-call | tf_op jit(solution)/shard_map/by_column/pallas_call | solution.py:282
  171.2 1.4 add_convert_fusion
  (46 shorter events, 0.3 us)
Async XLA Ops:
  1.7 9.5 %collective-permute-start.1 = (bf16[256,512]{1,0:T(8,128)(2,1)S(1)}, bf16[256,512]{1,0:T(8,128)(2,1)S(1)}, u32[]{:S(2)}, u32[]{:S(2)}) collective-permute-start(bf16[256,512]{1,0:T(8,128)(2,1)S(1)} %get-tuple-element.103), channel_id=1, source_target_pairs={{0,16},{4,20},{8,24},{12,28},{16,0},{20,4},{24,8},{28,12},{1,17},{... | collective-permute-start | bytes 786440 | tf_op jit(solution)/shard_map/ppermute | solution.py:293
  4.7 9.2 %collective-permute-start = (bf16[256,512]{1,0:T(8,128)(2,1)S(1)}, bf16[256,512]{1,0:T(8,128)(2,1)S(1)}, u32[]{:S(2)}, u32[]{:S(2)}) collective-permute-start(bf16[256,512]{1,0:T(8,128)(2,1)S(1)} %get-tuple-element.103), channel_id=1, source_target_pairs={{0,8},{4,12},{8,0},{12,4},{16,24},{20,28},{24,16},{28,20},{1,9},{5... | collective-permute-start | bytes 786440 | tf_op jit(solution)/shard_map/ppermute | solution.py:293
  6.2 11.7 %collective-permute-start.2 = (bf16[256,512]{1,0:T(8,128)(2,1)S(1)}, bf16[256,512]{1,0:T(8,128)(2,1)S(1)}, u32[]{:S(2)}, u32[]{:S(2)}) collective-permute-start(bf16[256,512]{1,0:T(8,128)(2,1)S(1)} %get-tuple-element.103), channel_id=1, source_target_pairs={{0,24},{4,28},{8,16},{12,20},{16,8},{20,12},{24,0},{28,4},{1,25},{... | collective-permute-start | bytes 786440 | tf_op jit(solution)/shard_map/ppermute | solution.py:293
  9.9 9.2 %copy-start.3 = (s32[2048]{0:T(1024)S(1)}, s32[2048]{0:T(1024)}, u32[]{:S(2)}) copy-start(s32[2048]{0:T(1024)} %param.11) | copy-start | bytes 24580
  18.0 4.5 %collective-permute-start.3 = (bf16[4,256,512]{2,1,0:T(8,128)(2,1)S(1)}, bf16[4,256,512]{2,1,0:T(8,128)(2,1)}, u32[]{:S(2)}, u32[]{:S(2)}) collective-permute-start(bf16[4,256,512]{2,1,0:T(8,128)(2,1)S(1)} %pad_maximum_fusion.1.kv_even), channel_id=1, source_target_pairs={{0,4},{4,0},{8,12},{12,8},{16,20},{20,16},{24,28},{28,24},{1,5},{5... | collective-permute-start | bytes 3145736 | tf_op jit(solution)/shard_map/ppermute | solution.py:293
  18.1 1.0 copy-start
  19.3 28.4 %collective-permute-start.5 = (bf16[256,2048]{1,0:T(8,128)(2,1)}, bf16[256,2048]{1,0:T(8,128)(2,1)S(1)}, u32[]{:S(2)}, u32[]{:S(2)}) collective-permute-start(bf16[256,2048]{1,0:T(8,128)(2,1)} %get-tuple-element.50), channel_id=1, source_target_pairs={{0,8},{4,12},{8,0},{12,4},{16,24},{20,28},{24,16},{28,20},{1,9},{5... | collective-permute-start | bytes 3145736 | tf_op jit(solution)/shard_map/ppermute | solution.py:293
  21.0 26.7 %collective-permute-start.6 = (bf16[256,2048]{1,0:T(8,128)(2,1)}, bf16[256,2048]{1,0:T(8,128)(2,1)}, u32[]{:S(2)}, u32[]{:S(2)}) collective-permute-start(bf16[256,2048]{1,0:T(8,128)(2,1)} %get-tuple-element.46.refs_0_), channel_id=1, source_target_pairs={{0,16},{4,20},{8,24},{12,28},{16,0},{20,4},{24,8},{28,12},{1,17},{... | collective-permute-start | bytes 3145736 | tf_op jit(solution)/shard_map/ppermute | solution.py:293
  22.5 1.2 copy-start.1
  23.7 1.2 copy-start.4
  24.9 1.2 copy-start.5
  42.6 8.0 %collective-permute-start.8 = (bf16[4,256,512]{2,1,0:T(8,128)(2,1)}, bf16[4,256,512]{2,1,0:T(8,128)(2,1)}, u32[]{:S(2)}, u32[]{:S(2)}) collective-permute-start(bf16[4,256,512]{2,1,0:T(8,128)(2,1)} %get-tuple-element.57), channel_id=1, source_target_pairs={{0,4},{4,0},{8,12},{12,8},{16,20},{20,16},{24,28},{28,24},{1,5},{5... | collective-permute-start | bytes 3145736 | tf_op jit(solution)/shard_map/ppermute | solution.py:293
  43.7 2.7 %collective-permute-start.4 = (bf16[2,256,512]{2,1,0:T(8,128)(2,1)}, bf16[2,256,512]{2,1,0:T(8,128)(2,1)}, u32[]{:S(2)}, u32[]{:S(2)}) collective-permute-start(bf16[2,256,512]{2,1,0:T(8,128)(2,1)} %get-tuple-element.96), channel_id=1, source_target_pairs={{0,4},{4,0},{8,12},{12,8},{16,20},{20,16},{24,28},{28,24},{1,5},{5... | collective-permute-start | bytes 1572872 | tf_op jit(solution)/shard_map/ppermute | solution.py:293
  47.7 14.0 %collective-permute-start.9 = (bf16[2,256,512]{2,1,0:T(8,128)(2,1)S(1)}, bf16[2,256,512]{2,1,0:T(8,128)(2,1)S(1)}, u32[]{:S(2)}, u32[]{:S(2)}) collective-permute-start(bf16[2,256,512]{2,1,0:T(8,128)(2,1)S(1)} %get-tuple-element.58), channel_id=1, source_target_pairs={{0,8},{4,12},{8,0},{12,4},{16,24},{20,28},{24,16},{28,20},{1,9},{5... | collective-permute-start | bytes 1572872 | tf_op jit(solution)/shard_map/ppermute | solution.py:293
  48.3 13.7 %collective-permute-start.7 = (bf16[128,2048]{1,0:T(8,128)(2,1)S(1)}, bf16[128,2048]{1,0:T(8,128)(2,1)S(1)}, u32[]{:S(2)}, u32[]{:S(2)}) collective-permute-start(bf16[128,2048]{1,0:T(8,128)(2,1)S(1)} %get-tuple-element.52.refs_1_), channel_id=1, source_target_pairs={{0,16},{4,20},{8,24},{12,28},{16,0},{20,4},{24,8},{28,12},{1,17},{... | collective-permute-start | bytes 1572872 | tf_op jit(solution)/shard_map/ppermute | solution.py:293
  50.6 11.4 %copy-start.10 = (bf16[256,2048]{1,0:T(8,128)(2,1)S(1)}, bf16[256,2048]{1,0:T(8,128)(2,1)}, u32[]{:S(2)}) copy-start(bf16[256,2048]{1,0:T(8,128)(2,1)} %get-tuple-element.59) | copy-start | bytes 3145732
  52.2 37.4 %copy-start.8 = (bf16[4,256,512]{2,1,0:T(8,128)(2,1)}, bf16[4,256,512]{2,1,0:T(8,128)(2,1)S(1)}, u32[]{:S(2)}) copy-start(bf16[4,256,512]{2,1,0:T(8,128)(2,1)S(1)} %add_convert_fusion.3) | copy-start | bytes 3145732
  52.2 37.4 %copy-start.14 = (s32[3]{0:T(128)S(1)}, s32[3]{0:T(128)}, u32[]{:S(2)}) copy-start(s32[3]{0:T(128)} %constant.89) | copy-start | bytes 40
  62.0 27.6 %copy-start.6 = (bf16[128,2048]{1,0:T(8,128)(2,1)}, bf16[128,2048]{1,0:T(8,128)(2,1)S(1)}, u32[]{:S(2)}) copy-start(bf16[128,2048]{1,0:T(8,128)(2,1)S(1)} %collective-permute-done.7.refs_6_) | copy-start | bytes 1572868
  62.0 24.4 %collective-permute-start.10 = (bf16[256,2048]{1,0:T(8,128)(2,1)S(1)}, bf16[256,2048]{1,0:T(8,128)(2,1)}, u32[]{:S(2)}, u32[]{:S(2)}) collective-permute-start(bf16[256,2048]{1,0:T(8,128)(2,1)S(1)} %copy-done.10), channel_id=1, source_target_pairs={{0,8},{4,12},{8,0},{12,4},{16,24},{20,28},{24,16},{28,20},{1,9},{5... | collective-permute-start | bytes 3145736 | tf_op jit(solution)/shard_map/ppermute | solution.py:293
  63.5 47.9 %collective-permute-start.11 = (bf16[384,2048]{1,0:T(8,128)(2,1)}, bf16[384,2048]{1,0:T(8,128)(2,1)}, u32[]{:S(2)}, u32[]{:S(2)}) collective-permute-start(bf16[384,2048]{1,0:T(8,128)(2,1)} %pad_maximum_fusion), channel_id=1, source_target_pairs={{0,16},{4,20},{8,24},{12,28},{16,0},{20,4},{24,8},{28,12},{1,17},{... | collective-permute-start | bytes 4718600 | tf_op jit(solution)/shard_map/ppermute | solution.py:293
  64.0 38.9 %collective-permute-start.13 = (bf16[1024,512]{1,0:T(8,128)(2,1)S(1)}, bf16[1024,512]{1,0:T(8,128)(2,1)}, u32[]{:S(2)}, u32[]{:S(2)}) collective-permute-start(bf16[1024,512]{1,0:T(8,128)(2,1)S(1)} %bitcast.28), channel_id=1, source_target_pairs={{3,0},{0,1},{1,2},{2,3},{7,4},{4,5},{5,6},{6,7},{11,8},{8,9},{9,10... | collective-permute-start | bytes 3145736 | tf_op jit(solution)/shard_map/ppermute | solution.py:298
  65.5 45.8 %collective-permute-start.12 = (bf16[1024,512]{1,0:T(8,128)(2,1)S(1)}, bf16[1024,512]{1,0:T(8,128)(2,1)}, u32[]{:S(2)}, u32[]{:S(2)}) collective-permute-start(bf16[1024,512]{1,0:T(8,128)(2,1)S(1)} %bitcast.29), channel_id=1, source_target_pairs={{1,0},{2,1},{3,2},{0,3},{5,4},{6,5},{7,6},{4,7},{9,8},{10,9},{11,1... | collective-permute-start | bytes 3145736 | tf_op jit(solution)/shard_map/ppermute | solution.py:298
  86.4 37.2 %collective-permute-start.14 = (bf16[256,2048]{1,0:T(8,128)(2,1)}, bf16[256,2048]{1,0:T(8,128)(2,1)}, u32[]{:S(2)}, u32[]{:S(2)}) collective-permute-start(bf16[256,2048]{1,0:T(8,128)(2,1)} %collective-permute-done.10.refs_4_), channel_id=1, source_target_pairs={{0,16},{4,20},{8,24},{12,28},{16,0},{20,4},{24,8},{28,12},{1,17},{... | collective-permute-start | bytes 3145736 | tf_op jit(solution)/shard_map/ppermute | solution.py:293
  88.0 11.9 %collective-permute-start.17 = (bf16[2,256,512]{2,1,0:T(8,128)(2,1)}, bf16[2,256,512]{2,1,0:T(8,128)(2,1)}, u32[]{:S(2)}, u32[]{:S(2)}) collective-permute-start(bf16[2,256,512]{2,1,0:T(8,128)(2,1)} %slice.25), channel_id=1, source_target_pairs={{0,8},{4,12},{8,0},{12,4},{16,24},{20,28},{24,16},{28,20},{1,9},{5... | collective-permute-start | bytes 1572872 | tf_op jit(solution)/shard_map/ppermute | solution.py:293
  90.2 33.4 %copy-start.2 = (bf16[256,2048]{1,0:T(8,128)(2,1)S(1)}, bf16[256,2048]{1,0:T(8,128)(2,1)}, u32[]{:S(2)}) copy-start(bf16[256,2048]{1,0:T(8,128)(2,1)} %get-tuple-element.46.refs_0_) | copy-start | bytes 3145732
  90.2 33.4 %copy-start.7 = (bf16[128,2048]{1,0:T(8,128)(2,1)S(1)}, bf16[128,2048]{1,0:T(8,128)(2,1)}, u32[]{:S(2)}) copy-start(bf16[128,2048]{1,0:T(8,128)(2,1)} %copy-done.6) | copy-start | bytes 1572868
  101.3 34.5 %collective-permute-start.18 = (bf16[256,512]{1,0:T(8,128)(2,1)S(1)}, bf16[256,512]{1,0:T(8,128)(2,1)S(1)}, u32[]{:S(2)}, u32[]{:S(2)}) collective-permute-start(bf16[256,512]{1,0:T(8,128)(2,1)S(1)} %slice_bitcast_fusion.1), channel_id=1, source_target_pairs={{0,16},{4,20},{8,24},{12,28},{16,0},{20,4},{24,8},{28,12},{1,17},{... | collective-permute-start | bytes 786440 | tf_op jit(solution)/shard_map/ppermute | solution.py:293
  113.5 22.2 %collective-permute-start.15 = (bf16[512,512]{1,0:T(8,128)(2,1)S(1)}, bf16[512,512]{1,0:T(8,128)(2,1)S(1)}, u32[]{:S(2)}, u32[]{:S(2)}) collective-permute-start(bf16[512,512]{1,0:T(8,128)(2,1)S(1)} %slice.22), channel_id=1, source_target_pairs={{1,0},{2,1},{3,2},{0,3},{5,4},{6,5},{7,6},{4,7},{9,8},{10,9},{11,1... | collective-permute-start | bytes 1572872 | tf_op jit(solution)/shard_map/ppermute | solution.py:298
  115.8 22.3 %collective-permute-start.16 = (bf16[512,512]{1,0:T(8,128)(2,1)S(1)}, bf16[512,512]{1,0:T(8,128)(2,1)S(1)}, u32[]{:S(2)}, u32[]{:S(2)}) collective-permute-start(bf16[512,512]{1,0:T(8,128)(2,1)S(1)} %slice.23), channel_id=1, source_target_pairs={{3,0},{0,1},{1,2},{2,3},{7,4},{4,5},{5,6},{6,7},{11,8},{8,9},{9,10... | collective-permute-start | bytes 1572872 | tf_op jit(solution)/shard_map/ppermute | solution.py:298
  141.8 2.7 %collective-permute-start.23 = (bf16[256,2048]{1,0:T(8,128)(2,1)S(1)}, bf16[256,2048]{1,0:T(8,128)(2,1)S(1)}, u32[]{:S(2)}, u32[]{:S(2)}) collective-permute-start(bf16[256,2048]{1,0:T(8,128)(2,1)S(1)} %get-tuple-element.82), channel_id=1, source_target_pairs={{0,4},{4,0},{8,12},{12,8},{16,20},{20,16},{24,28},{28,24},{1,5},{5... | collective-permute-start | bytes 3145736 | tf_op jit(solution)/shard_map/ppermute | solution.py:293
  141.9 8.3 %collective-permute-start.19 = (bf16[256,2048]{1,0:T(8,128)(2,1)S(1)}, bf16[256,2048]{1,0:T(8,128)(2,1)S(1)}, u32[]{:S(2)}, u32[]{:S(2)}) collective-permute-start(bf16[256,2048]{1,0:T(8,128)(2,1)S(1)} %get-tuple-element.78), channel_id=1, source_target_pairs={{0,4},{4,0},{8,12},{12,8},{16,20},{20,16},{24,28},{28,24},{1,5},{5... | collective-permute-start | bytes 3145736 | tf_op jit(solution)/shard_map/ppermute | solution.py:293
  144.9 26.2 %collective-permute-start.24 = (bf16[256,2048]{1,0:T(8,128)(2,1)S(1)}, bf16[256,2048]{1,0:T(8,128)(2,1)S(1)}, u32[]{:S(2)}, u32[]{:S(2)}) collective-permute-start(bf16[256,2048]{1,0:T(8,128)(2,1)S(1)} %add_convert_fusion.1), channel_id=1, source_target_pairs={{0,8},{4,12},{8,0},{12,4},{16,24},{20,28},{24,16},{28,20},{1,9},{5... | collective-permute-start | bytes 3145736 | tf_op jit(solution)/shard_map/ppermute | solution.py:293
  146.1 22.7 %copy-start.9 = (bf16[256,512]{1,0:T(8,128)(2,1)}, bf16[256,512]{1,0:T(8,128)(2,1)S(1)}, u32[]{:S(2)}) copy-start(bf16[256,512]{1,0:T(8,128)(2,1)S(1)} %fusion.4.refs_0_) | copy-start | bytes 786436
  146.1 11.2 %collective-permute-start.22 = (bf16[256,512]{1,0:T(8,128)(2,1)S(1)}, bf16[256,512]{1,0:T(8,128)(2,1)S(1)}, u32[]{:S(2)}, u32[]{:S(2)}) collective-permute-start(bf16[256,512]{1,0:T(8,128)(2,1)S(1)} %fusion.4.refs_0_), channel_id=1, source_target_pairs={{3,0},{0,1},{1,2},{2,3},{7,4},{4,5},{5,6},{6,7},{11,8},{8,9},{9,10... | collective-permute-start | bytes 786440 | tf_op jit(solution)/shard_map/ppermute | solution.py:298
  147.8 19.7 %collective-permute-start.21 = (bf16[256,512]{1,0:T(8,128)(2,1)S(1)}, bf16[256,512]{1,0:T(8,128)(2,1)S(1)}, u32[]{:S(2)}, u32[]{:S(2)}) collective-permute-start(bf16[256,512]{1,0:T(8,128)(2,1)S(1)} %fusion.4.refs_0_), channel_id=1, source_target_pairs={{2,0},{3,1},{0,2},{1,3},{6,4},{7,5},{4,6},{5,7},{10,8},{11,9},{8,1... | collective-permute-start | bytes 786440 | tf_op jit(solution)/shard_map/ppermute | solution.py:298
  148.7 18.8 %collective-permute-start.20 = (bf16[256,512]{1,0:T(8,128)(2,1)S(1)}, bf16[256,512]{1,0:T(8,128)(2,1)S(1)}, u32[]{:S(2)}, u32[]{:S(2)}) collective-permute-start(bf16[256,512]{1,0:T(8,128)(2,1)S(1)} %fusion.4.refs_0_), channel_id=1, source_target_pairs={{1,0},{2,1},{3,2},{0,3},{5,4},{6,5},{7,6},{4,7},{9,8},{10,9},{11,1... | collective-permute-start | bytes 786440 | tf_op jit(solution)/shard_map/ppermute | solution.py:298
  157.3 10.1 %copy-start.11 = (bf16[256,512]{1,0:T(8,128)(2,1)}, bf16[256,512]{1,0:T(8,128)(2,1)S(1)}, u32[]{:S(2)}) copy-start(bf16[256,512]{1,0:T(8,128)(2,1)S(1)} %collective-permute-done.22.refs_3_) | copy-start | bytes 786436
  167.4 0.7 copy-start.12
  168.1 0.7 copy-start.13

commit v6 on v5

--- a/solution.py
+++ b/solution.py
@@ -337,8 +337,7 @@
         wide = rows_w // 2
         pieces = []
         for start, size in (
-            (side * wide, wide // 2), (side * wide + wide // 2, wide // 4),
-            (side * wide + wide * 3 // 4, wide // 4),
+            (side * wide, wide // 2), (side * wide + wide // 2, wide // 2),
             ((1 - side) * wide, wide // 2), ((1 - side) * wide + wide // 2, wide // 2),
         ):
             pieces.append(lax.dynamic_slice_in_dim(q_weight, start, size, 0))
@@ -393,7 +392,7 @@
     core = me & 1
     side = (me >> 1) & 1
 
-    keep_w, (send_one, send_two) = pieces[:3], pieces[3:]
+    keep_w, (send_one, send_two) = pieces[:2], pieces[2:]
 
     def x(block):
         return across(block, 2)
@@ -410,17 +409,13 @@
     keep = lax.dynamic_index_in_dim(both, side, 0, keepdims=False)
     send = lax.dynamic_index_in_dim(both, 1 - side, 0, keepdims=False)
     send, w_one, keep_one_y = tied(send, w_one, keep_one_y)
-    keep_w[1], send = tied(keep_w[1], send)
-    keep_two_y = y(keep_w[1])
+    last_one = jnp.concatenate([keep_w[1], w_one], axis=0)
+    last_one_y = y(last_one)
     tokens = jnp.concatenate([keep, x(send)], axis=0)
     tokens = tokens.reshape(4 * rows, -1)
-    last_one = jnp.concatenate([keep_w[2], w_one], axis=0)
     dkv_terms = added(dkv_even, across(dkv_odd, 1))
-    send_two, last_one, keep_two_y, dkv_terms, tokens = tied(
-        send_two, last_one, keep_two_y, dkv_terms, tokens
-    )
+    send_two, dkv_terms, tokens = tied(send_two, dkv_terms, tokens)
     near = [turned(tokens, 1), turned(tokens, -1)]
-    last_one_y = y(last_one)
     w_two = x(send_two)
     dkv_x = x(dkv_terms[1::2])
     w_two_y = y(w_two)
@@ -430,12 +425,12 @@
     dkv_terms = added(dkv_terms[0::2], dkv_x)
     dkv_y = y(dkv_terms[1])
 
-    pieces = [*keep_w, w_one, w_two, keep_one_y, keep_two_y, last_one_y, w_two_y]
+    pieces = [*keep_w, w_one, w_two, keep_one_y, last_one_y, w_two_y]
     sizes = [piece.shape[0] for piece in pieces]
-    last = sizes[2]
+    last = sizes[1]
     weights = [
-        [(i, 0, sizes[i]) for i in (0, 1, 2)], [(i, 0, sizes[i]) for i in (3, 4)],
-        [(5, 0, sizes[5]), (6, 0, sizes[6]), (7, 0, last)], [(7, last, sizes[7] - last), (8, 0, sizes[8])],
+        [(i, 0, sizes[i]) for i in (0, 1)], [(i, 0, sizes[i]) for i in (2, 3)],
+        [(4, 0, sizes[4]), (5, 0, last)], [(5, last, sizes[5] - last), (6, 0, sizes[6])],
     ]
     slots = ((me >> 1) ^ ((col + jnp.arange(count)) % count)).astype(jnp.int32)
     devices = range(4)

time: 176 us -> 177 us (level)
  other arithmetic: 7.99 us -> 10.6 us
    ppermute x18 -> x17, starting transfers between devices: 17 us -> 15.9 us  [across(): return lax.ppermute(block, 'row', [(i, i ^ mask) for i in range(ranks)])]
    dynamic_slice x2 -> x1, local copies, waits for them, and re-layouts: 4.93 us -> 3.97 us  [local(): pieces.append(lax.dynamic_slice_in_dim(q_weight, start, size, 0))]
    ppermute x18 -> x17, waiting for transfers between devices: 56.7 us -> 57.6 us  [across(): return lax.ppermute(block, 'row', [(i, i ^ mask) for i in range(ranks)])]
  transfers between devices with their start and end apart: 25 -> 24, of which waited for: 13 -> 13; matrix products, arithmetic and copies ran while one was open for 10% -> 10% of each run, Pallas kernels for 18% -> 18%
where the time goes in v6:
time: 177 us; the launch traced here: 174 us
  waiting for transfers between devices  83.6 us (47%)
  Pallas kernels  35 us (20%)
  starting transfers between devices  26.8 us (15%)
  local copies, waits for them, and re-layouts  17.1 us (10%)
  other arithmetic  10.6 us (6%)
    ppermute x17, waiting for transfers between devices, across(): return lax.ppermute(block, 'row', [(i, i ^ mask) for i in range(ranks)])  57.6 us
    ppermute x7, waiting for transfers between devices, turned(): lax.ppermute(block, 'col', [((i + distance) % count, i) for i in range(co...  26 us
    pallas_call x1, Pallas kernels, attention(): pl.pallas_call(functools.partial(attention_kernel, per_kv, rows, ranks),...  16.4 us
    ppermute x17, starting transfers between devices, across(): return lax.ppermute(block, 'row', [(i, i ^ mask) for i in range(ranks)])  15.9 us
    pallas_call x1, Pallas kernels, project(): pl.pallas_call(functools.partial(most_kernel, len(pieces), weights, place...  12.6 us
    ppermute x7, starting transfers between devices, turned(): lax.ppermute(block, 'col', [((i + distance) % count, i) for i in range(co...  10.9 us
    unnamed x30, local copies, waits for them, and re-layouts  6.78 us
    convert_element_type x6, other arithmetic, added(): (one.astype(jnp.float32) + two.astype(jnp.float32)).astype(jnp.bfloat16)  5.14 us
  transfers between devices with their start and end apart: 24, of which 13 were waited for; matrix products, arithmetic and copies ran while one was open for 10% of the time, Pallas kernels for 18%

profile of v6, /device:TPU:0, one launch (start us, length us, event | category | flops | bytes accessed | tf_op | source)
XLA Modules:
  0.0 174.0 jit_solution(16096162584796211436)
XLA Ops:
  0.7 1.0 constant_dynamic-slice_fusion.8
  1.7 3.0 %collective-permute-start.1 = (bf16[256,512]{1,0:T(8,128)(2,1)S(1)}, bf16[256,512]{1,0:T(8,128)(2,1)S(1)}, u32[]{:S(2)}, u32[]{:S(2)}) collective-permute-start(bf16[256,512]{1,0:T(8,128)(2,1)S(1)} %get-tuple-element.92), channel_id=1, source_target_pairs={{0,16},{4,20},{8,24},{12,28},{16,0},{20,4},{24,8},{28,12},{1,17},{... | collective-permute-start | bytes 786440 | tf_op jit(solution)/shard_map/ppermute | solution.py:293
  4.7 1.5 collective-permute-start
  6.2 4.0 %constant_dynamic-slice_fusion.2 = (bf16[256,2048]{1,0:T(8,128)(2,1)}, bf16[256,2048]{1,0:T(8,128)(2,1)S(1)}, bf16[256,2048]{1,0:T(8,128)(2,1)S(1)}, bf16[256,2048]{1,0:T(8,128)(2,1)}) fusion(bf16[1024,2048]{1,0:T(8,128)(2,1)} %param.12, s32[]{:T(128)S(6)} %select_n.62, s32[]{:T(128)S(6)} %select_n.60, s32[]{:T(128)S(6)} %select_n.59, s32[]{:T(128)S(6)} %select_n.61), kind=kLoop, calls=%fused_computation.27 | loop fusion | bytes 8388624 | tf_op jit(solution)/shard_map/dynamic_slice | solution.py:343
  10.2 0.8 collective-permute-done.1
  11.0 2.9 %collective-permute-done = bf16[256,512]{1,0:T(8,128)(2,1)S(1)} collective-permute-done((bf16[256,512]{1,0:T(8,128)(2,1)S(1)}, bf16[256,512]{1,0:T(8,128)(2,1)S(1)}, u32[]{:S(2)}, u32[]{:S(2)}) %collective-permute-start) | collective-permute-done | bytes 262176 | tf_op jit(solution)/shard_map/ppermute | solution.py:293
  13.9 3.9 %collective-permute-done.2 = bf16[256,512]{1,0:T(8,128)(2,1)S(1)} collective-permute-done((bf16[256,512]{1,0:T(8,128)(2,1)S(1)}, bf16[256,512]{1,0:T(8,128)(2,1)S(1)}, u32[]{:S(2)}, u32[]{:S(2)}) %collective-permute-start.2) | collective-permute-done | bytes 262176 | tf_op jit(solution)/shard_map/ppermute | solution.py:293
  17.9 0.7 copy-done.13
  18.6 1.2 pad_maximum_fusion.1.kv_even
  19.8 0.1 collective-permute-start.3
  19.9 1.0 copy-done
  20.9 0.1 copy.10.seg_query
  21.1 1.7 collective-permute-start.5
  22.8 1.5 collective-permute-start.6
  24.3 1.2 copy-done.1
  25.5 1.2 copy-done.3
  26.7 1.2 copy-done.4
  28.0 16.4 %attention.1 = (bf16[2,2,256,512]{3,2,1,0:T(8,128)(2,1)S(1)}, bf16[4,256,512]{2,1,0:T(8,128)(2,1)S(1)}, bf16[4,256,512]{2,1,0:T(8,128)(2,1)}) custom-call(s32[1]{0:T(128)} %bitcast.4.me_ref, s32[2,128,1]{2,1,0:T(8,128)S(1)} %copy.10.seg_query, s32[16,1,128]{2,1,0:T(1,128)S(1)} %bitcast.32, bf16[256,2048]{1,0:T(8,128)(2,1)S(1)} %copy-done.3, ...), custom_call_target="tpu_custom_call" | custom-call | flops 3400000000 | bytes 8000000 | tf_op jit(solution)/shard_map/attention/pallas_call | solution.py:135
  44.4 1.0 dynamic-slice_bitcast_fusion
  45.4 0.5 collective-permute-start.4
  45.9 2.2 %collective-permute-done.4 = bf16[2,256,512]{2,1,0:T(8,128)(2,1)} collective-permute-done((bf16[2,256,512]{2,1,0:T(8,128)(2,1)}, bf16[2,256,512]{2,1,0:T(8,128)(2,1)}, u32[]{:S(2)}, u32[]{:S(2)}) %collective-permute-start.4) | collective-permute-done | bytes 524320 | tf_op jit(solution)/shard_map/ppermute | solution.py:293
  48.1 1.3 fusion.1
  49.4 0.6 collective-permute-start.8
  50.1 2.8 %pad_maximum_fusion = bf16[512,2048]{1,0:T(8,128)(2,1)} fusion(bf16[256,2048]{1,0:T(8,128)(2,1)} %collective-permute-done.5.refs_2_, bf16[256,2048]{1,0:T(8,128)(2,1)S(1)} %get-tuple-element.42.refs_1_), kind=kLoop, calls=%fused_computation.1 | loop fusion | flops 4194304 | bytes 4194304 | tf_op jit(solution)/shard_map/concatenate | solution.py:412
  52.8 1.0 collective-permute-start.10
  53.9 1.6 add_convert_fusion.3
  55.5 8.0 %collective-permute-done.8 = bf16[2,256,512]{2,1,0:T(8,128)(2,1)S(1)} collective-permute-done((bf16[2,256,512]{2,1,0:T(8,128)(2,1)S(1)}, bf16[2,256,512]{2,1,0:T(8,128)(2,1)S(1)}, u32[]{:S(2)}, u32[]{:S(2)}) %collective-permute-start.8) | collective-permute-done | bytes 524320 | tf_op jit(solution)/shard_map/ppermute | solution.py:293
  63.5 0.1 pad_maximum_fusion.2
  63.6 0.6 collective-permute-start.9
  64.2 1.6 collective-permute-start.12
  65.8 2.2 %collective-permute-start.11 = (bf16[1024,512]{1,0:T(8,128)(2,1)S(1)}, bf16[1024,512]{1,0:T(8,128)(2,1)}, u32[]{:S(2)}, u32[]{:S(2)}) collective-permute-start(bf16[1024,512]{1,0:T(8,128)(2,1)S(1)} %bitcast.29), channel_id=1, source_target_pairs={{1,0},{2,1},{3,2},{0,3},{5,4},{6,5},{7,6},{4,7},{9,8},{10,9},{11,1... | collective-permute-start | bytes 3145736 | tf_op jit(solution)/shard_map/ppermute | solution.py:298
  68.0 20.2 %collective-permute-done.9.refs_3_ = bf16[256,2048]{1,0:T(8,128)(2,1)} collective-permute-done((bf16[256,2048]{1,0:T(8,128)(2,1)S(1)}, bf16[256,2048]{1,0:T(8,128)(2,1)}, u32[]{:S(2)}, u32[]{:S(2)}) %collective-permute-start.9) | collective-permute-done | bytes 1048608 | tf_op jit(solution)/shard_map/ppermute | solution.py:293
  88.2 0.5 collective-permute-start.13
  88.7 0.8 slice.25
  89.6 1.1 collective-permute-start.16
  90.6 0.6 slice.21.last_ref
  91.2 0.6 gather_fusion
  91.9 10.0 %collective-permute-done.16 = bf16[2,256,512]{2,1,0:T(8,128)(2,1)} collective-permute-done((bf16[2,256,512]{2,1,0:T(8,128)(2,1)}, bf16[2,256,512]{2,1,0:T(8,128)(2,1)}, u32[]{:S(2)}, u32[]{:S(2)}) %collective-permute-start.16) | collective-permute-done | bytes 524320 | tf_op jit(solution)/shard_map/ppermute | solution.py:293
  101.9 1.3 add_convert_fusion.4
  103.3 1.6 collective-permute-start.17
  104.9 7.4 %collective-permute-done.11.refs_8_ = bf16[1024,512]{1,0:T(8,128)(2,1)} collective-permute-done((bf16[1024,512]{1,0:T(8,128)(2,1)S(1)}, bf16[1024,512]{1,0:T(8,128)(2,1)}, u32[]{:S(2)}, u32[]{:S(2)}) %collective-permute-start.11) | collective-permute-done | bytes 1048608 | tf_op jit(solution)/shard_map/ppermute | solution.py:298
  112.3 1.1 slice.23
  113.4 1.1 slice.22
  114.4 2.4 %collective-permute-start.14 = (bf16[512,512]{1,0:T(8,128)(2,1)S(1)}, bf16[512,512]{1,0:T(8,128)(2,1)S(1)}, u32[]{:S(2)}, u32[]{:S(2)}) collective-permute-start(bf16[512,512]{1,0:T(8,128)(2,1)S(1)} %slice.22), channel_id=1, source_target_pairs={{1,0},{2,1},{3,2},{0,3},{5,4},{6,5},{7,6},{4,7},{9,8},{10,9},{11,1... | collective-permute-start | bytes 1572872 | tf_op jit(solution)/shard_map/ppermute | solution.py:298
  116.8 7.3 %collective-permute-done.13.refs_6_ = bf16[256,2048]{1,0:T(8,128)(2,1)} collective-permute-done((bf16[256,2048]{1,0:T(8,128)(2,1)}, bf16[256,2048]{1,0:T(8,128)(2,1)}, u32[]{:S(2)}, u32[]{:S(2)}) %collective-permute-start.13) | collective-permute-done | bytes 1048608 | tf_op jit(solution)/shard_map/ppermute | solution.py:293
  124.1 12.6 %project_most.1 = (bf16[256,2048]{1,0:T(8,128)(2,1)S(1)}, bf16[256,2048]{1,0:T(8,128)(2,1)S(1)}, bf16[256,2048]{1,0:T(8,128)(2,1)S(1)}, bf16[256,2048]{1,0:T(8,128)(2,1)S(1)}, bf16[512,2048]{1,0:T(8,128)(2,1)S(1)}) custom-call(s32[1]{0:T(128)} %slice.21.last_ref, s32[3]{0:T(128)S(1)} %gather_fusion, bf16[256,2048]{1,0:T(8,128)(2,1)S(1)} %get-tuple-element.41.refs_0_, ...), custom_call_target="tpu_custom_call" | custom-call | flops 6442450944 | bytes 10485760 | tf_op jit(solution)/shard_map/project_most/pallas_call | solution.py:230
  136.7 2.4 %collective-permute-done.15.refs_1_ = bf16[512,512]{1,0:T(8,128)(2,1)S(1)} collective-permute-done((bf16[512,512]{1,0:T(8,128)(2,1)S(1)}, bf16[512,512]{1,0:T(8,128)(2,1)S(1)}, u32[]{:S(2)}, u32[]{:S(2)}) %collective-permute-start.15) | collective-permute-done | bytes 524320 | tf_op jit(solution)/shard_map/ppermute | solution.py:298
  139.1 3.7 %project_rest.1 = (bf16[256,2048]{1,0:T(8,128)(2,1)S(1)}, bf16[256,2048]{1,0:T(8,128)(2,1)S(1)}, bf16[256,2048]{1,0:T(8,128)(2,1)S(1)}, bf16[256,2048]{1,0:T(8,128)(2,1)S(1)}) custom-call(bf16[512,2048]{1,0:T(8,128)(2,1)S(1)} %get-tuple-element.57.weight_ref, bf16[512,512]{1,0:T(8,128)(2,1)S(1)} %collective-permute-done.14.refs_0_, ...), custom_call_target="tpu_custom_call" | custom-call | flops 2147483648 | bytes 10485760 | tf_op jit(solution)/shard_map/project_rest/pallas_call | solution.py:252
  142.8 0.1 collective-permute-start.22
  142.9 0.5 collective-permute-start.18
  143.4 2.1 %collective-permute-done.22 = bf16[256,2048]{1,0:T(8,128)(2,1)S(1)} collective-permute-done((bf16[256,2048]{1,0:T(8,128)(2,1)S(1)}, bf16[256,2048]{1,0:T(8,128)(2,1)S(1)}, u32[]{:S(2)}, u32[]{:S(2)}) %collective-permute-start.22) | collective-permute-done | bytes 1048608 | tf_op jit(solution)/shard_map/ppermute | solution.py:293
  145.5 0.4 add_convert_fusion.1
  145.9 1.6 collective-permute-start.23
  147.5 0.1 fusion.4.refs_0_
  147.5 1.6 collective-permute-start.21
  149.2 1.5 collective-permute-start.20
  150.6 1.6 collective-permute-start.19
  152.2 0.4 add_convert_fusion.2
  152.6 6.1 %collective-permute-done.21.refs_3_ = bf16[256,512]{1,0:T(8,128)(2,1)S(1)} collective-permute-done((bf16[256,512]{1,0:T(8,128)(2,1)S(1)}, bf16[256,512]{1,0:T(8,128)(2,1)S(1)}, u32[]{:S(2)}, u32[]{:S(2)}) %collective-permute-start.21) | collective-permute-done | bytes 262176 | tf_op jit(solution)/shard_map/ppermute | solution.py:298
  158.7 10.1 %collective-permute-done.20.refs_2_ = bf16[256,512]{1,0:T(8,128)(2,1)S(1)} collective-permute-done((bf16[256,512]{1,0:T(8,128)(2,1)S(1)}, bf16[256,512]{1,0:T(8,128)(2,1)S(1)}, u32[]{:S(2)}, u32[]{:S(2)}) %collective-permute-start.20) | collective-permute-done | bytes 262176 | tf_op jit(solution)/shard_map/ppermute | solution.py:298
  168.8 0.7 copy-done.9
  169.5 0.7 copy-done.10
  170.2 2.3 %by_column.1 = (bf16[256,1024]{1,0:T(8,128)(2,1)}, bf16[256,1024]{1,0:T(8,128)(2,1)}) custom-call(s32[1]{0:T(128)} %bitcast.16.col_ref, bf16[256,512]{1,0:T(8,128)(2,1)} %copy-done.7, bf16[256,512]{1,0:T(8,128)(2,1)} %copy-done.10, bf16[256,512]{1,0:T(8,128)(2,1)} %copy-done.9, bf16[256,512]{1,0:T(8,128)(2,1)} %copy-done.8), custom_call_target="tpu_custom_call" | custom-call | tf_op jit(solution)/shard_map/by_column/pallas_call | solution.py:282
  172.6 1.4 add_convert_fusion
  (43 shorter events, 0.2 us)
Async XLA Ops:
  1.7 9.3 %collective-permute-start.1 = (bf16[256,512]{1,0:T(8,128)(2,1)S(1)}, bf16[256,512]{1,0:T(8,128)(2,1)S(1)}, u32[]{:S(2)}, u32[]{:S(2)}) collective-permute-start(bf16[256,512]{1,0:T(8,128)(2,1)S(1)} %get-tuple-element.92), channel_id=1, source_target_pairs={{0,16},{4,20},{8,24},{12,28},{16,0},{20,4},{24,8},{28,12},{1,17},{... | collective-permute-start | bytes 786440 | tf_op jit(solution)/shard_map/ppermute | solution.py:293
  4.7 9.2 %collective-permute-start = (bf16[256,512]{1,0:T(8,128)(2,1)S(1)}, bf16[256,512]{1,0:T(8,128)(2,1)S(1)}, u32[]{:S(2)}, u32[]{:S(2)}) collective-permute-start(bf16[256,512]{1,0:T(8,128)(2,1)S(1)} %get-tuple-element.92), channel_id=1, source_target_pairs={{0,8},{4,12},{8,0},{12,4},{16,24},{20,28},{24,16},{28,20},{1,9},{5... | collective-permute-start | bytes 786440 | tf_op jit(solution)/shard_map/ppermute | solution.py:293
  6.2 11.7 %collective-permute-start.2 = (bf16[256,512]{1,0:T(8,128)(2,1)S(1)}, bf16[256,512]{1,0:T(8,128)(2,1)S(1)}, u32[]{:S(2)}, u32[]{:S(2)}) collective-permute-start(bf16[256,512]{1,0:T(8,128)(2,1)S(1)} %get-tuple-element.92), channel_id=1, source_target_pairs={{0,24},{4,28},{8,16},{12,20},{16,8},{20,12},{24,0},{28,4},{1,25},{... | collective-permute-start | bytes 786440 | tf_op jit(solution)/shard_map/ppermute | solution.py:293
  10.2 10.7 %copy-start.2 = (s32[2048]{0:T(1024)S(1)}, s32[2048]{0:T(1024)}, u32[]{:S(2)}) copy-start(s32[2048]{0:T(1024)} %param.11) | copy-start | bytes 24580
  11.0 6.9 %copy-start.11 = (bf16[256,512]{1,0:T(8,128)(2,1)}, bf16[256,512]{1,0:T(8,128)(2,1)S(1)}, u32[]{:S(2)}) copy-start(bf16[256,512]{1,0:T(8,128)(2,1)S(1)} %collective-permute-done.1) | copy-start | bytes 786436
  13.9 4.0 %copy-start.12 = (bf16[256,512]{1,0:T(8,128)(2,1)}, bf16[256,512]{1,0:T(8,128)(2,1)S(1)}, u32[]{:S(2)}) copy-start(bf16[256,512]{1,0:T(8,128)(2,1)S(1)} %collective-permute-done) | copy-start | bytes 786436
  17.9 0.7 copy-start.13
  19.8 4.5 %collective-permute-start.3 = (bf16[4,256,512]{2,1,0:T(8,128)(2,1)S(1)}, bf16[4,256,512]{2,1,0:T(8,128)(2,1)}, u32[]{:S(2)}, u32[]{:S(2)}) collective-permute-start(bf16[4,256,512]{2,1,0:T(8,128)(2,1)S(1)} %pad_maximum_fusion.1.kv_even), channel_id=1, source_target_pairs={{0,4},{4,0},{8,12},{12,8},{16,20},{20,16},{24,28},{28,24},{1,5},{5... | collective-permute-start | bytes 3145736 | tf_op jit(solution)/shard_map/ppermute | solution.py:293
  19.9 1.0 copy-start
  21.1 28.4 %collective-permute-start.5 = (bf16[256,2048]{1,0:T(8,128)(2,1)}, bf16[256,2048]{1,0:T(8,128)(2,1)}, u32[]{:S(2)}, u32[]{:S(2)}) collective-permute-start(bf16[256,2048]{1,0:T(8,128)(2,1)} %get-tuple-element.45), channel_id=1, source_target_pairs={{0,8},{4,12},{8,0},{12,4},{16,24},{20,28},{24,16},{28,20},{1,9},{5... | collective-permute-start | bytes 3145736 | tf_op jit(solution)/shard_map/ppermute | solution.py:293
  22.8 26.7 %collective-permute-start.6 = (bf16[256,2048]{1,0:T(8,128)(2,1)S(1)}, bf16[256,2048]{1,0:T(8,128)(2,1)}, u32[]{:S(2)}, u32[]{:S(2)}) collective-permute-start(bf16[256,2048]{1,0:T(8,128)(2,1)S(1)} %get-tuple-element.41.refs_0_), channel_id=1, source_target_pairs={{0,16},{4,20},{8,24},{12,28},{16,0},{20,4},{24,8},{28,12},{1,17},{... | collective-permute-start | bytes 3145736 | tf_op jit(solution)/shard_map/ppermute | solution.py:293
  24.3 1.2 copy-start.1
  25.5 1.2 copy-start.3
  26.7 1.2 copy-start.4
  44.4 9.5 %collective-permute-start.7 = (bf16[4,256,512]{2,1,0:T(8,128)(2,1)}, bf16[4,256,512]{2,1,0:T(8,128)(2,1)}, u32[]{:S(2)}, u32[]{:S(2)}) collective-permute-start(bf16[4,256,512]{2,1,0:T(8,128)(2,1)} %get-tuple-element.49), channel_id=1, source_target_pairs={{0,4},{4,0},{8,12},{12,8},{16,20},{20,16},{24,28},{28,24},{1,5},{5... | collective-permute-start | bytes 3145736 | tf_op jit(solution)/shard_map/ppermute | solution.py:293
  45.4 2.7 %collective-permute-start.4 = (bf16[2,256,512]{2,1,0:T(8,128)(2,1)}, bf16[2,256,512]{2,1,0:T(8,128)(2,1)}, u32[]{:S(2)}, u32[]{:S(2)}) collective-permute-start(bf16[2,256,512]{2,1,0:T(8,128)(2,1)} %get-tuple-element.85), channel_id=1, source_target_pairs={{0,4},{4,0},{8,12},{12,8},{16,20},{20,16},{24,28},{28,24},{1,5},{5... | collective-permute-start | bytes 1572872 | tf_op jit(solution)/shard_map/ppermute | solution.py:293
  49.4 14.0 %collective-permute-start.8 = (bf16[2,256,512]{2,1,0:T(8,128)(2,1)S(1)}, bf16[2,256,512]{2,1,0:T(8,128)(2,1)S(1)}, u32[]{:S(2)}, u32[]{:S(2)}) collective-permute-start(bf16[2,256,512]{2,1,0:T(8,128)(2,1)S(1)} %get-tuple-element.50), channel_id=1, source_target_pairs={{0,8},{4,12},{8,0},{12,4},{16,24},{20,28},{24,16},{28,20},{1,9},{5... | collective-permute-start | bytes 1572872 | tf_op jit(solution)/shard_map/ppermute | solution.py:293
  52.8 59.4 %collective-permute-start.10 = (bf16[512,2048]{1,0:T(8,128)(2,1)}, bf16[512,2048]{1,0:T(8,128)(2,1)}, u32[]{:S(2)}, u32[]{:S(2)}) collective-permute-start(bf16[512,2048]{1,0:T(8,128)(2,1)} %pad_maximum_fusion), channel_id=1, source_target_pairs={{0,16},{4,20},{8,24},{12,28},{16,0},{20,4},{24,8},{28,12},{1,17},{... | collective-permute-start | bytes 6291464 | tf_op jit(solution)/shard_map/ppermute | solution.py:293
  53.9 9.7 %copy-start.6 = (bf16[256,2048]{1,0:T(8,128)(2,1)S(1)}, bf16[256,2048]{1,0:T(8,128)(2,1)}, u32[]{:S(2)}) copy-start(bf16[256,2048]{1,0:T(8,128)(2,1)} %get-tuple-element.51) | copy-start | bytes 3145732
  55.5 35.8 %copy-start.5 = (bf16[4,256,512]{2,1,0:T(8,128)(2,1)}, bf16[4,256,512]{2,1,0:T(8,128)(2,1)S(1)}, u32[]{:S(2)}) copy-start(bf16[4,256,512]{2,1,0:T(8,128)(2,1)S(1)} %add_convert_fusion.3) | copy-start | bytes 3145732
  55.5 35.8 %copy-start.14 = (s32[3]{0:T(128)S(1)}, s32[3]{0:T(128)}, u32[]{:S(2)}) copy-start(s32[3]{0:T(128)} %constant.85) | copy-start | bytes 40
  63.6 24.6 %collective-permute-start.9 = (bf16[256,2048]{1,0:T(8,128)(2,1)S(1)}, bf16[256,2048]{1,0:T(8,128)(2,1)}, u32[]{:S(2)}, u32[]{:S(2)}) collective-permute-start(bf16[256,2048]{1,0:T(8,128)(2,1)S(1)} %copy-done.6), channel_id=1, source_target_pairs={{0,8},{4,12},{8,0},{12,4},{16,24},{20,28},{24,16},{28,20},{1,9},{5... | collective-permute-start | bytes 3145736 | tf_op jit(solution)/shard_map/ppermute | solution.py:293
  64.2 40.7 %collective-permute-start.12 = (bf16[1024,512]{1,0:T(8,128)(2,1)S(1)}, bf16[1024,512]{1,0:T(8,128)(2,1)}, u32[]{:S(2)}, u32[]{:S(2)}) collective-permute-start(bf16[1024,512]{1,0:T(8,128)(2,1)S(1)} %bitcast.28), channel_id=1, source_target_pairs={{3,0},{0,1},{1,2},{2,3},{7,4},{4,5},{5,6},{6,7},{11,8},{8,9},{9,10... | collective-permute-start | bytes 3145736 | tf_op jit(solution)/shard_map/ppermute | solution.py:298
  65.8 46.5 %collective-permute-start.11 = (bf16[1024,512]{1,0:T(8,128)(2,1)S(1)}, bf16[1024,512]{1,0:T(8,128)(2,1)}, u32[]{:S(2)}, u32[]{:S(2)}) collective-permute-start(bf16[1024,512]{1,0:T(8,128)(2,1)S(1)} %bitcast.29), channel_id=1, source_target_pairs={{1,0},{2,1},{3,2},{0,3},{5,4},{6,5},{7,6},{4,7},{9,8},{10,9},{11,1... | collective-permute-start | bytes 3145736 | tf_op jit(solution)/shard_map/ppermute | solution.py:298
  88.2 35.9 %collective-permute-start.13 = (bf16[256,2048]{1,0:T(8,128)(2,1)}, bf16[256,2048]{1,0:T(8,128)(2,1)}, u32[]{:S(2)}, u32[]{:S(2)}) collective-permute-start(bf16[256,2048]{1,0:T(8,128)(2,1)} %collective-permute-done.9.refs_3_), channel_id=1, source_target_pairs={{0,16},{4,20},{8,24},{12,28},{16,0},{20,4},{24,8},{28,12},{1,17},{... | collective-permute-start | bytes 3145736 | tf_op jit(solution)/shard_map/ppermute | solution.py:293
  89.6 12.4 %collective-permute-start.16 = (bf16[2,256,512]{2,1,0:T(8,128)(2,1)}, bf16[2,256,512]{2,1,0:T(8,128)(2,1)}, u32[]{:S(2)}, u32[]{:S(2)}) collective-permute-start(bf16[2,256,512]{2,1,0:T(8,128)(2,1)} %slice.25), channel_id=1, source_target_pairs={{0,8},{4,12},{8,0},{12,4},{16,24},{20,28},{24,16},{28,20},{1,9},{5... | collective-permute-start | bytes 1572872 | tf_op jit(solution)/shard_map/ppermute | solution.py:293
  103.3 33.4 %collective-permute-start.17 = (bf16[256,512]{1,0:T(8,128)(2,1)S(1)}, bf16[256,512]{1,0:T(8,128)(2,1)S(1)}, u32[]{:S(2)}, u32[]{:S(2)}) collective-permute-start(bf16[256,512]{1,0:T(8,128)(2,1)S(1)} %slice_bitcast_fusion.1), channel_id=1, source_target_pairs={{0,16},{4,20},{8,24},{12,28},{16,0},{20,4},{24,8},{28,12},{1,17},{... | collective-permute-start | bytes 786440 | tf_op jit(solution)/shard_map/ppermute | solution.py:293
  114.4 22.3 %collective-permute-start.14 = (bf16[512,512]{1,0:T(8,128)(2,1)S(1)}, bf16[512,512]{1,0:T(8,128)(2,1)S(1)}, u32[]{:S(2)}, u32[]{:S(2)}) collective-permute-start(bf16[512,512]{1,0:T(8,128)(2,1)S(1)} %slice.22), channel_id=1, source_target_pairs={{1,0},{2,1},{3,2},{0,3},{5,4},{6,5},{7,6},{4,7},{9,8},{10,9},{11,1... | collective-permute-start | bytes 1572872 | tf_op jit(solution)/shard_map/ppermute | solution.py:298
  116.8 22.3 %collective-permute-start.15 = (bf16[512,512]{1,0:T(8,128)(2,1)S(1)}, bf16[512,512]{1,0:T(8,128)(2,1)S(1)}, u32[]{:S(2)}, u32[]{:S(2)}) collective-permute-start(bf16[512,512]{1,0:T(8,128)(2,1)S(1)} %slice.23), channel_id=1, source_target_pairs={{3,0},{0,1},{1,2},{2,3},{7,4},{4,5},{5,6},{6,7},{11,8},{8,9},{9,10... | collective-permute-start | bytes 1572872 | tf_op jit(solution)/shard_map/ppermute | solution.py:298
  142.8 2.7 %collective-permute-start.22 = (bf16[256,2048]{1,0:T(8,128)(2,1)S(1)}, bf16[256,2048]{1,0:T(8,128)(2,1)S(1)}, u32[]{:S(2)}, u32[]{:S(2)}) collective-permute-start(bf16[256,2048]{1,0:T(8,128)(2,1)S(1)} %get-tuple-element.72), channel_id=1, source_target_pairs={{0,4},{4,0},{8,12},{12,8},{16,20},{20,16},{24,28},{28,24},{1,5},{5... | collective-permute-start | bytes 3145736 | tf_op jit(solution)/shard_map/ppermute | solution.py:293
  142.9 9.4 %collective-permute-start.18 = (bf16[256,2048]{1,0:T(8,128)(2,1)S(1)}, bf16[256,2048]{1,0:T(8,128)(2,1)S(1)}, u32[]{:S(2)}, u32[]{:S(2)}) collective-permute-start(bf16[256,2048]{1,0:T(8,128)(2,1)S(1)} %get-tuple-element.68), channel_id=1, source_target_pairs={{0,4},{4,0},{8,12},{12,8},{16,20},{20,16},{24,28},{28,24},{1,5},{5... | collective-permute-start | bytes 3145736 | tf_op jit(solution)/shard_map/ppermute | solution.py:293
  145.9 26.7 %collective-permute-start.23 = (bf16[256,2048]{1,0:T(8,128)(2,1)S(1)}, bf16[256,2048]{1,0:T(8,128)(2,1)S(1)}, u32[]{:S(2)}, u32[]{:S(2)}) collective-permute-start(bf16[256,2048]{1,0:T(8,128)(2,1)S(1)} %add_convert_fusion.1), channel_id=1, source_target_pairs={{0,8},{4,12},{8,0},{12,4},{16,24},{20,28},{24,16},{28,20},{1,9},{5... | collective-permute-start | bytes 3145736 | tf_op jit(solution)/shard_map/ppermute | solution.py:293
  147.5 22.7 %copy-start.7 = (bf16[256,512]{1,0:T(8,128)(2,1)}, bf16[256,512]{1,0:T(8,128)(2,1)S(1)}, u32[]{:S(2)}) copy-start(bf16[256,512]{1,0:T(8,128)(2,1)S(1)} %fusion.4.refs_0_) | copy-start | bytes 786436
  147.5 11.2 %collective-permute-start.21 = (bf16[256,512]{1,0:T(8,128)(2,1)S(1)}, bf16[256,512]{1,0:T(8,128)(2,1)S(1)}, u32[]{:S(2)}, u32[]{:S(2)}) collective-permute-start(bf16[256,512]{1,0:T(8,128)(2,1)S(1)} %fusion.4.refs_0_), channel_id=1, source_target_pairs={{3,0},{0,1},{1,2},{2,3},{7,4},{4,5},{5,6},{6,7},{11,8},{8,9},{9,10... | collective-permute-start | bytes 786440 | tf_op jit(solution)/shard_map/ppermute | solution.py:298
  149.2 19.7 %collective-permute-start.20 = (bf16[256,512]{1,0:T(8,128)(2,1)S(1)}, bf16[256,512]{1,0:T(8,128)(2,1)S(1)}, u32[]{:S(2)}, u32[]{:S(2)}) collective-permute-start(bf16[256,512]{1,0:T(8,128)(2,1)S(1)} %fusion.4.refs_0_), channel_id=1, source_target_pairs={{2,0},{3,1},{0,2},{1,3},{6,4},{7,5},{4,6},{5,7},{10,8},{11,9},{8,1... | collective-permute-start | bytes 786440 | tf_op jit(solution)/shard_map/ppermute | solution.py:298
  150.6 18.2 %collective-permute-start.19 = (bf16[256,512]{1,0:T(8,128)(2,1)S(1)}, bf16[256,512]{1,0:T(8,128)(2,1)S(1)}, u32[]{:S(2)}, u32[]{:S(2)}) collective-permute-start(bf16[256,512]{1,0:T(8,128)(2,1)S(1)} %fusion.4.refs_0_), channel_id=1, source_target_pairs={{1,0},{2,1},{3,2},{0,3},{5,4},{6,5},{7,6},{4,7},{9,8},{10,9},{11,1... | collective-permute-start | bytes 786440 | tf_op jit(solution)/shard_map/ppermute | solution.py:298
  158.7 10.1 %copy-start.8 = (bf16[256,512]{1,0:T(8,128)(2,1)}, bf16[256,512]{1,0:T(8,128)(2,1)S(1)}, u32[]{:S(2)}) copy-start(bf16[256,512]{1,0:T(8,128)(2,1)S(1)} %collective-permute-done.21.refs_3_) | copy-start | bytes 786436
  168.8 0.7 copy-start.9
  169.5 0.7 copy-start.10
